TPU v7x, 128 devices: a whole 4x4x4 slice. The times are simulated.
128 devices in a mesh: batch: 2 (over z_lo), seq: 32 (over y, x, core), tensor: 2 (over z_hi).
Axes of the slice: x: 4, y: 4, z: 4 (z_hi: 2, z_lo: 2; z = z_hi * 2 + z_lo), core: 2. Of those that a mesh axis runs over, the one named last changes fastest.
Arguments:
- tokens: bfloat16 [8192, 2560], P(('batch', 'seq')), may hold values from -6 to 6
- cotangent: bfloat16 [8192, 2560], P(('batch', 'seq')), may hold values from -6 to 6
- query_weight: float32 [2560, 2560], P(('batch', 'seq'), 'tensor'), may hold values from -0.125 to 0.125
- query_moment: float32 [2560, 2560], P(('batch', 'seq'), 'tensor'), may hold values from -16 to 16
- query_second: float32 [2560, 2560], P(('batch', 'seq'), 'tensor'), may hold values from 26.95168 to 107.80672
- keyvalue_weight: float32 [2560, 512], P(('batch', 'seq')), may hold values from -0.125 to 0.125
- keyvalue_moment: float32 [2560, 512], P(('batch', 'seq')), may hold values from -64 to 64
- keyvalue_second: float32 [2560, 512], P(('batch', 'seq')), may hold values from 430.8992 to 1724.416
- output_weight: float32 [2560, 2560], P(('batch', 'seq'), 'tensor'), may hold values from -0.625 to 0.625
- output_moment: float32 [2560, 2560], P(('batch', 'seq'), 'tensor'), may hold values from -6 to 6
- output_second: float32 [2560, 2560], P(('batch', 'seq'), 'tensor'), may hold values from 17.2032 to 68.8128
- feedforward_weight: float32 [3, 2560, 7680], P(None, ('batch', 'seq'), 'tensor'), may hold values from -0.125 to 0.125
- feedforward_moment: float32 [3, 2560, 7680], P(None, ('batch', 'seq'), 'tensor'), may hold values from -32 to 32
- feedforward_second: float32 [3, 2560, 7680], P(None, ('batch', 'seq'), 'tensor'), may hold values from 107.80672 to 430.8992
- norm_gains: float32 [2, 2560], P(None, ('batch', 'seq')), may hold values from 0.5 to 1.5
- gains_moment: float32 [2, 2560], P(None, ('batch', 'seq')), may hold values from -32 to 32
- gains_second: float32 [2, 2560], P(None, ('batch', 'seq')), may hold values from 107.80672 to 430.8992
Outputs:
- out_tokens: bfloat16 [8192, 2560], P(('batch', 'seq'))
- input_grad: float32 [8192, 2560], P(('batch', 'seq'))
- query_moment_new: float32 [2560, 2560], P(('batch', 'seq'), 'tensor')
- query_second_new: float32 [2560, 2560], P(('batch', 'seq'), 'tensor')
- query_weight_new: float32 [2560, 2560], P(('batch', 'seq'), 'tensor')
- keyvalue_moment_new: float32 [2560, 512], P(('batch', 'seq'))
- keyvalue_second_new: float32 [2560, 512], P(('batch', 'seq'))
- keyvalue_weight_new: float32 [2560, 512], P(('batch', 'seq'))
- output_moment_new: float32 [2560, 2560], P(('batch', 'seq'), 'tensor')
- output_second_new: float32 [2560, 2560], P(('batch', 'seq'), 'tensor')
- output_weight_new: float32 [2560, 2560], P(('batch', 'seq'), 'tensor')
- feedforward_moment_new: float32 [3, 2560, 7680], P(None, ('batch', 'seq'), 'tensor')
- feedforward_second_new: float32 [3, 2560, 7680], P(None, ('batch', 'seq'), 'tensor')
- feedforward_weight_new: float32 [3, 2560, 7680], P(None, ('batch', 'seq'), 'tensor')
- gains_moment_new: float32 [2, 2560], P(None, ('batch', 'seq'))
- gains_second_new: float32 [2, 2560], P(None, ('batch', 'seq'))
- norm_gains_new: float32 [2, 2560], P(None, ('batch', 'seq'))
All inputs are finite; a program needn't handle non-finite values.
Results may differ from a plain program's by a relative error of at most 0.018.
Values may be sent and summed in bfloat16 or wider, within the bound.
No kernel may reach another device: no remote copies, remote signals or barrier semaphores. Data moves between devices by JAX's collectives and lax.ppermute only.
A program may use at most 576 MiB of HBM per device.

v0:
```python
import math

import jax
import jax.numpy as jnp
from jax import lax
from jax.sharding import PartitionSpec as P

D = 2560
HEADS = 10
HEAD_DIM = 256
WINDOW = 2048
STEP = 10


def rms_scale(values, gain):
    return values * lax.rsqrt(jnp.mean(values * values, axis=-1, keepdims=True) + 1e-06) * gain


def rotate(values, places, sign):
    half = values.shape[-1] // 2
    steps = jnp.arange(half, dtype=jnp.float32)
    freqs = jnp.exp(steps * (-2.0 * math.log(10000.0) / values.shape[-1]))
    angle = places[:, None] * freqs[None, :]
    cosine = jnp.cos(angle)[:, None, :]
    sine = sign * jnp.sin(angle)[:, None, :]
    first = values[..., :half]
    second = values[..., half:]
    return jnp.concatenate(
        [first * cosine - second * sine, second * cosine + first * sine], axis=-1
    )


def gelu_mix(gate_in, up_in):
    return jax.nn.gelu(gate_in, approximate=True) * up_in


def adam(weight, grad, moment, second, rate, decay):
    moment_new = 0.9 * moment + 0.1 * grad
    second_new = 0.95 * second + 0.05 * grad * grad
    ratio = moment_new / (1.0 - 0.9**STEP) / (jnp.sqrt(second_new / (1.0 - 0.95**STEP)) + 1e-08)
    return (moment_new, second_new, weight - rate * (ratio + decay * weight))


def local(
    tokens,
    cotangent,
    query_weight,
    query_moment,
    query_second,
    keyvalue_weight,
    keyvalue_moment,
    keyvalue_second,
    output_weight,
    output_moment,
    output_second,
    feedforward_weight,
    feedforward_moment,
    feedforward_second,
    norm_gains,
    gains_moment,
    gains_second,
):
    row_count = tokens.shape[0]
    head_size = keyvalue_weight.shape[1] // 2
    query_cols = query_weight.shape[1]
    local_heads = query_cols // head_size
    feed_width = feedforward_weight.shape[2]
    owner_rows = query_weight.shape[0]
    seq_total = lax.axis_size("seq") * row_count
    scaling = head_size ** (-0.5)
    wide_rate = 1.5 * D ** (-0.5)
    output_rate = 1.5 * (HEADS * HEAD_DIM // 32) ** (-0.5)
    first_row = lax.axis_index("seq") * row_count
    row_places = first_row + jnp.arange(row_count, dtype=jnp.int32)
    places = row_places.astype(jnp.float32)
    w_query, w_pair, w_output, gain_low = (
        lax.all_gather(query_weight.astype(jnp.bfloat16), ("batch", "seq"), axis=0, tiled=True),
        lax.all_gather(keyvalue_weight.astype(jnp.bfloat16), ("batch", "seq"), axis=0, tiled=True),
        lax.all_gather(output_weight.astype(jnp.bfloat16), ("batch", "seq"), axis=0, tiled=True),
        lax.all_gather(norm_gains.astype(jnp.bfloat16), ("batch", "seq"), axis=1, tiled=True),
    )
    w_feed = lax.all_gather(
        feedforward_weight.astype(jnp.bfloat16), ("batch", "seq"), axis=1, tiled=True
    )
    gain_rows = gain_low.astype(jnp.float32)
    inflow = tokens.astype(jnp.float32)
    normed_a = rms_scale(inflow, gain_rows[0]).astype(jnp.bfloat16)
    query_raw = jnp.dot(normed_a, w_query, preferred_element_type=jnp.float32)
    pair_raw = jnp.dot(normed_a, w_pair, preferred_element_type=jnp.float32)
    queries = rotate(query_raw.reshape(row_count, local_heads, head_size), places, 1.0).astype(
        jnp.bfloat16
    )
    key_low = rotate(pair_raw[:, None, :head_size], places, 1.0)[:, 0].astype(jnp.bfloat16)
    value_low = pair_raw[:, head_size:].astype(jnp.bfloat16)
    pair_low = jnp.concatenate([key_low, value_low], axis=1)
    pairs_all = lax.all_gather(pair_low, "seq", axis=0, tiled=True)
    key_span = min(seq_total, WINDOW + row_count)
    key_start = jnp.clip(first_row + row_count - key_span, 0, seq_total - key_span)
    distance = row_places[:, None] - (key_start + jnp.arange(key_span, dtype=jnp.int32))[None, :]
    inside = (distance >= 0) & (distance < WINDOW)

    def window(gathered):
        span_rows = lax.dynamic_slice_in_dim(gathered, key_start, key_span, 0)
        return (span_rows[:, :head_size], span_rows[:, head_size:])

    def softmax_rows(key_rows):
        scores = (
            jnp.einsum("qhd,kd->hqk", queries, key_rows, preferred_element_type=jnp.float32)
            * scaling
        )
        scores = jnp.where(inside[None], scores, -1e30)
        row_max = jnp.max(scores, axis=-1, keepdims=True)
        weights_exp = jnp.exp(scores - row_max)
        return weights_exp / jnp.sum(weights_exp, axis=-1, keepdims=True)

    key_rows, value_rows = window(pairs_all)
    probs = softmax_rows(key_rows)
    probs_low = probs.astype(jnp.bfloat16)
    attended = (
        jnp.einsum("hqk,kd->qhd", probs_low, value_rows, preferred_element_type=jnp.float32)
        .reshape(row_count, query_cols)
        .astype(jnp.bfloat16)
    )
    branch_part = jnp.einsum("tc,dc->td", attended, w_output, preferred_element_type=jnp.float32)
    residual = inflow + lax.psum(branch_part, "tensor")
    normed_b = rms_scale(residual, gain_rows[1]).astype(jnp.bfloat16)
    gate_pre = jnp.dot(normed_b, w_feed[0], preferred_element_type=jnp.float32)
    up_pre = jnp.dot(normed_b, w_feed[1], preferred_element_type=jnp.float32)
    activated = gelu_mix(gate_pre, up_pre).astype(jnp.bfloat16)
    feed_part = jnp.einsum("tf,df->td", activated, w_feed[2], preferred_element_type=jnp.float32)
    out_tokens = (
        residual + lax.psum(feed_part.astype(jnp.bfloat16), "tensor").astype(jnp.float32)
    ).astype(jnp.bfloat16)
    feed_back = lax.all_gather(
        feedforward_weight.astype(jnp.bfloat16), ("batch", "seq"), axis=1, tiled=True
    )
    grad_act = jnp.dot(cotangent, feed_back[2], preferred_element_type=jnp.float32)
    unused_mix, pull_mix = jax.vjp(gelu_mix, gate_pre, up_pre)
    grad_gate, grad_up = pull_mix(grad_act)
    grad_gate_low = grad_gate.astype(jnp.bfloat16)
    grad_up_low = grad_up.astype(jnp.bfloat16)
    normb_part = jnp.einsum(
        "tf,df->td", grad_gate_low, feed_back[0], preferred_element_type=jnp.float32
    )
    normb_part = normb_part + jnp.einsum(
        "tf,df->td", grad_up_low, feed_back[1], preferred_element_type=jnp.float32
    )
    grad_normb = lax.psum(normb_part, "tensor")
    unused_b, pull_b = jax.vjp(rms_scale, residual, gain_rows[1])
    resid_from_norm, grad_gain_b = pull_b(grad_normb)
    grad_resid = cotangent.astype(jnp.float32) + resid_from_norm
    gate_up_low = jnp.concatenate([grad_gate_low, grad_up_low], axis=1)
    feed_grad = lax.psum_scatter(
        jnp.concatenate(
            [
                jnp.einsum("tr,tf->rf", normed_b, gate_up_low, preferred_element_type=jnp.float32),
                jnp.einsum("tr,tf->rf", cotangent, activated, preferred_element_type=jnp.float32),
            ],
            axis=1,
        ),
        ("batch", "seq"),
        scatter_dimension=0,
        tiled=True,
    )
    feed_grad = feed_grad.reshape(owner_rows, 3, feed_width).transpose(1, 0, 2)
    feed_new = adam(
        feedforward_weight, feed_grad, feedforward_moment, feedforward_second, wide_rate, 0.1
    )
    query_back, pair_back, output_back = (
        lax.all_gather(query_weight.astype(jnp.bfloat16), ("batch", "seq"), axis=0, tiled=True),
        lax.all_gather(keyvalue_weight.astype(jnp.bfloat16), ("batch", "seq"), axis=0, tiled=True),
        lax.all_gather(output_weight.astype(jnp.bfloat16), ("batch", "seq"), axis=0, tiled=True),
    )
    pairs_back = lax.all_gather(pair_low, "seq", axis=0, tiled=True)
    resid_low = grad_resid.astype(jnp.bfloat16)
    grad_att = (
        jnp.dot(resid_low, output_back, preferred_element_type=jnp.float32)
        .astype(jnp.bfloat16)
        .reshape(row_count, local_heads, head_size)
    )
    key_back, value_back = window(pairs_back)
    probs_back = softmax_rows(key_back)
    probs_back_low = probs_back.astype(jnp.bfloat16)
    grad_probs = jnp.einsum("qhd,kd->hqk", grad_att, value_back, preferred_element_type=jnp.float32)
    grad_values = jnp.einsum(
        "hqk,qhd->kd", probs_back_low, grad_att, preferred_element_type=jnp.float32
    )
    grad_scores = (
        probs_back * (grad_probs - jnp.sum(probs_back * grad_probs, axis=-1, keepdims=True))
    ).astype(jnp.bfloat16)
    grad_queries = (
        jnp.einsum("hqk,kd->qhd", grad_scores, key_back, preferred_element_type=jnp.float32)
        * scaling
    )
    grad_keys = (
        jnp.einsum("hqk,qhd->kd", grad_scores, queries, preferred_element_type=jnp.float32)
        * scaling
    )
    window_term = jnp.concatenate([grad_keys, grad_values], axis=1)
    full_term = lax.dynamic_update_slice_in_dim(
        jnp.zeros((seq_total, 2 * head_size), jnp.float32), window_term, key_start, 0
    )
    pair_part = lax.psum_scatter(full_term, "seq", scatter_dimension=0, tiled=True)
    query_grad_low = (
        rotate(grad_queries, places, -1.0).reshape(row_count, query_cols).astype(jnp.bfloat16)
    )
    norma_part = jnp.einsum(
        "tc,dc->td", query_grad_low, query_back, preferred_element_type=jnp.float32
    )
    norma_sum, pair_sum = lax.psum((norma_part, pair_part), "tensor")
    key_grad = rotate(pair_sum[:, None, :head_size], places, -1.0)[:, 0]
    pair_grad_low = jnp.concatenate([key_grad, pair_sum[:, head_size:]], axis=1).astype(
        jnp.bfloat16
    )
    grad_norma = norma_sum + jnp.einsum(
        "tc,dc->td", pair_grad_low, pair_back, preferred_element_type=jnp.float32
    )
    unused_a, pull_a = jax.vjp(rms_scale, inflow, gain_rows[0])
    input_from_norm, grad_gain_a = pull_a(grad_norma)
    input_grad = grad_resid + input_from_norm
    attention_terms = jnp.concatenate(
        [
            jnp.einsum("td,tc->dc", normed_a, query_grad_low, preferred_element_type=jnp.float32),
            jnp.einsum("td,tc->dc", normed_a, pair_grad_low, preferred_element_type=jnp.float32),
            jnp.einsum("td,tc->dc", resid_low, attended, preferred_element_type=jnp.float32),
        ],
        axis=1,
    )
    gain_terms = jnp.stack([grad_gain_a, grad_gain_b])
    attention_grad, gain_grad = (
        lax.psum_scatter(attention_terms, ("batch", "seq"), scatter_dimension=0, tiled=True),
        lax.psum_scatter(gain_terms, ("batch", "seq"), scatter_dimension=1, tiled=True),
    )
    query_grad = attention_grad[:, :query_cols]
    pair_grad = attention_grad[:, query_cols : query_cols + 2 * head_size]
    output_grad = attention_grad[:, query_cols + 2 * head_size :]
    query_new = adam(query_weight, query_grad, query_moment, query_second, wide_rate, 0.1)
    pair_new = adam(keyvalue_weight, pair_grad, keyvalue_moment, keyvalue_second, wide_rate, 0.1)
    output_new = adam(output_weight, output_grad, output_moment, output_second, output_rate, 0.1)
    gains_new = adam(norm_gains, gain_grad, gains_moment, gains_second, 0.3, 0.0)
    return (
        out_tokens,
        input_grad,
        query_new[0],
        query_new[1],
        query_new[2],
        pair_new[0],
        pair_new[1],
        pair_new[2],
        output_new[0],
        output_new[1],
        output_new[2],
        feed_new[0],
        feed_new[1],
        feed_new[2],
        gains_new[0],
        gains_new[1],
        gains_new[2],
    )


def solution(mesh):
    placed = (
        P(("batch", "seq"), None),
        P(("batch", "seq"), None),
        P(("batch", "seq"), "tensor"),
        P(("batch", "seq"), "tensor"),
        P(("batch", "seq"), "tensor"),
        P(("batch", "seq"), None),
        P(("batch", "seq"), None),
        P(("batch", "seq"), None),
        P(("batch", "seq"), "tensor"),
        P(("batch", "seq"), "tensor"),
        P(("batch", "seq"), "tensor"),
        P(None, ("batch", "seq"), "tensor"),
        P(None, ("batch", "seq"), "tensor"),
        P(None, ("batch", "seq"), "tensor"),
        P(None, ("batch", "seq")),
        P(None, ("batch", "seq")),
        P(None, ("batch", "seq")),
    )
    return jax.shard_map(
        local,
        mesh=mesh,
        in_specs=placed,
        out_specs=(
            P(("batch", "seq"), None),
            P(("batch", "seq"), None),
            P(("batch", "seq"), "tensor"),
            P(("batch", "seq"), "tensor"),
            P(("batch", "seq"), "tensor"),
            P(("batch", "seq"), None),
            P(("batch", "seq"), None),
            P(("batch", "seq"), None),
            P(("batch", "seq"), "tensor"),
            P(("batch", "seq"), "tensor"),
            P(("batch", "seq"), "tensor"),
            P(None, ("batch", "seq"), "tensor"),
            P(None, ("batch", "seq"), "tensor"),
            P(None, ("batch", "seq"), "tensor"),
            P(None, ("batch", "seq")),
            P(None, ("batch", "seq")),
            P(None, ("batch", "seq")),
        ),
        check_vma=False,
    )
```

profile of v0, /device:TPU:0, one launch (start us, length us, event | category | flops | bytes accessed | tf_op | source)
XLA Modules:
  0.0 2158.1 jit_solution(10620056758428324223)
XLA Ops:
  7.2 1.5 convert_element_type.96
  8.8 1.6 convert_element_type.99
  10.5 0.7 convert_bitcast_fusion
  11.2 82.3 %all-gather = bf16[64,40,2]{1,2,0:T(2,128)(2,1)S(1)} all-gather(bf16[1,40,2]{1,2,0:T(2,128)(2,1)S(1)} %convert_bitcast_fusion), channel_id=1, replica_groups=mesh['batch'=2,'seq'=32,'tensor'=2] {'batch','seq'}, dimensions={0}, use_global_device_ids=true | all-gather | bytes 10400 | tf_op jit(solution)/shard_map/all_gather | solution.py:80
  93.9 1.3 fusion.38
  95.3 21.9 %all-gather.7.cloned.1.call-done = bf16[2560,512]{1,0:T(8,128)(2,1)} async-done(((bf16[40,512]{1,0:T(8,128)(2,1)}), bf16[2560,512]{1,0:T(8,128)(2,1)}) %all-gather.7.cloned.1.call-update) | async-done | bytes 2621456 | tf_op jit(solution)/shard_map/all_gather | solution.py:78
  117.1 2.6 fusion.93
  120.1 0.7 pad_maximum_fusion.5
  120.8 0.7 convert_element_type.104
  121.6 0.9 broadcast_multiply_fusion
  122.6 1.0 fusion.44
  123.6 104.1 %all-gather.11.cloned.1.call-done = bf16[2560,1280]{1,0:T(8,128)(2,1)} async-done(((bf16[40,1280]{1,0:T(8,128)(2,1)}), bf16[2560,1280]{1,0:T(8,128)(2,1)}) %all-gather.11.cloned.1.call-update) | async-done | bytes 6553616 | tf_op jit(solution)/shard_map/all_gather | solution.py:77
  227.7 5.6 fusion.91
  233.8 41.7 %all-gather.9.cloned.1.call-done = bf16[4096,512]{1,0:T(8,128)(2,1)} async-done(((bf16[128,512]{1,0:T(8,128)(2,1)}), bf16[4096,512]{1,0:T(8,128)(2,1)}) %all-gather.9.cloned.1.call-update) | async-done | bytes 4194320 | tf_op jit(solution)/shard_map/all_gather | solution.py:96
  275.5 5.6 fusion.102
  281.1 5.3 fusion.41
  286.5 99.8 %all-gather.13.cloned.1.call-done = bf16[2560,1280]{1,0:T(8,128)(2,1)} async-done(((bf16[40,1280]{1,0:T(8,128)(2,1)}), bf16[2560,1280]{1,0:T(8,128)(2,1)}) %all-gather.13.cloned.1.call-update) | async-done | bytes 6553616 | tf_op jit(solution)/shard_map/all_gather | solution.py:79
  386.3 6.4 fusion.103
  392.8 1.0 convert_element_type.106
  394.3 51.3 %all-reduce.8.cloned.1.call-done = f32[128,2560]{1,0:T(8,128)} async-done(((f32[128,2560]{1,0:T(8,128)}), f32[128,2560]{1,0:T(8,128)}) %all-reduce.8.cloned.1.call-update) | async-done | bytes 1310736 | tf_op jit(solution)/shard_map/psum | solution.py:125
  445.7 1.6 multiply_reduce_fusion.2
  447.5 318.9 %all-gather.15.cloned.1.call-done = bf16[3,2560,3840]{2,1,0:T(8,128)(2,1)} async-done(((bf16[3,40,3840]{2,1,0:T(8,128)(2,1)}), bf16[3,2560,3840]{2,1,0:T(8,128)(2,1)}) %all-gather.15.cloned.1.call-update) | async-done | bytes 58982416 | tf_op jit(solution)/shard_map/all_gather | solution.py:82
  766.4 8.1 fusion.4
  774.6 8.2 fusion.2
  782.8 9.5 multiply_convert_fusion
  792.3 11.1 fusion.1
  803.4 11.7 fusion.13
  815.2 11.3 fusion.14
  826.8 43.2 %all-reduce.12.cloned.1.call-done = f32[128,2560]{1,0:T(8,128)} async-done(((f32[128,2560]{1,0:T(8,128)}), f32[128,2560]{1,0:T(8,128)}) %all-reduce.12.cloned.1.call-update) | async-done | bytes 1310736 | tf_op jit(solution)/shard_map/psum | solution.py:148
  870.0 2.3 multiply_reduce_fusion
  872.3 39.5 %all-reduce.10.cloned.1.call-done = bf16[128,2560]{1,0:T(8,128)(2,1)} async-done(((bf16[128,2560]{1,0:T(8,128)(2,1)}), bf16[128,2560]{1,0:T(8,128)(2,1)}) %all-reduce.10.cloned.1.call-update) | async-done | bytes 655376 | tf_op jit(solution)/shard_map/psum | solution.py:132
  911.9 3.0 fusion.36
  914.9 4.4 convolution_convert_fusion
  919.4 4.4 fusion.8
  924.0 0.7 fusion.10
  924.7 1.6 copy-done.4
  926.3 2.4 fusion.12
  928.7 5.9 convolution_bitcast_fusion.1
  934.6 5.0 pad_maximum_fusion.2
  939.7 4.4 broadcast_in_dim.30
  944.0 12.5 dynamic_update_slice.3
  956.8 3.4 fusion.40
  960.6 6.2 fusion.104
  966.8 81.7 %reduce-scatter.10.cloned.1.call-done = f32[128,512]{1,0:T(8,128)} async-done(((f32[4096,512]{1,0:T(8,128)}), f32[128,512]{1,0:T(8,128)}) %reduce-scatter.10.cloned.1.call-update) | async-done | bytes 262160 | tf_op jit(solution)/shard_map/reduce_scatter | solution.py:203
  1048.6 6.6 fusion.89
  1055.3 6.7 fusion.46
  1062.0 48.7 %all-reduce.14.cloned.1.call-done = (f32[128,2560]{1,0:T(8,128)}, f32[128,512]{1,0:T(8,128)}) async-done(((f32[128,2560]{1,0:T(8,128)}, f32[128,512]{1,0:T(8,128)}), (f32[128,2560]{1,0:T(8,128)}, f32[128,512]{1,0:T(8,128)})) %all-reduce.14.cloned.1.call-update) | async-done | bytes 1572880 | tf_op jit(solution)/shard_map/psum | solution.py:210
  1110.7 0.9 slice.154
  1111.6 0.9 slice_bitcast_fusion.13
  1113.0 3.2 fusion.61
  1116.2 22.9 %pad_maximum_fusion.1 = f32[2560,3072]{0,1:T(8,128)} fusion(f32[2560,1280]{0,1:T(8,128)} %fusion.46, f32[2560,512]{0,1:T(8,128)} %fusion.61, f32[2560,1280]{0,1:T(8,128)} %fusion.89), kind=kLoop, calls=%fused_computation.2 | loop fusion | flops 15728640 | bytes 62914560 | tf_op jit(solution)/shard_map/concatenate | solution.py:221
  1139.1 30.7 %copy.203 = f32[2560,3072]{1,0:T(8,128)} copy(f32[2560,3072]{0,1:T(8,128)} %pad_maximum_fusion.1) | data formatting | bytes 62914560
  1170.2 0.7 copy-done.10
  1171.2 15.8 convolution_bitcast_fusion
  1187.0 28.9 %fusion.22 = f32[2560,7680]{1,0:T(8,128)} fusion(bf16[128,2560]{1,0:T(8,128)(2,1)S(1)} %copy-done.8, bf16[128,3840]{1,0:T(8,128)(2,1)S(1)} %copy-done.16, bf16[128,3840]{1,0:T(8,128)(2,1)} %copy-done.17), kind=kOutput, calls=%fused_computation.45 | convolution fusion | flops 5037096960 | bytes 81264640 | tf_op jit(solution)/shard_map/tr,tf->rf/dot_general | solution.py:156
  1215.9 78.4 %pad_maximum_fusion = f32[2560,11520]{1,0:T(8,128)} fusion(f32[2560,3840]{1,0:T(8,128)} %convolution_bitcast_fusion, f32[2560,7680]{1,0:T(8,128)} %fusion.22), kind=kLoop, calls=%fused_computation.1 | loop fusion | flops 29491200 | bytes 235929600 | tf_op jit(solution)/shard_map/concatenate | solution.py:154
  1296.4 3.4 fusion.35
  1299.8 280.7 %all-reduce.1 = f32[2,2560]{1,0:T(2,128)S(1)} all-reduce(f32[2,2560]{1,0:T(2,128)S(1)} %pad_maximum_fusion.15), channel_id=5, replica_groups=mesh['batch'=2,'seq'=32,'tensor'=2] {'batch','seq'}, use_global_device_ids=true, to_apply=%region_17.18.clone | all-reduce | flops 5120 | bytes 40960
  1580.5 0.7 multiply_subtract_fusion.4
  1581.2 1.5 fusion.37
  1582.6 1.9 multiply_subtract_fusion.3
  1584.5 2.6 multiply_subtract_fusion.1
  1587.1 557.8 %reduce-scatter.14.cloned.1.call-done = f32[40,11520]{1,0:T(8,128)} async-done(((f32[2560,11520]{1,0:T(8,128)}), f32[40,11520]{1,0:T(8,128)}) %reduce-scatter.14.cloned.1.call-update) | async-done | bytes 1843216
  2144.9 5.9 multiply_subtract_fusion
  (145 shorter events, 5.9 us)
Async XLA Ops:
  7.2 109.9 %all-gather.7.cloned.1.call-start = ((), (), s32[]{:S(2)}) async-start(), calls=%async_computation.3 | async-start | bytes 2662400 | tf_op jit(solution)/shard_map/all_gather | solution.py:78
  8.8 218.9 %all-gather.11.cloned.1.call-start = ((), (), s32[]{:S(2)}) async-start(), calls=%async_computation.5 | async-start | bytes 6656000 | tf_op jit(solution)/shard_map/all_gather | solution.py:77
  10.4 265.1 %all-gather.9.cloned.1.call-start = ((), (), s32[]{:S(2)}) async-start(), calls=%async_computation.4 | async-start | bytes 4325376 | tf_op jit(solution)/shard_map/all_gather | solution.py:96
  93.8 27.8 %copy-start.33 = (f32[128]{0:T(128)}, f32[128]{0:T(128)S(1)}, u32[]{:S(2)}) copy-start(f32[128]{0:T(128)S(1)} %multiply_exponential_fusion) | copy-start | bytes 1540
  93.9 27.8 %copy-start.35 = (f32[128]{0:T(128)}, f32[128]{0:T(128)S(1)}, u32[]{:S(2)}) copy-start(f32[128]{0:T(128)S(1)} %fusion.87) | copy-start | bytes 1540
  93.9 1019.0 %copy-start.18 = (f32[2560]{0:T(1024)}, f32[2560]{0:T(1024)S(1)}, u32[]{:S(2)}) copy-start(f32[2560]{0:T(1024)S(1)} %get-tuple-element.73) | copy-start | bytes 30724
  95.2 24.5 %copy-start.40 = (f32[128]{0:T(128)}, f32[128]{0:T(128)S(1)}, u32[]{:S(2)}) copy-start(f32[128]{0:T(128)S(1)} %fusion.38) | copy-start | bytes 1540
  95.3 1017.7 %copy-start.31 = (f32[128]{0:T(128)}, f32[128]{0:T(128)S(1)}, u32[]{:S(2)}) copy-start(f32[128]{0:T(128)S(1)} %fusion.76) | copy-start | bytes 1540
  117.1 3.7 copy-start.21
  117.1 110.6 %copy-start = (bf16[128,2560]{1,0:T(8,128)(2,1)S(1)}, bf16[128,2560]{1,0:T(8,128)(2,1)}, u32[]{:S(2)}) copy-start(bf16[128,2560]{1,0:T(8,128)(2,1)} %param.17) | copy-start | bytes 1966084
  120.8 265.5 %all-gather.13.cloned.1.call-start = ((), (), s32[]{:S(2)}) async-start(), calls=%async_computation.6 | async-start | bytes 6656000 | tf_op jit(solution)/shard_map/all_gather | solution.py:79
  121.5 324.1 %all-reduce.8.cloned.1.call-start = ((), (), s32[]{:S(2)}) async-start(), calls=%async_computation.7 | async-start | bytes 2621440 | tf_op jit(solution)/shard_map/psum | solution.py:125
  123.6 157.5 %copy-start.28 = (pred[128,2176]{0,1:T(8,128)(4,1)}, pred[128,2176]{0,1:T(8,128)(4,1)S(1)}, u32[]{:S(2)}) copy-start(pred[128,2176]{0,1:T(8,128)(4,1)S(1)} %fusion.44) | copy-start | bytes 835588
  233.8 47.3 %copy-start.22 = (bf16[128,5,128]{2,0,1:T(8,128)(2,1)}, bf16[128,5,128]{2,0,1:T(8,128)(2,1)S(1)}, u32[]{:S(2)}) copy-start(bf16[128,5,128]{2,0,1:T(8,128)(2,1)S(1)} %get-tuple-element.101) | copy-start | bytes 491524
  286.5 106.2 %copy-start.11 = (bf16[256,5,128]{2,0,1:T(8,128)(2,1)}, bf16[256,5,128]{2,0,1:T(8,128)(2,1)S(1)}, u32[]{:S(2)}) copy-start(bf16[256,5,128]{2,0,1:T(8,128)(2,1)S(1)} %fusion.41) | copy-start | bytes 983044
  386.3 6.5 copy-start.5
  392.7 373.7 %all-gather.15.cloned.1.call-start = ((), (), s32[]{:S(2)}) async-start(), calls=%async_computation.8 | async-start | bytes 59904000 | tf_op jit(solution)/shard_map/all_gather | solution.py:82
  393.8 476.2 %all-reduce.12.cloned.1.call-start = ((), (), s32[]{:S(2)}) async-start(), calls=%async_computation.10 | async-start | bytes 2621440 | tf_op jit(solution)/shard_map/psum | solution.py:148
  447.5 327.1 %copy-start.7 = (bf16[128,2560]{1,0:T(8,128)(2,1)}, bf16[128,2560]{1,0:T(8,128)(2,1)S(1)}, u32[]{:S(2)}) copy-start(bf16[128,2560]{1,0:T(8,128)(2,1)S(1)} %multiply_convert_fusion.2) | copy-start | bytes 1966084
  774.6 8.2 copy-start.9
  792.3 11.1 copy-start.17
  792.3 11.1 copy-start.15
  803.4 11.8 copy-start.13
  815.1 96.7 %all-reduce.10.cloned.1.call-start = ((), (), s32[]{:S(2)}) async-start(), calls=%async_computation.9 | async-start | bytes 1310720 | tf_op jit(solution)/shard_map/psum | solution.py:132
  826.6 222.0 %reduce-scatter.10.cloned.1.call-start = ((), (), s32[]{:S(2)}) async-start(), calls=%async_computation.11 | async-start | bytes 8650752 | tf_op jit(solution)/shard_map/reduce_scatter | solution.py:203
  914.8 140.4 %copy-start.2 = (f32[128,2560]{1,0:T(8,128)}, f32[128,2560]{1,0:T(8,128)S(1)}, u32[]{:S(2)}) copy-start(f32[128,2560]{1,0:T(8,128)S(1)} %get-tuple-element.96) | copy-start | bytes 3932164
  919.4 4.5 slice-start
  919.4 4.5 slice-start.1
  924.0 2.3 copy-start.23
  924.7 1.6 copy-start.4
  956.6 3.7 copy-start.29
  956.6 154.1 %all-reduce.14.cloned.1.call-start = ((), (), s32[]{:S(2)}) async-start(), calls=%async_computation.14 | async-start | bytes 3145728 | tf_op jit(solution)/shard_map/psum | solution.py:210
  1048.6 6.7 copy-start.12
  1048.6 534.1 %reduce-scatter.12.cloned.1.call-start = ((), (), s32[]{:S(2)}) async-start(), calls=%async_computation.12 | async-start | bytes 31948800 | tf_op jit(solution)/shard_map/reduce_scatter | solution.py:231
  1055.3 57.3 %copy-start.34 = (f32[128]{0:T(128)S(1)}, f32[128]{0:T(128)}, u32[]{:S(2)}) copy-start(f32[128]{0:T(128)} %copy-done.33) | copy-start | bytes 1540
  1055.3 57.3 %copy-start.36 = (f32[128]{0:T(128)S(1)}, f32[128]{0:T(128)}, u32[]{:S(2)}) copy-start(f32[128]{0:T(128)} %copy-done.35) | copy-start | bytes 1540
  1111.6 4.6 copy-start.24
  1113.0 3.3 copy-start.26
  1169.8 1.1 copy-start.10
  1169.8 1.4 copy-start.14
  1169.8 17.2 copy-start.8
  1169.9 17.1 copy-start.16
  1169.9 975.0 %reduce-scatter.14.cloned.1.call-start = ((), (), s32[]{:S(2)}) async-start(), calls=%async_computation.13 | async-start | bytes 119808000
  1294.3 0.7 copy-start.42
  1294.3 1.9 copy-start.30
  1294.3 1.9 copy-start.1
  1294.4 1.9 copy-start.19
  1294.4 1.9 copy-start.25
  1294.4 1.9 copy-start.27
  1294.4 1.9 copy-start.32
  1296.3 284.2 %copy-start.41 = (f32[128]{0:T(128)S(1)}, f32[128]{0:T(128)}, u32[]{:S(2)}) copy-start(f32[128]{0:T(128)} %copy-done.40) | copy-start | bytes 1540
  1296.3 284.2 %copy-start.37 = (f32[2,40]{1,0:T(2,128)S(1)}, f32[2,40]{1,0:T(2,128)}, u32[]{:S(2)}) copy-start(f32[2,40]{1,0:T(2,128)} %param.31) | copy-start | bytes 964
  1296.3 284.2 %copy-start.38 = (f32[2,40]{1,0:T(2,128)S(1)}, f32[2,40]{1,0:T(2,128)}, u32[]{:S(2)}) copy-start(f32[2,40]{1,0:T(2,128)} %param.33) | copy-start | bytes 964
  1296.3 284.2 %copy-start.39 = (f32[2,40]{1,0:T(2,128)S(1)}, f32[2,40]{1,0:T(2,128)}, u32[]{:S(2)}) copy-start(f32[2,40]{1,0:T(2,128)} %param.32) | copy-start | bytes 964
  1296.3 284.8 %copy-start.3 = (f32[128,2560]{1,0:T(8,128)S(1)}, f32[128,2560]{1,0:T(8,128)}, u32[]{:S(2)}) copy-start(f32[128,2560]{1,0:T(8,128)} %copy-done.2) | copy-start | bytes 3932164
  1581.2 3.3 copy-start.20
  1582.6 562.3 %copy-start.6 = (f32[3,40,3840]{2,1,0:T(8,128)S(1)}, f32[3,40,3840]{2,1,0:T(8,128)}, u32[]{:S(2)}) copy-start(f32[3,40,3840]{2,1,0:T(8,128)} %param.28) | copy-start | bytes 5529604
Sparse Core Ops, SparseCore 0:
  10.3 106.7 all-gather.6
  119.4 108.2 all-gather.10
  230.6 44.9 all-gather.8
  277.7 108.5 all-gather.12
  392.8 52.7 all-reduce.7
  447.8 318.5 all-gather.14
  815.3 54.6 all-reduce.11
  873.0 38.7 all-reduce.9
  956.7 91.8 reduce-scatter.9
  1051.5 59.1 all-reduce.13
  1170.0 336.3 reduce-scatter.11
  1508.8 636.1 reduce-scatter.13
where the time goes:
time: 2170 us; the launch traced here: 2160 us
  waiting for transfers between devices  1410 us (65%)
  blocking collectives  363 us (17%)
  matrix products  177 us (8%)
  other arithmetic  137 us (6%)
  local copies, waits for them, and re-layouts  54.6 us (3%)
    unnamed x13, waiting for transfers between devices  558 us
    all_gather x1, waiting for transfers between devices, local(): lax.all_gather(feedforward_weight.astype(jnp.bfloat16), ('batch', 'seq'),...  319 us
    unnamed x1, blocking collectives  281 us
    all_gather x1, waiting for transfers between devices, local(): lax.all_gather(query_weight.astype(jnp.bfloat16), ('batch', 'seq'), axis=...  104 us
    all_gather x1, waiting for transfers between devices, local(): lax.all_gather(output_weight.astype(jnp.bfloat16), ('batch', 'seq'), axis...  99.8 us
    all_gather x1, blocking collectives, local(): lax.all_gather(norm_gains.astype(jnp.bfloat16), ('batch', 'seq'), axis=1,...  82.3 us
    reduce_scatter x1, waiting for transfers between devices, local(): lax.psum_scatter(full_term, 'seq', scatter_dimension=0, tiled=True)  81.7 us
    concatenate x1, other arithmetic, local(): jnp.concatenate([jnp.einsum('tr,tf->rf', normed_b, gate_up_low, preferred...  78.4 us
  transfers between devices with their start and end apart: 12, of which 11 were waited for; matrix products, arithmetic and copies ran while one was open for 9% of the time, Pallas kernels for 0%

commit v1 on v0

v1 whole, which is shorter than its diff:
```python
import math

import jax
import jax.numpy as jnp
from jax import lax
from jax.experimental import pallas as pl
from jax.experimental.pallas import tpu as pltpu
from jax.sharding import Mesh
from jax.sharding import PartitionSpec as P

D = 2560
HEADS = 10
HEAD_DIM = 256
STEP = 10
ROWS = 128
GROUP = 8
OWNED = 40
Q_PART = 160
KV_PART = 64
F_PART = 480
F_PAD = 512
LOCAL_HEADS = 5
TILES = 17
BF = jnp.bfloat16
F32 = jnp.float32
ANY = pl.BlockSpec(memory_space=pl.ANY)
SMEM = pl.BlockSpec(memory_space=pltpu.SMEM)
VMEM = pl.BlockSpec(memory_space=pltpu.VMEM)


def params(mib):
    return pltpu.CompilerParams(vmem_limit_bytes=mib * 1024 * 1024)


def dot(left, right, left_dim, right_dim):
    return lax.dot_general(
        left, right, (((left_dim,), (right_dim,)), ((), ())), preferred_element_type=F32
    )


def shift(value, axis, step):
    return lax.ppermute(value, axis, [(i, (i + step) % 4) for i in range(4)])


def push(value, axis, step):
    return lax.ppermute(value, axis, [(i, i + step) for i in range(4) if 0 <= i + step < 4])


def swap(value, axis):
    return lax.ppermute(value, axis, [(0, 1), (1, 0)])


def place(pieces, index, shape, target):
    count = len(pieces)

    def body(index_ref, *refs):
        out, sems = refs[count], refs[count + 1]
        copies = [
            pltpu.make_async_copy(refs[k], target(out, index_ref, k), sems.at[k])
            for k in range(count)
        ]
        for copy in copies:
            copy.start()
        for copy in copies:
            copy.wait()

    return pl.pallas_call(
        body,
        out_shape=jax.ShapeDtypeStruct(shape, pieces[0].dtype),
        in_specs=[SMEM] + [VMEM] * count,
        out_specs=ANY,
        scratch_shapes=[pltpu.SemaphoreType.DMA((count,))],
        compiler_params=params(24),
    )(index, *pieces)


def ring_pieces(value, axis):
    half = value.shape[0] // 2
    left = shift(value, axis, 1)
    right = shift(value, axis, -1)
    top = shift(left[:half], axis, 1)
    bottom = shift(right[half:], axis, -1)
    return [value, left, right, top, bottom]


def group_pieces(value):
    mine = ring_pieces(value, "x")
    return mine + [swap(piece, "c") for piece in mine]


RING = ((0, None), (1, None), (2, None), (3, 0), (3, 1))


def group_gather(value, index):
    half = value.shape[0] // 2
    shape = (GROUP, 2, half) + value.shape[1:]
    pieces = []
    for k, piece in enumerate(group_pieces(value)):
        if RING[k % 5][1] is None:
            piece = piece.reshape((2, half) + value.shape[1:])
        pieces.append(piece)

    def target(out, index_ref, k):
        slot, part = RING[k % 5]
        spot = index_ref[slot + 4 * (k // 5)]
        return out.at[spot] if part is None else out.at[spot, part]

    out = place(pieces, index, shape, target)
    return out.reshape((GROUP,) + value.shape)


def row_gather(value, group_index, outer_index):
    width = value.shape[1]
    pair = jnp.stack([value, swap(value, "b")])
    pieces = ring_pieces(pair, "y")

    def outer_target(out, index_ref, k):
        slot, part = RING[k]
        spot = index_ref[slot]
        return out.at[spot] if part is None else out.at[spot, part]

    by_y = place(
        [p if RING[k][1] is None else p.reshape(OWNED, width) for k, p in enumerate(pieces)],
        outer_index,
        (4, 2, OWNED, width),
        outer_target,
    )
    block = by_y.transpose(1, 0, 2, 3).reshape(8, OWNED, width)
    first = lax.axis_index("b") * 4
    block = jnp.roll(block, first, axis=0)
    half = 4

    def target(out, index_ref, k):
        slot, part = RING[k % 5]
        spot = index_ref[slot + 4 * (k // 5)]
        if part is None:
            return out.at[:, spot]
        return out.at[pl.ds(part * half, half), spot]

    out = place(group_pieces(block), group_index, (8, GROUP, OWNED, width), target)
    return out.reshape(D, width)


def group_scatter(parts, x, c):
    low = lax.optimization_barrier(parts.astype(BF))
    shaped = low.reshape((4, 2) + low.shape[1:])
    theirs = lax.dynamic_index_in_dim(shaped, 1 - c, 1, keepdims=False)
    mine = lax.dynamic_index_in_dim(shaped, c, 1, keepdims=False)
    both = mine.astype(F32) + swap(theirs, "c").astype(F32)
    half = both.shape[1] // 2

    def block(step):
        return lax.dynamic_index_in_dim(both, (x + step) % 4, 0, keepdims=False)

    own, left, right, far = block(0), block(3), block(1), block(2)
    far_top = shift(far[:half].astype(BF), "x", -1)
    far_bottom = shift(far[half:].astype(BF), "x", 1)
    left_bottom = shift(left[half:].astype(BF), "x", -1)
    right_top = shift(right[:half].astype(BF), "x", 1)
    left_top = shift((left[:half] + far_top.astype(F32)).astype(BF), "x", -1)
    right_bottom = shift((right[half:] + far_bottom.astype(F32)).astype(BF), "x", 1)
    top = own[:half] + left_top.astype(F32) + right_top.astype(F32)
    bottom = own[half:] + left_bottom.astype(F32) + right_bottom.astype(F32)
    return jnp.concatenate([top, bottom], axis=0)


def tensor_sum(value):
    low = lax.optimization_barrier(value.astype(BF))
    return low.astype(F32) + swap(low, "t").astype(F32)


def exchange(value):
    return lax.all_to_all(value, ("x", "c"), split_axis=0, concat_axis=0, tiled=True)


def pack_small(q_ref, kv_ref, gain_ref, out_ref):
    rest = jnp.zeros((OWNED, 256 - Q_PART - KV_PART - 2), F32)
    for j in range(GROUP):
        out_ref[j] = jnp.concatenate(
            [
                q_ref[:, Q_PART * j : Q_PART * (j + 1)],
                kv_ref[:, KV_PART * j : KV_PART * (j + 1)],
                gain_ref[...],
                rest,
            ],
            axis=1,
        ).astype(BF)


def pack_feed(w_ref, out_ref):
    rest = jnp.zeros((OWNED, F_PAD - F_PART), F32)
    for j in range(GROUP):
        out_ref[j] = jnp.concatenate(
            [w_ref[0, :, F_PART * j : F_PART * (j + 1)], rest], axis=1
        ).astype(BF)


def adam(weight, grad, moment, second, rate, decay):
    moment_new = 0.9 * moment + 0.1 * grad
    second_new = 0.95 * second + 0.05 * grad * grad
    ratio = moment_new / (1.0 - 0.9**STEP) / (jnp.sqrt(second_new / (1.0 - 0.95**STEP)) + 1e-08)
    return (moment_new, second_new, weight - rate * (ratio + decay * weight))


def adam_columns(part, start, rate):
    def body(g_ref, w_ref, m_ref, v_ref, mo_ref, vo_ref, wo_ref):
        grad = jnp.concatenate(
            [g_ref[j, :, start : start + part].astype(F32) for j in range(GROUP)], axis=1
        )
        index = (0,) if len(w_ref.shape) == 3 else (slice(None),)
        m, v, w = adam(w_ref[index], grad, m_ref[index], v_ref[index], rate, 0.1)
        mo_ref[index] = m
        vo_ref[index] = v
        wo_ref[index] = w

    return body


def attend_place(base_ref, i):
    block = base_ref[0] * 8 + base_ref[1] + (i - 16 + 32)
    return block % 8, base_ref[0] + 4 - block // 8, block >= 32


def attend(base_ref, q_ref, kv_ref, p_ref, a_ref, qs):
    for h in range(LOCAL_HEADS):
        qs[:, ROWS * h : ROWS * (h + 1)] = q_ref[h]
    width = LOCAL_HEADS * ROWS
    key_at = lax.broadcasted_iota(jnp.int32, (ROWS, width), 0)
    query_at = lax.broadcasted_iota(jnp.int32, (ROWS, width), 1) % ROWS
    top = jnp.full((1, width), -1e30, F32)
    for i in range(TILES):
        at, back, exists = attend_place(base_ref, i)
        scores = dot(kv_ref[at, back, :HEAD_DIM, :], qs[...], 0, 0) * (HEAD_DIM**-0.5)
        if i == 0:
            scores = jnp.where((key_at > query_at) & exists, scores, -1e30)
        elif i == TILES - 1:
            scores = jnp.where(key_at <= query_at, scores, -1e30)
        else:
            scores = jnp.where(exists, scores, -1e30)
        p_ref[i] = scores
        top = jnp.maximum(top, jnp.max(scores, axis=0, keepdims=True))
    total = jnp.zeros((1, width), F32)
    for i in range(TILES):
        weights = jnp.exp(p_ref[i] - top)
        p_ref[i] = weights
        total = total + jnp.sum(weights, axis=0, keepdims=True)
    scale = 1.0 / total
    result = jnp.zeros((HEAD_DIM, width), F32)
    for i in range(TILES):
        at, back, _ = attend_place(base_ref, i)
        probs = p_ref[i] * scale
        p_ref[i] = probs
        result = result + dot(kv_ref[at, back, HEAD_DIM:, :], probs.astype(BF), 1, 0)
    for h in range(LOCAL_HEADS):
        a_ref[h] = result[:, ROWS * h : ROWS * (h + 1)].astype(BF)


def attend_back(base_ref, q_ref, kv_ref, p_ref, da_ref, dq_ref, dkv_ref, qs, das, dps):
    width = LOCAL_HEADS * ROWS
    for h in range(LOCAL_HEADS):
        qs[:, ROWS * h : ROWS * (h + 1)] = q_ref[h]
        das[:, ROWS * h : ROWS * (h + 1)] = da_ref[h]
    dkv_ref[...] = jnp.zeros(dkv_ref.shape, BF)
    delta = jnp.zeros((1, width), F32)
    for i in range(TILES):
        at, back, _ = attend_place(base_ref, i)
        probs = p_ref[i]
        d_probs = dot(kv_ref[at, back, HEAD_DIM:, :], das[...], 0, 0)
        dps[i] = d_probs
        delta = delta + jnp.sum(probs * d_probs, axis=0, keepdims=True)
        dkv_ref[at, back, HEAD_DIM:, :] = dot(das[...], probs.astype(BF), 1, 1).astype(BF)
    dq = jnp.zeros((HEAD_DIM, width), F32)
    for i in range(TILES):
        at, back, _ = attend_place(base_ref, i)
        d_scores = (p_ref[i] * (dps[i] - delta)).astype(BF)
        dq = dq + dot(kv_ref[at, back, :HEAD_DIM, :], d_scores, 1, 0)
        dk = dot(qs[...], d_scores, 1, 1) * (HEAD_DIM**-0.5)
        dkv_ref[at, back, :HEAD_DIM, :] = dk.astype(BF)
    for h in range(LOCAL_HEADS):
        dq_ref[h] = dq[:, ROWS * h : ROWS * (h + 1)] * (HEAD_DIM**-0.5)


def rms_rate(values):
    return lax.rsqrt(jnp.mean(values * values, axis=-1, keepdims=True) + 1e-06)


def rotate(values, cosine, sine):
    first, second = values[..., 0, :, :], values[..., 1, :, :]
    return jnp.stack([first * cosine - second * sine, second * cosine + first * sine], axis=-3)


def local(
    tokens,
    cotangent,
    query_weight,
    query_moment,
    query_second,
    keyvalue_weight,
    keyvalue_moment,
    keyvalue_second,
    output_weight,
    output_moment,
    output_second,
    feedforward_weight,
    feedforward_moment,
    feedforward_second,
    norm_gains,
    gains_moment,
    gains_second,
):
    x, y, c = lax.axis_index("x"), lax.axis_index("y"), lax.axis_index("c")
    j = 2 * x + c
    wide_rate = 1.5 * D**-0.5
    output_rate = 1.5 * (HEADS * HEAD_DIM // 32) ** -0.5
    ring_x = jnp.stack([x, (x + 3) % 4, (x + 1) % 4, (x + 2) % 4]).astype(jnp.int32)
    group_index = jnp.concatenate([2 * ring_x + c, 2 * ring_x + 1 - c])
    outer_index = jnp.stack([y, (y + 3) % 4, (y + 1) % 4, (y + 2) % 4]).astype(jnp.int32)
    base = jnp.stack([y, j]).astype(jnp.int32)

    small = pl.pallas_call(
        pack_small,
        out_shape=jax.ShapeDtypeStruct((GROUP, OWNED, 256), BF),
        in_specs=[VMEM] * 3,
        out_specs=VMEM,
    )(query_weight, keyvalue_weight, norm_gains.T)
    feed = pl.pallas_call(
        pack_feed,
        grid=(3,),
        out_shape=jax.ShapeDtypeStruct((GROUP, OWNED, 3 * F_PAD), BF),
        in_specs=[pl.BlockSpec((1, OWNED, 8 * F_PART), lambda k: (k, 0, 0))],
        out_specs=pl.BlockSpec((GROUP, OWNED, F_PAD), lambda k: (0, 0, k)),
    )(feedforward_weight)
    small = exchange(small).reshape(GROUP * OWNED, 256)
    w_small = lax.all_gather(small, ("b", "y"), axis=0, tiled=True)
    feed = exchange(feed).reshape(GROUP * OWNED, 3 * F_PAD)
    w_feed = lax.all_gather(feed, ("b", "y"), axis=0, tiled=True)
    w_output = row_gather(output_weight.astype(BF), group_index, outer_index)
    w_back = row_gather(
        jnp.concatenate([query_weight, keyvalue_weight], axis=1).astype(BF),
        group_index,
        outer_index,
    )
    gains = w_small[:, Q_PART + KV_PART : Q_PART + KV_PART + 2].astype(F32).T

    inflow = tokens.astype(F32)
    group_tokens = group_gather(tokens, group_index)
    group_flow = group_tokens.astype(F32)
    normed_a = (group_flow * rms_rate(group_flow) * gains[0]).astype(BF).reshape(1024, D)
    raw = dot(w_small, normed_a, 0, 1).astype(BF)
    raw = exchange(raw.reshape(256, GROUP, ROWS).transpose(1, 0, 2))
    steps = jnp.arange(HEAD_DIM // 2, dtype=F32)
    freqs = jnp.exp(steps * (-2.0 * math.log(10000.0) / HEAD_DIM))
    places = ((y * GROUP + j) * ROWS + jnp.arange(ROWS, dtype=jnp.int32)).astype(F32)
    angle = freqs[:, None] * places[None, :]
    cosine, sine = jnp.cos(angle), jnp.sin(angle)
    q_raw = raw[:, :Q_PART].astype(F32).reshape(LOCAL_HEADS, 2, HEAD_DIM // 2, ROWS)
    kv_raw = raw[:, Q_PART : Q_PART + KV_PART].astype(F32).reshape(2, 2, HEAD_DIM // 2, ROWS)
    queries = rotate(q_raw, cosine, sine).astype(BF).reshape(LOCAL_HEADS, HEAD_DIM, ROWS)
    keys = rotate(kv_raw[0], cosine, sine)
    pair = jnp.stack([keys, kv_raw[1]]).astype(BF).reshape(2 * HEAD_DIM, ROWS)
    spans = jnp.concatenate([pair, push(pair, "y", 1), push(pair, "y", 2)])
    spans = group_gather(spans, group_index).reshape(GROUP, 3, 2 * HEAD_DIM, ROWS)

    width = LOCAL_HEADS * ROWS
    probs, attended = pl.pallas_call(
        attend,
        out_shape=(
            jax.ShapeDtypeStruct((TILES, ROWS, width), F32),
            jax.ShapeDtypeStruct((LOCAL_HEADS, HEAD_DIM, ROWS), BF),
        ),
        in_specs=[SMEM, VMEM, VMEM],
        out_specs=(VMEM, VMEM),
        scratch_shapes=[pltpu.VMEM((HEAD_DIM, width), BF)],
        compiler_params=params(40),
    )(base, queries, spans)
    attended = attended.reshape(LOCAL_HEADS * HEAD_DIM, ROWS)
    residual = inflow + tensor_sum(dot(attended, w_output, 0, 1))

    rate_b = rms_rate(residual)
    normed_b = (residual * rate_b * gains[1]).astype(BF)
    group_b = group_gather(normed_b, group_index).reshape(1024, D)
    group_back = group_gather(cotangent, group_index).reshape(1024, D)
    gate_up = dot(group_b, w_feed[:, : 2 * F_PAD], 1, 0)
    gate, up = gate_up[:, :F_PAD], gate_up[:, F_PAD:]
    d_hidden = dot(group_back, w_feed[:, 2 * F_PAD :], 1, 0)
    root = math.sqrt(2.0 / math.pi)
    bend = jnp.tanh(root * (gate + 0.044715 * gate * gate * gate))
    gelu = 0.5 * gate * (1.0 + bend)
    slope = 0.5 * (1.0 + bend) + 0.5 * gate * (1.0 - bend * bend) * root * (
        1.0 + 3.0 * 0.044715 * gate * gate
    )
    hidden = (gelu * up).astype(BF)
    d_gate_up = jnp.concatenate(
        [(d_hidden * up * slope).astype(BF), (d_hidden * gelu).astype(BF)], axis=1
    )
    normb_part = dot(d_gate_up, w_feed[:, : 2 * F_PAD], 1, 1)
    grad_normb = tensor_sum(group_scatter(normb_part.reshape(GROUP, ROWS, D), x, c))
    feed_part = dot(hidden, w_feed[:, 2 * F_PAD :], 1, 1)
    out_sum = tensor_sum(group_scatter(feed_part.reshape(GROUP, ROWS, D), x, c))
    out_tokens = (residual + out_sum).astype(BF)
    down_grad = dot(group_back, hidden, 0, 0).astype(BF)
    gate_grad = dot(group_b, d_gate_up, 0, 0).astype(BF)
    down_grad = lax.psum_scatter(down_grad, ("b", "y"), scatter_dimension=0, tiled=True)
    gate_grad = lax.psum_scatter(gate_grad, ("b", "y"), scatter_dimension=0, tiled=True)

    scaled = grad_normb * gains[1]
    grad_resid = (
        cotangent.astype(F32)
        + rate_b * scaled
        - residual * rate_b**3 * jnp.mean(scaled * residual, axis=-1, keepdims=True)
    )
    gain_b = jnp.sum(grad_normb * residual * rate_b, axis=0)
    resid_low = grad_resid.astype(BF)
    grad_att = dot(w_output, resid_low, 0, 1).astype(BF).reshape(LOCAL_HEADS, HEAD_DIM, ROWS)

    grad_q, grad_spans = pl.pallas_call(
        attend_back,
        out_shape=(
            jax.ShapeDtypeStruct((LOCAL_HEADS, HEAD_DIM, ROWS), F32),
            jax.ShapeDtypeStruct((GROUP, 3, 2 * HEAD_DIM, ROWS), BF),
        ),
        in_specs=[SMEM, VMEM, VMEM, VMEM, VMEM],
        out_specs=(VMEM, VMEM),
        scratch_shapes=[
            pltpu.VMEM((HEAD_DIM, width), BF),
            pltpu.VMEM((HEAD_DIM, width), BF),
            pltpu.VMEM((TILES, ROWS, width), F32),
        ],
        compiler_params=params(44),
    )(base, queries, spans, probs, grad_att)
    back = group_scatter(grad_spans.reshape(GROUP, 3 * 2 * HEAD_DIM, ROWS), x, c)
    back = back.reshape(3, 2 * HEAD_DIM, ROWS)
    back = (
        back[0]
        + push(back[1].astype(BF), "y", -1).astype(F32)
        + push(back[2].astype(BF), "y", -2).astype(F32)
    )
    back = tensor_sum(back).reshape(2, 2, HEAD_DIM // 2, ROWS)
    pair_grad = (
        jnp.stack([rotate(back[0], cosine, -sine), back[1]]).astype(BF).reshape(2 * HEAD_DIM, ROWS)
    )
    query_grad = (
        rotate(grad_q.reshape(LOCAL_HEADS, 2, HEAD_DIM // 2, ROWS), cosine, -sine)
        .astype(BF)
        .reshape(LOCAL_HEADS * HEAD_DIM, ROWS)
    )

    all_grad = jnp.concatenate([query_grad, pair_grad * jnp.asarray(0.5, BF)])
    norma_part = dot(all_grad, w_back, 0, 1)
    rate_a = rms_rate(inflow)
    gain_a = jnp.sum(norma_part * inflow * rate_a, axis=0)
    grad_norma = tensor_sum(norma_part)
    scaled = grad_norma * gains[0]
    input_grad = (
        grad_resid
        + rate_a * scaled
        - inflow * rate_a**3 * jnp.mean(scaled * inflow, axis=-1, keepdims=True)
    )

    sent = jnp.concatenate(
        [query_grad.reshape(GROUP, Q_PART, ROWS), pair_grad.reshape(GROUP, KV_PART, ROWS)], axis=1
    )
    sent = exchange(sent).transpose(1, 0, 2).reshape(Q_PART + KV_PART, 1024)
    small_grad = dot(normed_a, sent, 0, 1)
    gain_terms = jnp.stack([gain_a, 0.5 * gain_b], axis=1)
    small_grad = jnp.concatenate(
        [small_grad, gain_terms, jnp.zeros((D, 256 - Q_PART - KV_PART - 2), F32)], axis=1
    ).astype(BF)
    small_grad = lax.psum_scatter(small_grad, ("b", "y"), scatter_dimension=0, tiled=True)
    small_grad = exchange(small_grad.reshape(GROUP, OWNED, 256))
    sent = exchange(attended.reshape(GROUP, Q_PART, ROWS)).transpose(1, 0, 2)
    group_resid = group_gather(resid_low, group_index).reshape(1024, D)
    output_grad = dot(group_resid, sent.reshape(Q_PART, 1024), 0, 1).astype(BF)
    output_grad = lax.psum_scatter(output_grad, ("b", "y"), scatter_dimension=0, tiled=True)
    output_grad = exchange(output_grad.reshape(GROUP, OWNED, Q_PART))
    down_grad = exchange(down_grad.reshape(GROUP, OWNED, F_PAD))
    gate_grad = exchange(gate_grad.reshape(GROUP, OWNED, 2 * F_PAD))

    def update(grad, weight, moment, second, part, start, rate):
        return pl.pallas_call(
            adam_columns(part, start, rate),
            out_shape=(jax.ShapeDtypeStruct(weight.shape, F32),) * 3,
            in_specs=[VMEM] * 4,
            out_specs=(VMEM,) * 3,
            compiler_params=params(32),
        )(grad, weight, moment, second)

    query_new = update(small_grad, query_weight, query_moment, query_second, Q_PART, 0, wide_rate)
    pair_new = update(
        small_grad, keyvalue_weight, keyvalue_moment, keyvalue_second, KV_PART, Q_PART, wide_rate
    )
    output_new = update(
        output_grad, output_weight, output_moment, output_second, Q_PART, 0, output_rate
    )
    feed_grad = jnp.concatenate([gate_grad, down_grad], axis=2)
    matrix = pl.BlockSpec((1, OWNED, 8 * F_PART), lambda k: (k, 0, 0))
    feed_new = pl.pallas_call(
        adam_columns(F_PART, 0, wide_rate),
        grid=(3,),
        out_shape=(jax.ShapeDtypeStruct(feedforward_weight.shape, F32),) * 3,
        in_specs=[pl.BlockSpec((GROUP, OWNED, F_PAD), lambda k: (0, 0, k))] + [matrix] * 3,
        out_specs=(matrix,) * 3,
        compiler_params=params(32),
    )(feed_grad, feedforward_weight, feedforward_moment, feedforward_second)
    gain_grad = jnp.sum(
        small_grad[:, :, Q_PART + KV_PART : Q_PART + KV_PART + 2].astype(F32), axis=0
    ).T
    gain_grad = gain_grad + swap(gain_grad, "t")
    gains_new = adam(norm_gains, gain_grad, gains_moment, gains_second, 0.3, 0.0)
    return (
        out_tokens,
        input_grad,
        *query_new,
        *pair_new,
        *output_new,
        *feed_new,
        *gains_new,
    )


def solution(mesh):
    grid = Mesh(mesh.devices.reshape(2, 4, 4, 2, 2), ("b", "y", "x", "c", "t"))
    rows = ("b", "y", "x", "c")
    token = P(rows, None)
    split = P(rows, "t")
    whole = P(rows, None)
    feed = P(None, rows, "t")
    gain = P(None, rows)
    weights = (split,) * 3 + (whole,) * 3 + (split,) * 3 + (feed,) * 3 + (gain,) * 3
    return jax.shard_map(
        local,
        mesh=grid,
        in_specs=(token, token) + weights,
        out_specs=(token, token) + weights,
        check_vma=False,
    )
```

time: 2170 us -> 714 us (0.33)
  waiting for transfers between devices: 1410 us -> 284 us
  blocking collectives: 363 us -> 30.7 us
  starting transfers between devices: 1.6 us -> 144 us
  matrix products: 177 us -> 61.4 us
  other arithmetic: 137 us -> 52.1 us
  Pallas kernels: 0 us -> 48.7 us
    all_gather x5 -> x2, waiting for transfers between devices: 586 us -> 0.01 us  [the longest x1 0.01 us: local(): w_small = lax.all_gather(small, ('b', 'y'), axis=0, tiled=True)]
    unnamed x13 -> x6, waiting for transfers between devices: 558 us -> 0.1 us
    unnamed x1 -> x0, blocking collectives: 281 us -> none
    ppermute x0 -> x104, waiting for transfers between devices: none -> 197 us  [the longest x54 132 us: shift(): return lax.ppermute(value, axis, [(i, (i + step) % 4) for i in range(4)])]
    psum x4 -> x0, waiting for transfers between devices: 183 us -> none  [the longest x1 51.3 us: local(): residual = inflow + lax.psum(branch_part, 'tensor')]
    ppermute x0 -> x104, starting transfers between devices: none -> 114 us  [the longest x54 77.4 us: shift(): return lax.ppermute(value, axis, [(i, (i + step) % 4) for i in range(4)])]
    dot_general x22 -> x12, matrix products: 171 us -> 61.4 us  [dot(): lax.dot_general(left, right, (((left_dim,), (right_dim,)), ((), ())), pre...]
    concatenate x5 -> x13, other arithmetic: 107 us -> 6.05 us  [the longest x3 2.87 us: local(): jnp.concatenate([query_weight, keyvalue_weight], axis=1).astype(BF)]
  transfers between devices with their start and end apart: 12 -> 117, of which waited for: 11 -> 38; matrix products, arithmetic and copies ran while one was open for 9% -> 19% of each run, Pallas kernels for 0% -> 6%
where the time goes in v1:
time: 714 us; the launch traced here: 703 us
  waiting for transfers between devices  284 us (40%)
  starting transfers between devices  144 us (20%)
  local copies, waits for them, and re-layouts  66.3 us (9%)
  matrix products  61.4 us (9%)
  other arithmetic  52.1 us (7%)
  Pallas kernels  48.7 us (7%)
  blocking collectives  30.7 us (4%)
  between operations  16.2 us (2%)
    ppermute x54, waiting for transfers between devices, shift(): return lax.ppermute(value, axis, [(i, (i + step) % 4) for i in range(4)])  132 us
    ppermute x54, starting transfers between devices, shift(): return lax.ppermute(value, axis, [(i, (i + step) % 4) for i in range(4)])  77.4 us
    dot_general x12, matrix products, dot(): lax.dot_general(left, right, (((left_dim,), (right_dim,)), ((), ())), pre...  61.4 us
    ppermute x46, waiting for transfers between devices, swap(): return lax.ppermute(value, axis, [(0, 1), (1, 0)])  56 us
    reduce_scatter x1, waiting for transfers between devices, local(): lax.psum_scatter(gate_grad, ('b', 'y'), scatter_dimension=0, tiled=True)  53.4 us
    unnamed x237, local copies, waits for them, and re-layouts  44.8 us
    all_to_all x2, blocking collectives, exchange(): lax.all_to_all(value, ('x', 'c'), split_axis=0, concat_axis=0, tiled=True)  30.7 us
    all_to_all x7, starting transfers between devices, exchange(): lax.all_to_all(value, ('x', 'c'), split_axis=0, concat_axis=0, tiled=True)  29.7 us
  transfers between devices with their start and end apart: 117, of which 38 were waited for; matrix products, arithmetic and copies ran while one was open for 19% of the time, Pallas kernels for 6%

profile of v1, /device:TPU:0, one launch (start us, length us, event | category | flops | bytes accessed | tf_op | source)
XLA Modules:
  0.0 703.2 jit_solution(7551004233215530752)
XLA Ops:
  10.4 11.0 %all_to_all.45 = bf16[8,40,256]{2,1,0:T(8,128)(2,1)} all-to-all(bf16[8,40,256]{2,1,0:T(8,128)(2,1)} %shard_map.296), channel_id=1, replica_groups=mesh['b'=2,'y'=4,'x'=4,'c'=2,'t'=2] {'x','c'}, dimensions={0} | all-to-all | bytes 327680 | tf_op jit(solution)/shard_map/all_to_all | solution.py:173
  21.4 3.4 shard_map.303
  24.9 19.7 %all_to_all.46 = bf16[8,40,1536]{2,1,0:T(8,128)(2,1)} all-to-all(bf16[8,40,1536]{2,1,0:T(8,128)(2,1)} %shard_map.303), channel_id=1, replica_groups=mesh['b'=2,'y'=4,'x'=4,'c'=2,'t'=2] {'x','c'}, dimensions={0} | all-to-all | bytes 1966080 | tf_op jit(solution)/shard_map/all_to_all | solution.py:173
  50.1 12.3 %collective-permute-done = bf16[128,2560]{1,0:T(8,128)(2,1)S(1)} collective-permute-done((bf16[128,2560]{1,0:T(8,128)(2,1)S(1)}, bf16[128,2560]{1,0:T(8,128)(2,1)S(1)}, u32[]{:S(2)}, u32[]{:S(2)}) %collective-permute-start) | collective-permute-done | bytes 655392 | tf_op jit(solution)/shard_map/ppermute | solution.py:42
  66.9 5.4 collective-permute-done.2.refs_3_
  85.1 3.9 fusion.3
  91.5 4.1 all-to-all-start.1
  96.3 3.8 collective-permute-start.24
  100.2 5.1 collective-permute-done.23
  112.8 4.5 collective-permute-start.10
  117.3 3.9 collective-permute-start.9
  121.3 7.1 %collective-permute-done.25.refs_1_ = bf16[8,40,1280]{2,1,0:T(8,128)(2,1)S(1)} collective-permute-done((bf16[8,40,1280]{2,1,0:T(8,128)(2,1)S(1)}, bf16[8,40,1280]{2,1,0:T(8,128)(2,1)S(1)}, u32[]{:S(2)}, u32[]{:S(2)}) %collective-permute-start.25) | collective-permute-done | bytes 819232 | tf_op jit(solution)/shard_map/ppermute | solution.py:42
  132.0 10.1 %collective-permute-done.27.refs_3_ = bf16[4,40,1280]{2,1,0:T(8,128)(2,1)S(1)} collective-permute-done((bf16[4,40,1280]{2,1,0:T(8,128)(2,1)S(1)}, bf16[4,40,1280]{2,1,0:T(8,128)(2,1)S(1)}, u32[]{:S(2)}, u32[]{:S(2)}) %collective-permute-start.27) | collective-permute-done | bytes 409632 | tf_op jit(solution)/shard_map/ppermute | solution.py:42
  142.9 5.4 collective-permute-done.11
  148.3 5.3 collective-permute-done.12
  166.9 5.5 shard_map.299
  172.4 3.6 convolution_convert_fusion.5
  176.0 4.0 collective-permute-start.34
  183.2 12.0 %collective-permute-done.34 = bf16[128,2560]{1,0:T(8,128)(2,1)S(1)} collective-permute-done((bf16[128,2560]{1,0:T(8,128)(2,1)S(1)}, bf16[128,2560]{1,0:T(8,128)(2,1)S(1)}, u32[]{:S(2)}, u32[]{:S(2)}) %collective-permute-start.34) | collective-permute-done | bytes 655392 | tf_op jit(solution)/shard_map/ppermute | solution.py:50
  204.5 18.2 %collective-permute-done.54.refs_3_ = bf16[64,2560]{1,0:T(8,128)(2,1)S(1)} collective-permute-done((bf16[64,2560]{1,0:T(8,128)(2,1)S(1)}, bf16[64,2560]{1,0:T(8,128)(2,1)S(1)}, u32[]{:S(2)}, u32[]{:S(2)}) %collective-permute-start.54) | collective-permute-done | bytes 327712 | tf_op jit(solution)/shard_map/ppermute | solution.py:42
  234.7 4.1 collective-permute-done.37.refs_3_
  260.0 4.2 shard_map.302
  266.5 9.3 %fusion.5 = f32[1024,1024]{0,1:T(8,128)S(1)} fusion(bf16[1024,2560]{1,0:T(8,128)(2,1)} %bitcast.300, bf16[2560,1536]{1,0:T(8,128)(2,1)} %all-gather.5.cloned.1.call-done), kind=kOutput, calls=%fused_computation.13 | convolution fusion | flops 5368709120 | bytes 14680064 | tf_op jit(solution)/shard_map/dot_general | solution.py:36
  275.8 4.5 fusion.17
  291.2 5.9 convolution_convert_fusion.2
  305.3 3.5 collective-permute-done.82
  314.0 3.5 convert_add_fusion.1
  317.6 3.5 collective-permute-start.45
  327.3 7.7 %collective-permute-done.62 = bf16[64,2560]{1,0:T(8,128)(2,1)S(1)} collective-permute-done((bf16[64,2560]{1,0:T(8,128)(2,1)S(1)}, bf16[64,2560]{1,0:T(8,128)(2,1)S(1)}, u32[]{:S(2)}, u32[]{:S(2)}) %collective-permute-start.62) | collective-permute-done | bytes 327712 | tf_op jit(solution)/shard_map/ppermute | solution.py:42
  338.8 8.2 %collective-permute-done.66 = bf16[64,2560]{1,0:T(8,128)(2,1)S(1)} collective-permute-done((bf16[64,2560]{1,0:T(8,128)(2,1)S(1)}, bf16[64,2560]{1,0:T(8,128)(2,1)S(1)}, u32[]{:S(2)}, u32[]{:S(2)}) %collective-permute-start.66) | collective-permute-done | bytes 327712 | tf_op jit(solution)/shard_map/ppermute | solution.py:42
  347.0 5.4 collective-permute-done.64
  354.7 13.4 %collective-permute-done.46 = bf16[64,2560]{1,0:T(8,128)(2,1)S(1)} collective-permute-done((bf16[64,2560]{1,0:T(8,128)(2,1)S(1)}, bf16[64,2560]{1,0:T(8,128)(2,1)S(1)}, u32[]{:S(2)}, u32[]{:S(2)}) %collective-permute-start.46) | collective-permute-done | bytes 327712 | tf_op jit(solution)/shard_map/ppermute | solution.py:42
  368.6 3.4 collective-permute-start.68
  372.0 5.3 collective-permute-done.50
  377.6 3.4 collective-permute-start.51
  389.0 10.1 %collective-permute-done.51 = bf16[128,2560]{1,0:T(8,128)(2,1)S(1)} collective-permute-done((bf16[128,2560]{1,0:T(8,128)(2,1)S(1)}, bf16[128,2560]{1,0:T(8,128)(2,1)S(1)}, u32[]{:S(2)}, u32[]{:S(2)}) %collective-permute-start.51) | collective-permute-done | bytes 655392 | tf_op jit(solution)/shard_map/ppermute | solution.py:50
  406.7 8.9 %shard_map.305 = (f32[5,256,128]{2,1,0:T(8,128)S(1)}, bf16[8,3,512,128]{3,2,1,0:T(8,128)(2,1)S(1)}) custom-call(s32[2]{0:T(128)S(1)} %copy-done.73, bf16[5,256,128]{2,1,0:T(8,128)(2,1)S(1)} %bitcast.309, bf16[8,3,512,128]{3,2,1,0:T(8,128)(2,1)S(1)} %bitcast.293, f32[17,128,640]{2,1,0:T(8,128)} %copy-done.8, bf16[5,256,128]{2,1,0:T(8,128)(2,1)S(1)} %bitcast.331), custom_call_target="tpu_custom_call" | custom-call | tf_op jit(solution)/shard_map/pallas_call | solution.py:416
  417.0 4.0 collective-permute-done.94
  427.8 5.7 collective-permute-done.96.refs_3_
  434.0 4.9 all-to-all-start.5
  445.5 3.6 shard_map.310
  451.5 3.6 convolution_convert_fusion.4
  465.1 4.1 collective-permute-done.74
  473.4 7.3 %convolution_convert_fusion.3 = bf16[2560,512]{1,0:T(8,128)(2,1)} fusion(bf16[1024,2560]{1,0:T(8,128)(2,1)} %bitcast.302, bf16[1024,512]{0,1:T(8,128)(2,1)} %copy-done.110), kind=kOutput, calls=%fused_computation.15 | convolution fusion | flops 2685665280 | bytes 8912896 | tf_op jit(solution)/shard_map/dot_general | solution.py:36
  487.4 6.1 fusion.1
  496.4 3.5 copy-done.1
  504.2 4.8 collective-permute-done.76
  509.1 4.3 collective-permute-done.77
  513.7 17.4 %collective-permute-done.78 = bf16[512,128]{1,0:T(8,128)(2,1)S(1)} collective-permute-done((bf16[512,128]{1,0:T(8,128)(2,1)S(1)}, bf16[512,128]{1,0:T(8,128)(2,1)S(1)}, u32[]{:S(2)}, u32[]{:S(2)}) %collective-permute-start.78) | collective-permute-done | bytes 131104 | tf_op jit(solution)/shard_map/ppermute | solution.py:50
  532.4 4.1 all-to-all-start.3
  536.8 6.8 fusion.90
  546.2 4.0 fusion.7
  550.2 12.0 %collective-permute-done.93 = bf16[128,2560]{1,0:T(8,128)(2,1)} collective-permute-done((bf16[128,2560]{1,0:T(8,128)(2,1)S(1)}, bf16[128,2560]{1,0:T(8,128)(2,1)}, u32[]{:S(2)}, u32[]{:S(2)}) %collective-permute-start.93) | collective-permute-done | bytes 655392 | tf_op jit(solution)/shard_map/ppermute | solution.py:50
  565.7 9.8 %convolution_convert_fusion.1 = bf16[2560,1024]{1,0:T(8,128)(2,1)} fusion(bf16[1024,2560]{1,0:T(8,128)(2,1)} %bitcast.301, bf16[1024,512]{0,1:T(8,128)(2,1)} %copy-done.112, bf16[1024,512]{0,1:T(8,128)(2,1)} %copy-done.111), kind=kOutput, calls=%fused_computation.8 | convolution fusion | flops 5375524864 | bytes 12582912 | tf_op jit(solution)/shard_map/dot_general | solution.py:36
  575.5 4.6 all-to-all-start.6
  580.2 6.5 all-to-all-done.6.g_ref
  586.6 3.4 all-to-all-start.8
  591.1 7.1 %all-to-all-done.8 = bf16[8,40,512]{2,1,0:T(8,128)(2,1)S(1)} async-done(((bf16[8,40,512]{2,1,0:T(8,128)(2,1)}), bf16[8,40,512]{2,1,0:T(8,128)(2,1)S(1)}, u32[]{:S(2)}, u32[]{:S(2)}) %all-to-all-start.8) | async-done | bytes 327712 | tf_op jit(solution)/shard_map/all_to_all | solution.py:173
  598.2 10.0 %reduce-scatter.13.cloned.1.call-done = bf16[320,256]{1,0:T(8,128)(2,1)} async-done(((bf16[2560,256]{1,0:T(8,128)(2,1)}), bf16[320,256]{1,0:T(8,128)(2,1)}) %reduce-scatter.13.cloned.1.call-update) | async-done | bytes 163856 | tf_op jit(solution)/shard_map/reduce_scatter | solution.py:469
  608.2 4.2 all-to-all-start.4
  612.4 6.5 all-to-all-done.4.g_ref
  618.9 53.4 %reduce-scatter.9.cloned.1.call-done = bf16[320,1024]{1,0:T(8,128)(2,1)} async-done(((bf16[2560,1024]{1,0:T(8,128)(2,1)}), bf16[320,1024]{1,0:T(8,128)(2,1)}) %reduce-scatter.9.cloned.1.call-update) | async-done | bytes 655376 | tf_op jit(solution)/shard_map/reduce_scatter | solution.py:404
  672.3 4.3 all-to-all-start.7
  692.6 3.6 shard_map.312
  (561 shorter events, 225.0 us)
Async XLA Ops:
  7.2 74.7 %all-gather.3.cloned.1.call-start = ((), (), s32[]{:S(2)}) async-start(), calls=%async_computation.13 | async-start | bytes 1474560 | tf_op jit(solution)/shard_map/all_gather | solution.py:334
  21.4 245.1 %all-gather.5.cloned.1.call-start = ((), (), s32[]{:S(2)}) async-start(), calls=%async_computation.14 | async-start | bytes 8847360 | tf_op jit(solution)/shard_map/all_gather | solution.py:336
  44.6 17.7 %collective-permute-start = (bf16[128,2560]{1,0:T(8,128)(2,1)S(1)}, bf16[128,2560]{1,0:T(8,128)(2,1)S(1)}, u32[]{:S(2)}, u32[]{:S(2)}) collective-permute-start(bf16[128,2560]{1,0:T(8,128)(2,1)S(1)} %copy-done.4), channel_id=1, source_target_pairs={{0,4},{4,8},{8,12},{12,0},{1,5},{5,9},{9,13},{13,1},{2,6},{6,10},{... | collective-permute-start | bytes 1966088 | tf_op jit(solution)/shard_map/ppermute | solution.py:42
  45.3 17.2 %collective-permute-start.1 = (bf16[128,2560]{1,0:T(8,128)(2,1)S(1)}, bf16[128,2560]{1,0:T(8,128)(2,1)S(1)}, u32[]{:S(2)}, u32[]{:S(2)}) collective-permute-start(bf16[128,2560]{1,0:T(8,128)(2,1)S(1)} %copy-done.4), channel_id=1, source_target_pairs={{0,12},{4,0},{8,4},{12,8},{1,13},{5,1},{9,5},{13,9},{2,14},{6,2},{... | collective-permute-start | bytes 1966088 | tf_op jit(solution)/shard_map/ppermute | solution.py:42
  47.9 25.9 %collective-permute-start.4 = (bf16[128,2560]{1,0:T(8,128)(2,1)S(1)}, bf16[128,2560]{1,0:T(8,128)(2,1)S(1)}, u32[]{:S(2)}, u32[]{:S(2)}) collective-permute-start(bf16[128,2560]{1,0:T(8,128)(2,1)S(1)} %copy-done.4), channel_id=1, source_target_pairs={{0,2},{2,0},{1,3},{3,1},{4,6},{6,4},{5,7},{7,5},{8,10},{10,8},{9,1... | collective-permute-start | bytes 1966088 | tf_op jit(solution)/shard_map/ppermute | solution.py:50
  48.0 17.8 %collective-permute-start.20 = (bf16[40,1280]{1,0:T(8,128)(2,1)S(1)}, bf16[40,1280]{1,0:T(8,128)(2,1)S(1)}, u32[]{:S(2)}, u32[]{:S(2)}) collective-permute-start(bf16[40,1280]{1,0:T(8,128)(2,1)S(1)} %convert_element_type.335), channel_id=1, source_target_pairs={{0,64},{64,0},{1,65},{65,1},{2,66},{66,2},{3,67},{67,3},{4,68},{68... | collective-permute-start | bytes 307208 | tf_op jit(solution)/shard_map/ppermute | solution.py:50
  73.8 22.4 %collective-permute-start.21 = (bf16[2,40,1280]{2,1,0:T(8,128)(2,1)S(1)}, bf16[2,40,1280]{2,1,0:T(8,128)(2,1)S(1)}, u32[]{:S(2)}, u32[]{:S(2)}) collective-permute-start(bf16[2,40,1280]{2,1,0:T(8,128)(2,1)S(1)} %pad_maximum_fusion.10.refs_0_), channel_id=1, source_target_pairs={{0,16},{16,32},{32,48},{48,0},{1,17},{17,33},{33,49},{49,1},{2,18}... | collective-permute-start | bytes 614408 | tf_op jit(solution)/shard_map/ppermute | solution.py:42
  74.8 21.5 %collective-permute-start.22 = (bf16[2,40,1280]{2,1,0:T(8,128)(2,1)S(1)}, bf16[2,40,1280]{2,1,0:T(8,128)(2,1)S(1)}, u32[]{:S(2)}, u32[]{:S(2)}) collective-permute-start(bf16[2,40,1280]{2,1,0:T(8,128)(2,1)S(1)} %pad_maximum_fusion.10.refs_0_), channel_id=1, source_target_pairs={{0,48},{16,0},{32,16},{48,32},{1,49},{17,1},{33,17},{49,33},{2,50}... | collective-permute-start | bytes 614408 | tf_op jit(solution)/shard_map/ppermute | solution.py:42
  91.5 19.1 %all-to-all-start.1 = ((bf16[8,256,128]{2,1,0:T(8,128)(2,1)}), bf16[8,256,128]{2,1,0:T(8,128)(2,1)}, u32[]{:S(2)}, u32[]{:S(2)}) async-start(bf16[8,256,128]{2,1,0:T(8,128)(2,1)} %bitcast.288), calls=%async_computation.1 | async-start | bytes 1048576 | tf_op jit(solution)/shard_map/all_to_all | solution.py:173
  107.3 21.1 %collective-permute-start.25 = (bf16[8,40,1280]{2,1,0:T(8,128)(2,1)S(1)}, bf16[8,40,1280]{2,1,0:T(8,128)(2,1)S(1)}, u32[]{:S(2)}, u32[]{:S(2)}) collective-permute-start(bf16[8,40,1280]{2,1,0:T(8,128)(2,1)S(1)} %fusion.27.refs_0_), channel_id=1, source_target_pairs={{0,4},{4,8},{8,12},{12,0},{1,5},{5,9},{9,13},{13,1},{2,6},{6,10},{... | collective-permute-start | bytes 2457608 | tf_op jit(solution)/shard_map/ppermute | solution.py:42
  109.2 19.7 %collective-permute-start.26 = (bf16[8,40,1280]{2,1,0:T(8,128)(2,1)S(1)}, bf16[8,40,1280]{2,1,0:T(8,128)(2,1)S(1)}, u32[]{:S(2)}, u32[]{:S(2)}) collective-permute-start(bf16[8,40,1280]{2,1,0:T(8,128)(2,1)S(1)} %fusion.27.refs_0_), channel_id=1, source_target_pairs={{0,12},{4,0},{8,4},{12,8},{1,13},{5,1},{9,5},{13,9},{2,14},{6,2},{... | collective-permute-start | bytes 2457608 | tf_op jit(solution)/shard_map/ppermute | solution.py:42
  112.8 19.0 %collective-permute-start.10 = (bf16[512,128]{1,0:T(8,128)(2,1)S(1)}, bf16[512,128]{1,0:T(8,128)(2,1)S(1)}, u32[]{:S(2)}, u32[]{:S(2)}) collective-permute-start(bf16[512,128]{1,0:T(8,128)(2,1)S(1)} %bitcast.350), channel_id=1, source_target_pairs={{0,32},{16,48},{1,33},{17,49},{2,34},{18,50},{3,35},{19,51},{4,36}... | collective-permute-start | bytes 393224 | tf_op jit(solution)/shard_map/ppermute | solution.py:46
  121.2 32.5 %collective-permute-start.29 = (bf16[8,40,1280]{2,1,0:T(8,128)(2,1)S(1)}, bf16[8,40,1280]{2,1,0:T(8,128)(2,1)S(1)}, u32[]{:S(2)}, u32[]{:S(2)}) collective-permute-start(bf16[8,40,1280]{2,1,0:T(8,128)(2,1)S(1)} %fusion.27.refs_0_), channel_id=1, source_target_pairs={{0,2},{2,0},{1,3},{3,1},{4,6},{6,4},{5,7},{7,5},{8,10},{10,8},{9,1... | collective-permute-start | bytes 2457608 | tf_op jit(solution)/shard_map/ppermute | solution.py:50
  131.8 16.5 %collective-permute-start.11 = (bf16[1536,128]{1,0:T(8,128)(2,1)S(1)}, bf16[1536,128]{1,0:T(8,128)(2,1)S(1)}, u32[]{:S(2)}, u32[]{:S(2)}) collective-permute-start(bf16[1536,128]{1,0:T(8,128)(2,1)S(1)} %pad_maximum_fusion.7), channel_id=1, source_target_pairs={{0,4},{4,8},{8,12},{12,0},{1,5},{5,9},{9,13},{13,1},{2,6},{6,10},{... | collective-permute-start | bytes 1179656 | tf_op jit(solution)/shard_map/ppermute | solution.py:42
  131.9 26.0 %collective-permute-start.30 = (bf16[8,40,1280]{2,1,0:T(8,128)(2,1)S(1)}, bf16[8,40,1280]{2,1,0:T(8,128)(2,1)S(1)}, u32[]{:S(2)}, u32[]{:S(2)}) collective-permute-start(bf16[8,40,1280]{2,1,0:T(8,128)(2,1)S(1)} %collective-permute-done.25.refs_1_), channel_id=1, source_target_pairs={{0,2},{2,0},{1,3},{3,1},{4,6},{6,4},{5,7},{7,5},{8,10},{10,8},{9,1... | collective-permute-start | bytes 2457608 | tf_op jit(solution)/shard_map/ppermute | solution.py:50
  142.1 16.4 %collective-permute-start.31 = (bf16[8,40,1280]{2,1,0:T(8,128)(2,1)S(1)}, bf16[8,40,1280]{2,1,0:T(8,128)(2,1)S(1)}, u32[]{:S(2)}, u32[]{:S(2)}) collective-permute-start(bf16[8,40,1280]{2,1,0:T(8,128)(2,1)S(1)} %collective-permute-done.26.refs_2_), channel_id=1, source_target_pairs={{0,2},{2,0},{1,3},{3,1},{4,6},{6,4},{5,7},{7,5},{8,10},{10,8},{9,1... | collective-permute-start | bytes 2457608 | tf_op jit(solution)/shard_map/ppermute | solution.py:50
  176.0 19.2 %collective-permute-start.34 = (bf16[128,2560]{1,0:T(8,128)(2,1)S(1)}, bf16[128,2560]{1,0:T(8,128)(2,1)S(1)}, u32[]{:S(2)}, u32[]{:S(2)}) collective-permute-start(bf16[128,2560]{1,0:T(8,128)(2,1)S(1)} %convolution_convert_fusion.5), channel_id=1, source_target_pairs={{0,1},{1,0},{2,3},{3,2},{4,5},{5,4},{6,7},{7,6},{8,9},{9,8},{10,11... | collective-permute-start | bytes 1966088 | tf_op jit(solution)/shard_map/ppermute | solution.py:50
  180.0 17.9 %collective-permute-start.52 = (bf16[128,2560]{1,0:T(8,128)(2,1)S(1)}, bf16[128,2560]{1,0:T(8,128)(2,1)S(1)}, u32[]{:S(2)}, u32[]{:S(2)}) collective-permute-start(bf16[128,2560]{1,0:T(8,128)(2,1)S(1)} %copy-done.18), channel_id=1, source_target_pairs={{0,4},{4,8},{8,12},{12,0},{1,5},{5,9},{9,13},{13,1},{2,6},{6,10},{... | collective-permute-start | bytes 1966088 | tf_op jit(solution)/shard_map/ppermute | solution.py:42
  180.0 21.2 %collective-permute-start.53 = (bf16[128,2560]{1,0:T(8,128)(2,1)S(1)}, bf16[128,2560]{1,0:T(8,128)(2,1)S(1)}, u32[]{:S(2)}, u32[]{:S(2)}) collective-permute-start(bf16[128,2560]{1,0:T(8,128)(2,1)S(1)} %copy-done.18), channel_id=1, source_target_pairs={{0,12},{4,0},{8,4},{12,8},{1,13},{5,1},{9,5},{13,9},{2,14},{6,2},{... | collective-permute-start | bytes 1966088 | tf_op jit(solution)/shard_map/ppermute | solution.py:42
  197.8 25.4 %collective-permute-start.35 = (bf16[128,2560]{1,0:T(8,128)(2,1)}, bf16[128,2560]{1,0:T(8,128)(2,1)}, u32[]{:S(2)}, u32[]{:S(2)}) collective-permute-start(bf16[128,2560]{1,0:T(8,128)(2,1)} %multiply_convert_fusion.2), channel_id=1, source_target_pairs={{0,4},{4,8},{8,12},{12,0},{1,5},{5,9},{9,13},{13,1},{2,6},{6,10},{... | collective-permute-start | bytes 1966088 | tf_op jit(solution)/shard_map/ppermute | solution.py:42
  197.9 25.4 %collective-permute-start.36 = (bf16[128,2560]{1,0:T(8,128)(2,1)}, bf16[128,2560]{1,0:T(8,128)(2,1)}, u32[]{:S(2)}, u32[]{:S(2)}) collective-permute-start(bf16[128,2560]{1,0:T(8,128)(2,1)} %multiply_convert_fusion.2), channel_id=1, source_target_pairs={{0,12},{4,0},{8,4},{12,8},{1,13},{5,1},{9,5},{13,9},{2,14},{6,2},{... | collective-permute-start | bytes 1966088 | tf_op jit(solution)/shard_map/ppermute | solution.py:42
  201.2 21.5 %collective-permute-start.54 = (bf16[64,2560]{1,0:T(8,128)(2,1)S(1)}, bf16[64,2560]{1,0:T(8,128)(2,1)S(1)}, u32[]{:S(2)}, u32[]{:S(2)}) collective-permute-start(bf16[64,2560]{1,0:T(8,128)(2,1)S(1)} %slice.391), channel_id=1, source_target_pairs={{0,4},{4,8},{8,12},{12,0},{1,5},{5,9},{9,13},{13,1},{2,6},{6,10},{... | collective-permute-start | bytes 983048 | tf_op jit(solution)/shard_map/ppermute | solution.py:42
  201.2 21.5 %collective-permute-start.55 = (bf16[64,2560]{1,0:T(8,128)(2,1)S(1)}, bf16[64,2560]{1,0:T(8,128)(2,1)S(1)}, u32[]{:S(2)}, u32[]{:S(2)}) collective-permute-start(bf16[64,2560]{1,0:T(8,128)(2,1)S(1)} %slice.392), channel_id=1, source_target_pairs={{0,12},{4,0},{8,4},{12,8},{1,13},{5,1},{9,5},{13,9},{2,14},{6,2},{... | collective-permute-start | bytes 983048 | tf_op jit(solution)/shard_map/ppermute | solution.py:42
  204.5 21.2 %collective-permute-start.56 = (bf16[128,2560]{1,0:T(8,128)(2,1)S(1)}, bf16[128,2560]{1,0:T(8,128)(2,1)S(1)}, u32[]{:S(2)}, u32[]{:S(2)}) collective-permute-start(bf16[128,2560]{1,0:T(8,128)(2,1)S(1)} %copy-done.18), channel_id=1, source_target_pairs={{0,2},{2,0},{1,3},{3,1},{4,6},{6,4},{5,7},{7,5},{8,10},{10,8},{9,1... | collective-permute-start | bytes 1966088 | tf_op jit(solution)/shard_map/ppermute | solution.py:50
  226.6 32.7 %collective-permute-start.39 = (bf16[128,2560]{1,0:T(8,128)(2,1)}, bf16[128,2560]{1,0:T(8,128)(2,1)}, u32[]{:S(2)}, u32[]{:S(2)}) collective-permute-start(bf16[128,2560]{1,0:T(8,128)(2,1)} %multiply_convert_fusion.2), channel_id=1, source_target_pairs={{0,2},{2,0},{1,3},{3,1},{4,6},{6,4},{5,7},{7,5},{8,10},{10,8},{9,1... | collective-permute-start | bytes 1966088 | tf_op jit(solution)/shard_map/ppermute | solution.py:50
  232.3 27.7 %collective-permute-start.40 = (bf16[128,2560]{1,0:T(8,128)(2,1)}, bf16[128,2560]{1,0:T(8,128)(2,1)}, u32[]{:S(2)}, u32[]{:S(2)}) collective-permute-start(bf16[128,2560]{1,0:T(8,128)(2,1)} %collective-permute-done.35), channel_id=1, source_target_pairs={{0,2},{2,0},{1,3},{3,1},{4,6},{6,4},{5,7},{7,5},{8,10},{10,8},{9,1... | collective-permute-start | bytes 1966088 | tf_op jit(solution)/shard_map/ppermute | solution.py:50
  233.1 26.8 %collective-permute-start.41 = (bf16[128,2560]{1,0:T(8,128)(2,1)}, bf16[128,2560]{1,0:T(8,128)(2,1)}, u32[]{:S(2)}, u32[]{:S(2)}) collective-permute-start(bf16[128,2560]{1,0:T(8,128)(2,1)} %collective-permute-done.36), channel_id=1, source_target_pairs={{0,2},{2,0},{1,3},{3,1},{4,6},{6,4},{5,7},{7,5},{8,10},{10,8},{9,1... | collective-permute-start | bytes 1966088 | tf_op jit(solution)/shard_map/ppermute | solution.py:50
  238.8 21.2 %collective-permute-start.42 = (bf16[64,2560]{1,0:T(8,128)(2,1)}, bf16[64,2560]{1,0:T(8,128)(2,1)}, u32[]{:S(2)}, u32[]{:S(2)}) collective-permute-start(bf16[64,2560]{1,0:T(8,128)(2,1)} %collective-permute-done.37.refs_3_), channel_id=1, source_target_pairs={{0,2},{2,0},{1,3},{3,1},{4,6},{6,4},{5,7},{7,5},{8,10},{10,8},{9,1... | collective-permute-start | bytes 983048 | tf_op jit(solution)/shard_map/ppermute | solution.py:50
  238.8 21.2 %collective-permute-start.43 = (bf16[64,2560]{1,0:T(8,128)(2,1)}, bf16[64,2560]{1,0:T(8,128)(2,1)}, u32[]{:S(2)}, u32[]{:S(2)}) collective-permute-start(bf16[64,2560]{1,0:T(8,128)(2,1)} %collective-permute-done.38.refs_4_), channel_id=1, source_target_pairs={{0,2},{2,0},{1,3},{3,1},{4,6},{6,4},{5,7},{7,5},{8,10},{10,8},{9,1... | collective-permute-start | bytes 983048 | tf_op jit(solution)/shard_map/ppermute | solution.py:50
  259.3 27.4 %collective-permute-start.79 = (bf16[40,1792]{1,0:T(8,128)(2,1)}, bf16[40,1792]{1,0:T(8,128)(2,1)}, u32[]{:S(2)}, u32[]{:S(2)}) collective-permute-start(bf16[40,1792]{1,0:T(8,128)(2,1)} %pad_maximum_fusion.11), channel_id=1, source_target_pairs={{0,64},{64,0},{1,65},{65,1},{2,66},{66,2},{3,67},{67,3},{4,68},{68... | collective-permute-start | bytes 430088 | tf_op jit(solution)/shard_map/ppermute | solution.py:50
  286.7 27.3 %collective-permute-start.44 = (bf16[4,128,2560]{2,1,0:T(8,128)(2,1)}, bf16[4,128,2560]{2,1,0:T(8,128)(2,1)}, u32[]{:S(2)}, u32[]{:S(2)}) collective-permute-start(bf16[4,128,2560]{2,1,0:T(8,128)(2,1)} %dynamic-slice_bitcast_fusion.1), channel_id=1, source_target_pairs={{0,2},{2,0},{1,3},{3,1},{4,6},{6,4},{5,7},{7,5},{8,10},{10,8},{9,1... | collective-permute-start | bytes 7864328 | tf_op jit(solution)/shard_map/ppermute | solution.py:50
  300.2 21.1 %collective-permute-start.61 = (bf16[4,128,2560]{2,1,0:T(8,128)(2,1)}, bf16[4,128,2560]{2,1,0:T(8,128)(2,1)}, u32[]{:S(2)}, u32[]{:S(2)}) collective-permute-start(bf16[4,128,2560]{2,1,0:T(8,128)(2,1)} %dynamic-slice_bitcast_fusion), channel_id=1, source_target_pairs={{0,2},{2,0},{1,3},{3,1},{4,6},{6,4},{5,7},{7,5},{8,10},{10,8},{9,1... | collective-permute-start | bytes 7864328 | tf_op jit(solution)/shard_map/ppermute | solution.py:50
  317.6 17.7 %collective-permute-start.45 = (bf16[64,2560]{1,0:T(8,128)(2,1)S(1)}, bf16[64,2560]{1,0:T(8,128)(2,1)S(1)}, u32[]{:S(2)}, u32[]{:S(2)}) collective-permute-start(bf16[64,2560]{1,0:T(8,128)(2,1)S(1)} %get-tuple-element.108), channel_id=1, source_target_pairs={{0,12},{4,0},{8,4},{12,8},{1,13},{5,1},{9,5},{13,9},{2,14},{6,2},{... | collective-permute-start | bytes 983048 | tf_op jit(solution)/shard_map/ppermute | solution.py:42
  321.1 31.5 %collective-permute-start.49 = (bf16[64,2560]{1,0:T(8,128)(2,1)S(1)}, bf16[64,2560]{1,0:T(8,128)(2,1)S(1)}, u32[]{:S(2)}, u32[]{:S(2)}) collective-permute-start(bf16[64,2560]{1,0:T(8,128)(2,1)S(1)} %get-tuple-element.109), channel_id=1, source_target_pairs={{0,4},{4,8},{8,12},{12,0},{1,5},{5,9},{9,13},{13,1},{2,6},{6,10},{... | collective-permute-start | bytes 983048 | tf_op jit(solution)/shard_map/ppermute | solution.py:42
  321.2 33.5 %collective-permute-start.47 = (bf16[64,2560]{1,0:T(8,128)(2,1)S(1)}, bf16[64,2560]{1,0:T(8,128)(2,1)S(1)}, u32[]{:S(2)}, u32[]{:S(2)}) collective-permute-start(bf16[64,2560]{1,0:T(8,128)(2,1)S(1)} %get-tuple-element.93), channel_id=1, source_target_pairs={{0,4},{4,8},{8,12},{12,0},{1,5},{5,9},{9,13},{13,1},{2,6},{6,10},{... | collective-permute-start | bytes 983048 | tf_op jit(solution)/shard_map/ppermute | solution.py:42
  327.2 19.8 %collective-permute-start.66 = (bf16[64,2560]{1,0:T(8,128)(2,1)S(1)}, bf16[64,2560]{1,0:T(8,128)(2,1)S(1)}, u32[]{:S(2)}, u32[]{:S(2)}) collective-permute-start(bf16[64,2560]{1,0:T(8,128)(2,1)S(1)} %get-tuple-element.107), channel_id=1, source_target_pairs={{0,4},{4,8},{8,12},{12,0},{1,5},{5,9},{9,13},{13,1},{2,6},{6,10},{... | collective-permute-start | bytes 983048 | tf_op jit(solution)/shard_map/ppermute | solution.py:42
  334.9 17.5 %collective-permute-start.64 = (bf16[64,2560]{1,0:T(8,128)(2,1)S(1)}, bf16[64,2560]{1,0:T(8,128)(2,1)S(1)}, u32[]{:S(2)}, u32[]{:S(2)}) collective-permute-start(bf16[64,2560]{1,0:T(8,128)(2,1)S(1)} %get-tuple-element.89), channel_id=1, source_target_pairs={{0,4},{4,8},{8,12},{12,0},{1,5},{5,9},{9,13},{13,1},{2,6},{6,10},{... | collective-permute-start | bytes 983048 | tf_op jit(solution)/shard_map/ppermute | solution.py:42
  335.4 17.0 %collective-permute-start.63 = (bf16[64,2560]{1,0:T(8,128)(2,1)S(1)}, bf16[64,2560]{1,0:T(8,128)(2,1)S(1)}, u32[]{:S(2)}, u32[]{:S(2)}) collective-permute-start(bf16[64,2560]{1,0:T(8,128)(2,1)S(1)} %fusion.34), channel_id=1, source_target_pairs={{0,12},{4,0},{8,4},{12,8},{1,13},{5,1},{9,5},{13,9},{2,14},{6,2},{... | collective-permute-start | bytes 983048 | tf_op jit(solution)/shard_map/ppermute | solution.py:42
  347.0 25.0 %collective-permute-start.48 = (bf16[64,2560]{1,0:T(8,128)(2,1)S(1)}, bf16[64,2560]{1,0:T(8,128)(2,1)S(1)}, u32[]{:S(2)}, u32[]{:S(2)}) collective-permute-start(bf16[64,2560]{1,0:T(8,128)(2,1)S(1)} %get-tuple-element.94), channel_id=1, source_target_pairs={{0,12},{4,0},{8,4},{12,8},{1,13},{5,1},{9,5},{13,9},{2,14},{6,2},{... | collective-permute-start | bytes 983048 | tf_op jit(solution)/shard_map/ppermute | solution.py:42
  352.4 16.0 %collective-permute-start.65 = (bf16[64,2560]{1,0:T(8,128)(2,1)S(1)}, bf16[64,2560]{1,0:T(8,128)(2,1)S(1)}, u32[]{:S(2)}, u32[]{:S(2)}) collective-permute-start(bf16[64,2560]{1,0:T(8,128)(2,1)S(1)} %get-tuple-element.90), channel_id=1, source_target_pairs={{0,12},{4,0},{8,4},{12,8},{1,13},{5,1},{9,5},{13,9},{2,14},{6,2},{... | collective-permute-start | bytes 983048 | tf_op jit(solution)/shard_map/ppermute | solution.py:42
  352.6 15.8 %collective-permute-start.67 = (bf16[64,2560]{1,0:T(8,128)(2,1)S(1)}, bf16[64,2560]{1,0:T(8,128)(2,1)S(1)}, u32[]{:S(2)}, u32[]{:S(2)}) collective-permute-start(bf16[64,2560]{1,0:T(8,128)(2,1)S(1)} %get-tuple-element.88), channel_id=1, source_target_pairs={{0,4},{4,8},{8,12},{12,0},{1,5},{5,9},{9,13},{13,1},{2,6},{6,10},{... | collective-permute-start | bytes 983048 | tf_op jit(solution)/shard_map/ppermute | solution.py:42
  368.6 19.3 %collective-permute-start.68 = (bf16[128,2560]{1,0:T(8,128)(2,1)S(1)}, bf16[128,2560]{1,0:T(8,128)(2,1)S(1)}, u32[]{:S(2)}, u32[]{:S(2)}) collective-permute-start(bf16[128,2560]{1,0:T(8,128)(2,1)S(1)} %pad_maximum_fusion.5), channel_id=1, source_target_pairs={{0,1},{1,0},{2,3},{3,2},{4,5},{5,4},{6,7},{7,6},{8,9},{9,8},{10,11... | collective-permute-start | bytes 1966088 | tf_op jit(solution)/shard_map/ppermute | solution.py:50
  377.6 21.6 %collective-permute-start.51 = (bf16[128,2560]{1,0:T(8,128)(2,1)S(1)}, bf16[128,2560]{1,0:T(8,128)(2,1)S(1)}, u32[]{:S(2)}, u32[]{:S(2)}) collective-permute-start(bf16[128,2560]{1,0:T(8,128)(2,1)S(1)} %pad_maximum_fusion.4), channel_id=1, source_target_pairs={{0,1},{1,0},{2,3},{3,2},{4,5},{5,4},{6,7},{7,6},{8,9},{9,8},{10,11... | collective-permute-start | bytes 1966088 | tf_op jit(solution)/shard_map/ppermute | solution.py:50
  381.4 41.7 %collective-permute-start.84 = (bf16[8,40,1792]{2,1,0:T(8,128)(2,1)S(1)}, bf16[8,40,1792]{2,1,0:T(8,128)(2,1)S(1)}, u32[]{:S(2)}, u32[]{:S(2)}) collective-permute-start(bf16[8,40,1792]{2,1,0:T(8,128)(2,1)S(1)} %fusion.26.refs_0_), channel_id=1, source_target_pairs={{0,4},{4,8},{8,12},{12,0},{1,5},{5,9},{9,13},{13,1},{2,6},{6,10},{... | collective-permute-start | bytes 3440648 | tf_op jit(solution)/shard_map/ppermute | solution.py:42
  381.5 44.9 %collective-permute-start.85 = (bf16[8,40,1792]{2,1,0:T(8,128)(2,1)S(1)}, bf16[8,40,1792]{2,1,0:T(8,128)(2,1)S(1)}, u32[]{:S(2)}, u32[]{:S(2)}) collective-permute-start(bf16[8,40,1792]{2,1,0:T(8,128)(2,1)S(1)} %fusion.26.refs_0_), channel_id=1, source_target_pairs={{0,12},{4,0},{8,4},{12,8},{1,13},{5,1},{9,5},{13,9},{2,14},{6,2},{... | collective-permute-start | bytes 3440648 | tf_op jit(solution)/shard_map/ppermute | solution.py:42
  401.2 19.8 %collective-permute-start.94 = (bf16[128,2560]{1,0:T(8,128)(2,1)S(1)}, bf16[128,2560]{1,0:T(8,128)(2,1)}, u32[]{:S(2)}, u32[]{:S(2)}) collective-permute-start(bf16[128,2560]{1,0:T(8,128)(2,1)S(1)} %get-tuple-element.79), channel_id=1, source_target_pairs={{0,4},{4,8},{8,12},{12,0},{1,5},{5,9},{9,13},{13,1},{2,6},{6,10},{... | collective-permute-start | bytes 1966088 | tf_op jit(solution)/shard_map/ppermute | solution.py:42
  401.6 20.4 %collective-permute-start.95 = (bf16[128,2560]{1,0:T(8,128)(2,1)S(1)}, bf16[128,2560]{1,0:T(8,128)(2,1)}, u32[]{:S(2)}, u32[]{:S(2)}) collective-permute-start(bf16[128,2560]{1,0:T(8,128)(2,1)S(1)} %get-tuple-element.79), channel_id=1, source_target_pairs={{0,12},{4,0},{8,4},{12,8},{1,13},{5,1},{9,5},{13,9},{2,14},{6,2},{... | collective-permute-start | bytes 1966088 | tf_op jit(solution)/shard_map/ppermute | solution.py:42
  404.5 21.9 %collective-permute-start.98 = (bf16[128,2560]{1,0:T(8,128)(2,1)S(1)}, bf16[128,2560]{1,0:T(8,128)(2,1)S(1)}, u32[]{:S(2)}, u32[]{:S(2)}) collective-permute-start(bf16[128,2560]{1,0:T(8,128)(2,1)S(1)} %get-tuple-element.79), channel_id=1, source_target_pairs={{0,2},{2,0},{1,3},{3,1},{4,6},{6,4},{5,7},{7,5},{8,10},{10,8},{9,1... | collective-permute-start | bytes 1966088 | tf_op jit(solution)/shard_map/ppermute | solution.py:50
  421.0 35.6 %collective-permute-start.69 = (bf16[4,1536,128]{2,1,0:T(8,128)(2,1)}, bf16[4,1536,128]{2,1,0:T(8,128)(2,1)}, u32[]{:S(2)}, u32[]{:S(2)}) collective-permute-start(bf16[4,1536,128]{2,1,0:T(8,128)(2,1)} %dynamic-slice_bitcast_fusion.2), channel_id=1, source_target_pairs={{0,2},{2,0},{1,3},{3,1},{4,6},{6,4},{5,7},{7,5},{8,10},{10,8},{9,1... | collective-permute-start | bytes 4718600 | tf_op jit(solution)/shard_map/ppermute | solution.py:50
  426.4 19.1 %collective-permute-start.99 = (bf16[128,2560]{1,0:T(8,128)(2,1)}, bf16[128,2560]{1,0:T(8,128)(2,1)S(1)}, u32[]{:S(2)}, u32[]{:S(2)}) collective-permute-start(bf16[128,2560]{1,0:T(8,128)(2,1)} %collective-permute-done.94), channel_id=1, source_target_pairs={{0,2},{2,0},{1,3},{3,1},{4,6},{6,4},{5,7},{7,5},{8,10},{10,8},{9,1... | collective-permute-start | bytes 1966088 | tf_op jit(solution)/shard_map/ppermute | solution.py:50
  427.4 18.1 %collective-permute-start.100 = (bf16[128,2560]{1,0:T(8,128)(2,1)}, bf16[128,2560]{1,0:T(8,128)(2,1)}, u32[]{:S(2)}, u32[]{:S(2)}) collective-permute-start(bf16[128,2560]{1,0:T(8,128)(2,1)} %collective-permute-done.95), channel_id=1, source_target_pairs={{0,2},{2,0},{1,3},{3,1},{4,6},{6,4},{5,7},{7,5},{8,10},{10,8},{9,1... | collective-permute-start | bytes 1966088 | tf_op jit(solution)/shard_map/ppermute | solution.py:50
  434.0 17.4 %all-to-all-start.5 = ((bf16[8,160,128]{2,1,0:T(8,128)(2,1)}), bf16[8,160,128]{2,1,0:T(8,128)(2,1)}, u32[]{:S(2)}, u32[]{:S(2)}) async-start(bf16[8,160,128]{2,1,0:T(8,128)(2,1)} %bitcast.123), calls=%async_computation.5 | async-start | bytes 655360 | tf_op jit(solution)/shard_map/all_to_all | solution.py:173
  439.0 136.5 %reduce-scatter.15.cloned.1.call-start = ((), (), s32[]{:S(2)}) async-start(), calls=%async_computation.18 | async-start | bytes 1474560 | tf_op jit(solution)/shard_map/reduce_scatter | solution.py:474
  441.8 29.6 %collective-permute-start.86 = (bf16[4,40,1792]{2,1,0:T(8,128)(2,1)}, bf16[4,40,1792]{2,1,0:T(8,128)(2,1)}, u32[]{:S(2)}, u32[]{:S(2)}) collective-permute-start(bf16[4,40,1792]{2,1,0:T(8,128)(2,1)} %slice.406), channel_id=1, source_target_pairs={{0,4},{4,8},{8,12},{12,0},{1,5},{5,9},{9,13},{13,1},{2,6},{6,10},{... | collective-permute-start | bytes 1720328 | tf_op jit(solution)/shard_map/ppermute | solution.py:42
  443.8 28.5 %collective-permute-start.87 = (bf16[4,40,1792]{2,1,0:T(8,128)(2,1)}, bf16[4,40,1792]{2,1,0:T(8,128)(2,1)}, u32[]{:S(2)}, u32[]{:S(2)}) collective-permute-start(bf16[4,40,1792]{2,1,0:T(8,128)(2,1)} %slice.407), channel_id=1, source_target_pairs={{0,12},{4,0},{8,4},{12,8},{1,13},{5,1},{9,5},{13,9},{2,14},{6,2},{... | collective-permute-start | bytes 1720328 | tf_op jit(solution)/shard_map/ppermute | solution.py:42
  456.6 123.6 %reduce-scatter.11.cloned.1.call-start = ((), (), s32[]{:S(2)}) async-start(), calls=%async_computation.16 | async-start | bytes 2949120 | tf_op jit(solution)/shard_map/reduce_scatter | solution.py:403
  462.7 21.4 %collective-permute-start.88 = (bf16[8,40,1792]{2,1,0:T(8,128)(2,1)S(1)}, bf16[8,40,1792]{2,1,0:T(8,128)(2,1)}, u32[]{:S(2)}, u32[]{:S(2)}) collective-permute-start(bf16[8,40,1792]{2,1,0:T(8,128)(2,1)S(1)} %copy-done.13), channel_id=1, source_target_pairs={{0,2},{2,0},{1,3},{3,1},{4,6},{6,4},{5,7},{7,5},{8,10},{10,8},{9,1... | collective-permute-start | bytes 3440648 | tf_op jit(solution)/shard_map/ppermute | solution.py:50
  462.8 23.0 %collective-permute-start.89 = (bf16[8,40,1792]{2,1,0:T(8,128)(2,1)S(1)}, bf16[8,40,1792]{2,1,0:T(8,128)(2,1)}, u32[]{:S(2)}, u32[]{:S(2)}) collective-permute-start(bf16[8,40,1792]{2,1,0:T(8,128)(2,1)S(1)} %copy-done.24), channel_id=1, source_target_pairs={{0,2},{2,0},{1,3},{3,1},{4,6},{6,4},{5,7},{7,5},{8,10},{10,8},{9,1... | collective-permute-start | bytes 3440648 | tf_op jit(solution)/shard_map/ppermute | solution.py:50
  484.1 15.8 %collective-permute-start.72 = (bf16[768,128]{1,0:T(8,128)(2,1)}, bf16[768,128]{1,0:T(8,128)(2,1)S(1)}, u32[]{:S(2)}, u32[]{:S(2)}) collective-permute-start(bf16[768,128]{1,0:T(8,128)(2,1)} %get-tuple-element.99), channel_id=1, source_target_pairs={{0,4},{4,8},{8,12},{12,0},{1,5},{5,9},{9,13},{13,1},{2,6},{6,10},{... | collective-permute-start | bytes 589832 | tf_op jit(solution)/shard_map/ppermute | solution.py:42
  513.5 17.7 %collective-permute-start.78 = (bf16[512,128]{1,0:T(8,128)(2,1)S(1)}, bf16[512,128]{1,0:T(8,128)(2,1)S(1)}, u32[]{:S(2)}, u32[]{:S(2)}) collective-permute-start(bf16[512,128]{1,0:T(8,128)(2,1)S(1)} %fusion.69), channel_id=1, source_target_pairs={{0,1},{1,0},{2,3},{3,2},{4,5},{5,4},{6,7},{7,6},{8,9},{9,8},{10,11... | collective-permute-start | bytes 393224 | tf_op jit(solution)/shard_map/ppermute | solution.py:50
  536.5 71.6 %reduce-scatter.13.cloned.1.call-start = ((), (), s32[]{:S(2)}) async-start(), calls=%async_computation.17 | async-start | bytes 1474560 | tf_op jit(solution)/shard_map/reduce_scatter | solution.py:469
  543.6 18.6 %collective-permute-start.93 = (bf16[128,2560]{1,0:T(8,128)(2,1)S(1)}, bf16[128,2560]{1,0:T(8,128)(2,1)}, u32[]{:S(2)}, u32[]{:S(2)}) collective-permute-start(bf16[128,2560]{1,0:T(8,128)(2,1)S(1)} %get-tuple-element.127), channel_id=1, source_target_pairs={{0,1},{1,0},{2,3},{3,2},{4,5},{5,4},{6,7},{7,6},{8,9},{9,8},{10,11... | collective-permute-start | bytes 1966088 | tf_op jit(solution)/shard_map/ppermute | solution.py:50
  565.7 106.7 %reduce-scatter.9.cloned.1.call-start = ((), (), s32[]{:S(2)}) async-start(), calls=%async_computation.15 | async-start | bytes 5898240 | tf_op jit(solution)/shard_map/reduce_scatter | solution.py:404
  672.3 16.1 %all-to-all-start.7 = ((bf16[8,40,1024]{2,1,0:T(8,128)(2,1)}), bf16[8,40,1024]{2,1,0:T(8,128)(2,1)}, u32[]{:S(2)}, u32[]{:S(2)}) async-start(bf16[8,40,1024]{2,1,0:T(8,128)(2,1)} %bitcast.346), calls=%async_computation.8 | async-start | bytes 1310720 | tf_op jit(solution)/shard_map/all_to_all | solution.py:173
  (170 other events, 1690.5 us)
Sparse Core Ops, SparseCore 0:
  21.5 40.2 all-gather.2
  63.4 93.6 all-gather.4
  456.7 39.1 reduce-scatter.14
  498.1 43.8 reduce-scatter.10
  565.8 42.3 reduce-scatter.12
  610.5 61.8 reduce-scatter.8

commit v2 on v1

v2 whole, which is shorter than its diff:
```python
import math

import jax
import jax.numpy as jnp
from jax import lax
from jax.experimental import pallas as pl
from jax.experimental.pallas import tpu as pltpu
from jax.sharding import Mesh
from jax.sharding import PartitionSpec as P

D = 2560
HEADS = 10
HEAD_DIM = 256
STEP = 10
ROWS = 128
GROUP = 8
OWNED = 40
Q_PART = 160
KV_PART = 64
F_PART = 480
F_PAD = 512
LOCAL_HEADS = 5
TILES = 17
BF = jnp.bfloat16
F32 = jnp.float32
ANY = pl.BlockSpec(memory_space=pl.ANY)
SMEM = pl.BlockSpec(memory_space=pltpu.SMEM)
VMEM = pl.BlockSpec(memory_space=pltpu.VMEM)


SMALL = pl.CostEstimate(flops=1, transcendentals=0, bytes_accessed=1)


def params(mib):
    return pltpu.CompilerParams(vmem_limit_bytes=mib * 1024 * 1024)


def dot(left, right, left_dim, right_dim):
    return lax.dot_general(
        left, right, (((left_dim,), (right_dim,)), ((), ())), preferred_element_type=F32
    )


def shift(value, axis, step):
    return lax.ppermute(value, axis, [(i, (i + step) % 4) for i in range(4)])


def push(value, axis, step):
    return lax.ppermute(value, axis, [(i, i + step) for i in range(4) if 0 <= i + step < 4])


def swap(value, axis):
    return lax.ppermute(value, axis, [(0, 1), (1, 0)])


STEPS = (0, 1, 3, 2)
Y_AT, X_AT, B_AT, C_AT = 0, 4, 8, 10


def tie(value, *others):
    def body(*refs):
        del refs

    return pl.pallas_call(
        body,
        out_shape=jax.ShapeDtypeStruct(value.shape, value.dtype),
        in_specs=[ANY] * (1 + len(others)),
        out_specs=ANY,
        input_output_aliases={0: 0},
        cost_estimate=SMALL,
    )(value, *others)


def place(pieces, index, shape, target):
    count = len(pieces)

    def body(index_ref, *refs):
        out, sems = refs[count], refs[count + 1]
        copies = [
            pltpu.make_async_copy(refs[k], target(out, index_ref, k), sems.at[k])
            for k in range(count)
        ]
        for copy in copies:
            copy.start()
        for copy in copies:
            copy.wait()

    return pl.pallas_call(
        body,
        out_shape=jax.ShapeDtypeStruct(shape, pieces[0].dtype),
        in_specs=[SMEM] + [VMEM] * count,
        out_specs=ANY,
        scratch_shapes=[pltpu.SemaphoreType.DMA((count,))],
        cost_estimate=SMALL,
        compiler_params=params(24),
    )(index, *pieces)


def direct(value, axis):
    return [value] + [shift(value, axis, step) for step in STEPS[1:]]


def group_place(mine, index):
    pieces = mine + [swap(piece, "c") for piece in mine]

    def target(out, index_ref, k):
        return out.at[2 * index_ref[X_AT + k % 4] + index_ref[C_AT + k // 4]]

    return place(pieces, index, (GROUP,) + mine[0].shape, target)


def group_gather(value, index):
    return group_place(direct(value, "x"), index)


def two_step_gather(value, index):
    half = value.shape[0] // 2
    left, right = shift(value, "x", 1), shift(value, "x", 3)
    top, bottom = shift(left[:half], "x", 1), shift(right[half:], "x", 3)
    mine = [value, left, right, top, bottom]
    pieces = mine + [swap(piece, "c") for piece in mine]
    pieces = [
        piece if k % 5 > 2 else piece.reshape((2, half) + value.shape[1:])
        for k, piece in enumerate(pieces)
    ]

    def target(out, index_ref, k):
        spot = 2 * index_ref[X_AT + min(k % 5, 3)] + index_ref[C_AT + k // 5]
        return out.at[spot] if k % 5 < 3 else out.at[spot, k % 5 - 3]

    out = place(pieces, index, (GROUP, 2, half) + value.shape[1:], target)
    return out.reshape((GROUP,) + value.shape), (left, right)


def place_rows(mine, index):
    pieces = mine + [swap(piece, "c") for piece in mine]

    def target(out, index_ref, k):
        spot = 2 * index_ref[X_AT + min(k % 5, 3)] + index_ref[C_AT + k // 5]
        if k % 5 < 3:
            return out.at[:, spot]
        return out.at[pl.ds((k % 5 - 3) * 4, 4), spot]

    width = mine[0].shape[2]
    return place(pieces, index, (8, GROUP, OWNED, width), target).reshape(D, width)


def pair_gather(mine, theirs, pair_axis, ring_axis, index, after=()):
    pieces = direct(jnp.stack([mine, theirs]), ring_axis)
    ring_at, pair_at = (X_AT, C_AT) if ring_axis == "x" else (Y_AT, B_AT)

    def body(index_ref, *refs):
        out, sems = refs[-2:]
        copies = []
        for k in range(4):
            for h in range(2):
                spot, side = index_ref[ring_at + k], index_ref[pair_at + h]
                to = out.at[spot, side] if ring_axis == "x" else out.at[side, spot]
                copies.append(pltpu.make_async_copy(refs[k].at[h], to, sems.at[2 * k + h]))
        for copy in copies:
            copy.start()
        for copy in copies:
            copy.wait()

    shape = ((4, 2) if ring_axis == "x" else (2, 4)) + mine.shape
    return pl.pallas_call(
        body,
        out_shape=jax.ShapeDtypeStruct(shape, mine.dtype),
        in_specs=[SMEM] + [VMEM] * 4 + [ANY] * len(after),
        out_specs=ANY,
        scratch_shapes=[pltpu.SemaphoreType.DMA((8,))],
        cost_estimate=SMALL,
        compiler_params=params(16),
    )(index, *pieces, *after)


def exchange_sends(mine, theirs, after=()):
    pair = jnp.stack([mine, swap(theirs, "c")], axis=1)
    if after:
        pair = tie(pair, *after)
    return [pair[0]] + [shift(pair[k], "x", STEPS[k]) for k in range(1, 4)]


def exchange_place(pieces, index):
    def body(index_ref, *refs):
        out, sems = refs[-2:]
        copies = []
        for k in range(4):
            for h in range(2):
                to = out.at[index_ref[X_AT + k], index_ref[C_AT + h]]
                copies.append(pltpu.make_async_copy(refs[k].at[h], to, sems.at[2 * k + h]))
        for copy in copies:
            copy.start()
        for copy in copies:
            copy.wait()

    return pl.pallas_call(
        body,
        out_shape=jax.ShapeDtypeStruct((4, 2) + pieces[0].shape[1:], pieces[0].dtype),
        in_specs=[SMEM] + [VMEM] * 4,
        out_specs=ANY,
        scratch_shapes=[pltpu.SemaphoreType.DMA((8,))],
        cost_estimate=SMALL,
        compiler_params=params(16),
    )(index, *pieces)


def group_exchange(mine, theirs, index):
    return exchange_place(exchange_sends(mine, theirs), index)


def fold(mine, received, index, at, after=()):
    shape = mine.shape[1:]

    def body(index_ref, mine_ref, received_ref, *refs):
        for k, out in enumerate(refs[len(after) :]):
            spot = index_ref[at + (0, 2, 1, 3)[k]]
            total = mine_ref[spot].astype(F32) + received_ref[spot].astype(F32)
            out[...] = total.astype(out.dtype)

    return pl.pallas_call(
        body,
        out_shape=(jax.ShapeDtypeStruct(shape, F32),) + (jax.ShapeDtypeStruct(shape, BF),) * 3,
        in_specs=[SMEM, VMEM, VMEM] + [ANY] * len(after),
        out_specs=(VMEM,) * 4,
        cost_estimate=SMALL,
        compiler_params=params(40),
    )(index, mine, received, *after)


def scatter_terms(mine, theirs, pair_axis, ring_axis, index, after=()):
    at = X_AT if ring_axis == "x" else Y_AT
    own, *others = fold(mine, swap(theirs, pair_axis), index, at, after)
    return [own] + [shift(other, ring_axis, step) for step, other in zip(STEPS[1:], others)]


def total_of(terms):
    return sum(term.astype(F32) for term in terms)


def scatter(*args, **kwargs):
    return total_of(scatter_terms(*args, **kwargs))


def pair_total(parts, axis, place_at, pair_axis):
    mine, theirs = sides(parts, axis, place_at)
    return mine.astype(F32) + swap(theirs, pair_axis).astype(F32)


def sides(parts, axis, place_at):
    return (
        lax.dynamic_index_in_dim(parts, place_at, axis, keepdims=False),
        lax.dynamic_index_in_dim(parts, 1 - place_at, axis, keepdims=False),
    )


def both_in_order(mine, theirs, place_at):
    first = place_at == 0
    return jnp.stack([jnp.where(first, mine, theirs), jnp.where(first, theirs, mine)])


def low_bits(value):
    return lax.optimization_barrier(value.astype(BF))


def tensor_sum(low):
    return low.astype(F32) + swap(low, "t").astype(F32)


def exchange(value):
    return lax.all_to_all(value, ("x", "c"), split_axis=0, concat_axis=0, tiled=True)


def hand_out(index_ref, held, mine_ref, theirs_ref):
    for k in range(4):
        spot = 2 * index_ref[X_AT + (0, 2, 1, 3)[k]]
        mine_ref[k] = held[spot + index_ref[C_AT]]
        theirs_ref[k] = held[spot + index_ref[C_AT + 1]]


def pack_small(index_ref, q_ref, kv_ref, gain_ref, mine_ref, theirs_ref, held):
    rest = jnp.zeros((OWNED, 256 - Q_PART - KV_PART - 2), F32)
    half, part = HEAD_DIM // 2, KV_PART // 4
    for j in range(GROUP):
        held[j] = jnp.concatenate(
            [
                q_ref[:, Q_PART * j : Q_PART * (j + 1)],
                kv_ref[:, part * j : part * (j + 1)],
                kv_ref[:, half + part * j : half + part * (j + 1)],
                kv_ref[:, 2 * half + 2 * part * j : 2 * half + 2 * part * (j + 1)],
                gain_ref[...],
                rest,
            ],
            axis=1,
        ).astype(BF)
    hand_out(index_ref, held, mine_ref, theirs_ref)


def pack_feed(index_ref, w_ref, after_ref, mine_ref, theirs_ref, held):
    del after_ref
    rest = jnp.zeros((OWNED, F_PAD - F_PART), F32)
    for j in range(GROUP):
        held[j] = jnp.concatenate(
            [w_ref[0, :, F_PART * j : F_PART * (j + 1)], rest], axis=1
        ).astype(BF)
    hand_out(index_ref, held, mine_ref, theirs_ref)


def adam(weight, grad, moment, second, rate, decay):
    moment_new = 0.9 * moment + 0.1 * grad
    second_new = 0.95 * second + 0.05 * grad * grad
    ratio = moment_new / (1.0 - 0.9**STEP) / (jnp.sqrt(second_new / (1.0 - 0.95**STEP)) + 1e-08)
    return (moment_new, second_new, weight - rate * (ratio + decay * weight))


def adam_columns(part, start, rate, pair=False):
    if pair:
        cuts = [(start, PART), (start + PART, PART), (start + 2 * PART, 2 * PART)]
    else:
        cuts = [(start, part)]

    def body(*refs):
        *g_refs, w_ref, m_ref, v_ref, mo_ref, vo_ref, wo_ref = refs
        grad = sum(
            jnp.concatenate(
                [
                    g_ref[j, :, at : at + count].astype(F32)
                    for at, count in cuts
                    for j in range(GROUP)
                ],
                axis=1,
            )
            for g_ref in g_refs
        )
        index = (0,) if len(w_ref.shape) == 3 else (slice(None),)
        m, v, w = adam(w_ref[index], grad, m_ref[index], v_ref[index], rate, 0.1)
        mo_ref[index] = m
        vo_ref[index] = v
        wo_ref[index] = w

    return body


def window(base_ref, i):
    start = pl.multiple_of(ROWS * (base_ref[1] + i), ROWS)
    return pl.ds(start, ROWS), base_ref[0] * 8 + base_ref[1] + i >= 16


PART = HEAD_DIM // 16


def head_rows(j):
    return (
        (slice(2 * PART * j, 2 * PART * j + PART), slice(PART * j, PART * j + PART)),
        (
            slice(2 * PART * j + PART, 2 * PART * (j + 1)),
            slice(HEAD_DIM // 2 + PART * j, HEAD_DIM // 2 + PART * (j + 1)),
        ),
    )


def hold_spans(index_ref, pieces, keys, values):
    for k, piece in enumerate(pieces):
        spot = 2 * index_ref[X_AT + k % 4] + index_ref[C_AT + k // 4]
        rows = pl.ds(pl.multiple_of(2 * PART * spot, 2 * PART), 2 * PART)
        for back in range(3):
            lanes = slice(1024 * (2 - back), 1024 * (3 - back))
            keys[rows, lanes] = piece[back, : 2 * PART]
            values[rows, lanes] = piece[back, 2 * PART :]


def hold_queries(q_ref, qs):
    for h in range(LOCAL_HEADS):
        for j in range(GROUP):
            for to, at in head_rows(j):
                qs[to, ROWS * h : ROWS * (h + 1)] = q_ref[h, at]


def attend(base_ref, index_ref, q_ref, *refs):
    pieces, (p_ref, a_ref, qs, keys, values) = refs[:GROUP], refs[GROUP:]
    hold_spans(index_ref, pieces, keys, values)
    hold_queries(q_ref, qs)
    width = LOCAL_HEADS * ROWS
    key_at = lax.broadcasted_iota(jnp.int32, (ROWS, width), 0)
    query_at = lax.broadcasted_iota(jnp.int32, (ROWS, width), 1) % ROWS
    top = jnp.full((1, width), -1e30, F32)
    for i in range(TILES):
        lanes, exists = window(base_ref, i)
        scores = dot(keys[:, lanes], qs[...], 0, 0) * (HEAD_DIM**-0.5)
        if i == 0:
            scores = jnp.where((key_at > query_at) & exists, scores, -1e30)
        elif i == TILES - 1:
            scores = jnp.where(key_at <= query_at, scores, -1e30)
        else:
            scores = jnp.where(exists, scores, -1e30)
        p_ref[i] = scores
        top = jnp.maximum(top, jnp.max(scores, axis=0, keepdims=True))
    total = jnp.zeros((1, width), F32)
    for i in range(TILES):
        weights = jnp.exp(p_ref[i] - top)
        p_ref[i] = weights
        total = total + jnp.sum(weights, axis=0, keepdims=True)
    scale = 1.0 / total
    result = jnp.zeros((HEAD_DIM, width), F32)
    for i in range(TILES):
        lanes, _ = window(base_ref, i)
        probs = p_ref[i] * scale
        p_ref[i] = probs
        result = result + dot(values[:, lanes], probs.astype(BF), 1, 0)
    for h in range(LOCAL_HEADS):
        a_ref[h] = result[:, ROWS * h : ROWS * (h + 1)].astype(BF)


def attend_back(base_ref, index_ref, q_ref, p_ref, da_ref, *refs):
    pieces = refs[:GROUP]
    dq_ref, mine_ref, theirs_ref, qs, das, dps, keys, values, d_keys, d_values = refs[-10:]
    hold_spans(index_ref, pieces, keys, values)
    hold_queries(q_ref, qs)
    width = LOCAL_HEADS * ROWS
    for h in range(LOCAL_HEADS):
        das[:, ROWS * h : ROWS * (h + 1)] = da_ref[h]
    d_keys[...] = jnp.zeros(d_keys.shape, BF)
    d_values[...] = jnp.zeros(d_values.shape, BF)
    delta = jnp.zeros((1, width), F32)
    for i in range(TILES):
        lanes, _ = window(base_ref, i)
        probs = p_ref[i]
        d_probs = dot(values[:, lanes], das[...], 0, 0)
        dps[i] = d_probs
        delta = delta + jnp.sum(probs * d_probs, axis=0, keepdims=True)
        d_values[:, lanes] = dot(das[...], probs.astype(BF), 1, 1).astype(BF)
    dq = jnp.zeros((HEAD_DIM, width), F32)
    for i in range(TILES):
        lanes, _ = window(base_ref, i)
        d_scores = (p_ref[i] * (dps[i] - delta)).astype(BF)
        dq = dq + dot(keys[:, lanes], d_scores, 1, 0)
        d_keys[:, lanes] = (dot(qs[...], d_scores, 1, 1) * (HEAD_DIM**-0.5)).astype(BF)
    for h in range(LOCAL_HEADS):
        for j in range(GROUP):
            for at, to in head_rows(j):
                dq_ref[h, to] = dq[at, ROWS * h : ROWS * (h + 1)] * (HEAD_DIM**-0.5)
    core = base_ref[1] % 2
    for j in range(GROUP):
        rows = slice(2 * PART * j, 2 * PART * (j + 1))
        for ref, match in ((mine_ref, j % 2), (theirs_ref, 1 - j % 2)):

            @pl.when(core == match)
            def _(ref=ref, rows=rows, j=j):
                for back in range(3):
                    lanes = slice(1024 * (2 - back), 1024 * (3 - back))
                    ref[j // 2, back, : 2 * PART] = d_keys[rows, lanes]
                    ref[j // 2, back, 2 * PART :] = d_values[rows, lanes]


def project(x_ref, w_ref, n_ref, raw_ref, gains_ref):
    @pl.when(pl.program_id(0) == 0)
    def _():
        turned = w_ref[:, 128:].astype(F32).T
        at = Q_PART + KV_PART - 128
        gains_ref[...] = turned[at : at + 8]

    x = x_ref[...].reshape(2 * ROWS, D).astype(F32)
    normed = (x * rms_rate(x) * gains_ref[0:1]).astype(BF)
    n_ref[...] = normed.reshape(2, ROWS, D)
    raw_ref[...] = dot(normed, w_ref[...], 1, 0).T


def project_back(index_ref, sent_ref, w_ref, x_ref, mine_ref, theirs_ref, gain_ref, held):
    @pl.when(pl.program_id(0) == 0)
    def _():
        gain_ref[...] = jnp.zeros(gain_ref.shape, F32)

    sent = sent_ref[...].astype(F32).T.astype(BF)
    part = dot(sent, w_ref[:, : Q_PART + KV_PART], 1, 1)
    x = x_ref[...].reshape(2 * ROWS, D).astype(F32)
    gain_ref[0:1] += jnp.sum(part * x * rms_rate(x), axis=0, keepdims=True)
    held[...] = part.astype(BF).reshape(2, ROWS, D)
    mine_ref[0] = held[index_ref[C_AT]]
    theirs_ref[0] = held[index_ref[C_AT + 1]]


def chunk_grad(part):
    def body(index_ref, rows_ref, cols_ref, extra_ref, *refs):
        *out_refs, total, held = refs[-6:]
        step = pl.program_id(0)

        @pl.when(step == 0)
        def _():
            total[...] = jnp.zeros(total.shape, F32)
            total[part : part + 8] = extra_ref[...]

        total[:part] += dot(cols_ref[...], rows_ref[...].reshape(2 * ROWS, D), 1, 0)

        @pl.when(step == 3)
        def _():
            block, whole = GROUP * OWNED, total[...].T
            for k in range(8):
                held[k % 4, k // 4] = whole[k * block : (k + 1) * block].astype(BF)
            for k, out in enumerate(out_refs):
                out[...] = held[index_ref[Y_AT + (0, 2, 1, 3)[k]]]

    return body


def grad_by_chunk(rows, cols, extra, index, after=()):
    part = cols.shape[0]
    shape = (2, GROUP * OWNED, 256)
    return pl.pallas_call(
        chunk_grad(part),
        grid=(4,),
        out_shape=(jax.ShapeDtypeStruct(shape, BF),) * 4,
        in_specs=[
            SMEM,
            pl.BlockSpec((2, ROWS, D), lambda k: (k, 0, 0)),
            pl.BlockSpec((part, 2 * ROWS), lambda k: (0, k)),
            pl.BlockSpec((8, D), lambda k: (0, 0)),
        ]
        + [ANY] * len(after),
        out_specs=(pl.BlockSpec(shape, lambda k: (0, 0, 0)),) * 4,
        scratch_shapes=[
            pltpu.VMEM((256, D), F32),
            pltpu.VMEM((4, 2, GROUP * OWNED, 256), BF),
        ],
        cost_estimate=SMALL,
        compiler_params=params(32),
    )(index, rows, cols, extra, *after)


def row_scatter(parts, b):
    total = parts[0].astype(F32)
    for step, part in zip(STEPS[1:], parts[1:]):
        total = total + shift(part, "y", step).astype(F32)
    return pair_total(low_bits(total), 0, b, "b").astype(BF)


def rms_rate(values):
    return lax.rsqrt(jnp.mean(values * values, axis=-1, keepdims=True) + 1e-06)


def rotate(values, cosine, sine):
    first, second = values[..., 0, :, :], values[..., 1, :, :]
    return jnp.stack([first * cosine - second * sine, second * cosine + first * sine], axis=-3)


def local(
    tokens,
    cotangent,
    query_weight,
    query_moment,
    query_second,
    keyvalue_weight,
    keyvalue_moment,
    keyvalue_second,
    output_weight,
    output_moment,
    output_second,
    feedforward_weight,
    feedforward_moment,
    feedforward_second,
    norm_gains,
    gains_moment,
    gains_second,
):
    x, y, c, b = (lax.axis_index(name) for name in "xycb")
    j = 2 * x + c
    wide_rate = 1.5 * D**-0.5
    output_rate = 1.5 * (HEADS * HEAD_DIM // 32) ** -0.5
    index = jnp.stack(
        [(y + 4 - step) % 4 for step in STEPS] + [(x + 4 - step) % 4 for step in STEPS]
        + [b, 1 - b, c, 1 - c]
    ).astype(jnp.int32)
    base = jnp.stack([y, j]).astype(jnp.int32)

    inflow = tokens.astype(F32)
    parcel = jax.ShapeDtypeStruct((4, OWNED, 256), BF)
    parcels = pl.pallas_call(
        pack_small,
        out_shape=(parcel, parcel),
        in_specs=[SMEM] + [VMEM] * 3,
        out_specs=(VMEM, VMEM),
        scratch_shapes=[pltpu.VMEM((GROUP, OWNED, 256), BF)],
        cost_estimate=SMALL,
        compiler_params=params(16),
    )(index, query_weight, keyvalue_weight, norm_gains.T)
    small = group_exchange(*parcels, index).reshape(GROUP * OWNED, 256)
    group_tokens = lax.all_gather(tie(tokens, small), ("x", "c"), axis=0)
    partner = swap(small, "b")
    w_small = pair_gather(small, partner, "b", "y", index).reshape(D, 256)
    rows = tie(output_weight.astype(BF), w_small)
    rows = pair_gather(rows, swap(rows, "b"), "b", "y", index).reshape(8, OWNED, -1)
    parcel = jax.ShapeDtypeStruct((4, OWNED, 3 * F_PAD), BF)
    parcel_block = pl.BlockSpec((4, OWNED, F_PAD), lambda k: (0, 0, k))
    parcels = pl.pallas_call(
        pack_feed,
        grid=(3,),
        out_shape=(parcel, parcel),
        in_specs=[SMEM, pl.BlockSpec((1, OWNED, 8 * F_PART), lambda k: (k, 0, 0)), ANY],
        out_specs=(parcel_block, parcel_block),
        scratch_shapes=[pltpu.VMEM((GROUP, OWNED, F_PAD), BF)],
        cost_estimate=SMALL,
        compiler_params=params(24),
    )(index, feedforward_weight, partner)
    feed = exchange_sends(*parcels, (group_tokens, rows))
    feed = exchange_place(feed, index).reshape(GROUP * OWNED, 3 * F_PAD)
    feed_partner = swap(feed, "b")
    w_small = tie(w_small, feed)
    rows = tie(rows, group_tokens)
    rows_left, rows_right = shift(rows, "x", 1), shift(rows, "x", 3)

    token_block = pl.BlockSpec((2, ROWS, D), lambda k: (k, 0, 0))
    small_block = pl.BlockSpec((D, 256), lambda k: (0, 0))
    gains_block = pl.BlockSpec((8, D), lambda k: (0, 0))
    normed_a, raw, gains = pl.pallas_call(
        project,
        grid=(4,),
        out_shape=(
            jax.ShapeDtypeStruct((GROUP, ROWS, D), BF),
            jax.ShapeDtypeStruct((256, 1024), F32),
            jax.ShapeDtypeStruct((8, D), F32),
        ),
        in_specs=[token_block, small_block],
        out_specs=(token_block, pl.BlockSpec((256, 2 * ROWS), lambda k: (0, k)), gains_block),
        cost_estimate=SMALL,
        compiler_params=params(32),
    )(group_tokens, w_small)
    steps = jnp.arange(HEAD_DIM // 2, dtype=F32)
    freqs = jnp.exp(steps * (-2.0 * math.log(10000.0) / HEAD_DIM))
    first = y * 1024

    def turn(frequencies, first, count):
        places = (first + jnp.arange(count, dtype=jnp.int32)).astype(F32)
        angle = frequencies[:, None] * places[None, :]
        return jnp.cos(angle), jnp.sin(angle)

    group_turn = turn(lax.dynamic_slice_in_dim(freqs, PART * j, PART), first, 1024)
    own_turn = turn(freqs, first + ROWS * j, ROWS)
    keys = rotate(raw[Q_PART : Q_PART + 2 * PART].reshape(2, PART, 1024), *group_turn)
    values = raw[Q_PART + 2 * PART : Q_PART + KV_PART].reshape(2, PART, 1024)
    pair = jnp.concatenate([keys, values]).astype(BF).reshape(KV_PART, 1024)
    pair_back = [push(pair, "y", 1), push(pair, "y", 2)]
    q_raw = raw[:Q_PART].astype(BF).reshape(Q_PART, GROUP, ROWS).transpose(1, 0, 2)
    q_raw = exchange(q_raw)
    feed_partner = tie(feed_partner, *pair_back)
    pair_back[0] = tie(pair_back[0], q_raw, rows_left, rows_right)
    rows_left, rows_right = tie(rows_left, q_raw), tie(rows_right, q_raw)
    rows_top, rows_bottom = shift(rows_left[:4], "x", 1), shift(rows_right[4:], "x", 3)
    q_raw = q_raw.astype(F32).reshape(LOCAL_HEADS, 2, HEAD_DIM // 2, ROWS)
    queries = rotate(q_raw, *own_turn).astype(BF).reshape(LOCAL_HEADS, HEAD_DIM, ROWS)
    spans = direct(jnp.stack([pair] + pair_back), "x")
    feed_pair = both_in_order(feed, feed_partner, b)
    w_feed = lax.all_gather(feed_pair, "y", axis=1, tiled=True).reshape(D, 3 * F_PAD)
    back_pieces = direct(tie(cotangent, *spans[1:]), "x")
    spans = spans + [swap(piece, "c") for piece in spans]
    rows_top = tie(rows_top, *spans[5:])
    w_output = place_rows([rows, rows_left, rows_right, rows_top, rows_bottom], index)

    width = LOCAL_HEADS * ROWS
    held_spans = [pltpu.VMEM((HEAD_DIM, 3072), BF)] * 2
    probs, attended = pl.pallas_call(
        attend,
        out_shape=(
            jax.ShapeDtypeStruct((TILES, ROWS, width), F32),
            jax.ShapeDtypeStruct((LOCAL_HEADS, HEAD_DIM, ROWS), BF),
        ),
        in_specs=[SMEM, SMEM] + [VMEM] * 9,
        out_specs=(VMEM, VMEM),
        scratch_shapes=[pltpu.VMEM((HEAD_DIM, width), BF)] + held_spans,
        cost_estimate=SMALL,
        compiler_params=params(40),
    )(base, index, queries, *spans)
    attended = attended.reshape(LOCAL_HEADS * HEAD_DIM, ROWS)
    branch = low_bits(dot(attended, w_output, 0, 1))
    back_pieces[1:] = [tie(piece, branch) for piece in back_pieces[1:]]
    other_branch = tie(swap(branch, "t"), *back_pieces[1:])
    residual = inflow + (branch.astype(F32) + other_branch.astype(F32))

    rate_b = rms_rate(residual)
    normed_b = tie((residual * rate_b * gains[1]).astype(BF), w_feed)
    group_b = lax.all_gather(normed_b, ("x", "c"), axis=0).reshape(1024, D)
    group_back = group_place(back_pieces, index).reshape(1024, D)
    d_hidden = dot(group_back, w_feed[:, 2 * F_PAD :], 1, 0)
    gate_up = dot(group_b, w_feed[:, : 2 * F_PAD], 1, 0)
    gate, up = gate_up[:, :F_PAD], gate_up[:, F_PAD:]
    root = math.sqrt(2.0 / math.pi)
    bend = jnp.tanh(root * (gate + 0.044715 * gate * gate * gate))
    gelu = 0.5 * gate * (1.0 + bend)
    slope = 0.5 * (1.0 + bend) + 0.5 * gate * (1.0 - bend * bend) * root * (
        1.0 + 3.0 * 0.044715 * gate * gate
    )
    hidden = (gelu * up).astype(BF)
    d_gate_up = jnp.concatenate(
        [(d_hidden * up * slope).astype(BF), (d_hidden * gelu).astype(BF)], axis=1
    )
    normb_part = low_bits(dot(d_gate_up, w_feed[:, : 2 * F_PAD], 1, 1))
    normb_low = lax.psum_scatter(
        normb_part.reshape(GROUP, ROWS, D), ("x", "c"), scatter_dimension=0
    )
    down_grad = dot(tie(group_back, normb_part), hidden, 0, 0).astype(BF)
    gate_grad = dot(tie(group_b, normb_part), d_gate_up, 0, 0).astype(BF)
    feed_part = low_bits(dot(hidden, w_feed[:, 2 * F_PAD :], 1, 1)).reshape(GROUP, ROWS, D)
    normb_low = tie(normb_low, down_grad, gate_grad, feed_part)
    grad_normb = tensor_sum(normb_low)
    feed_grad = jnp.concatenate([gate_grad, down_grad], axis=1).reshape(2, -1, 3 * F_PAD)
    feed_grad = lax.psum_scatter(feed_grad, "y", scatter_dimension=1, tiled=True)
    scaled = grad_normb * gains[1]
    grad_resid = (
        cotangent.astype(F32)
        + rate_b * scaled
        - residual * rate_b**3 * jnp.mean(scaled * residual, axis=-1, keepdims=True)
    )
    gain_b = jnp.sum(grad_normb * residual * rate_b, axis=0)
    resid_low = grad_resid.astype(BF)
    grad_att = dot(w_output, resid_low, 0, 1).astype(BF).reshape(LOCAL_HEADS, HEAD_DIM, ROWS)

    span_parts = jax.ShapeDtypeStruct((4, 3, KV_PART, 1024), BF)
    grad_q, span_mine, span_theirs = pl.pallas_call(
        attend_back,
        out_shape=(
            jax.ShapeDtypeStruct((LOCAL_HEADS, HEAD_DIM, ROWS), F32),
            span_parts,
            span_parts,
        ),
        in_specs=[SMEM, SMEM] + [VMEM] * 11,
        out_specs=(VMEM, VMEM, VMEM),
        scratch_shapes=[
            pltpu.VMEM((HEAD_DIM, width), BF),
            pltpu.VMEM((HEAD_DIM, width), BF),
            pltpu.VMEM((TILES, ROWS, width), F32),
        ]
        + held_spans * 2,
        cost_estimate=SMALL,
        compiler_params=params(44),
    )(base, index, queries, probs, grad_att, *spans)
    query_grad = (
        rotate(grad_q.reshape(LOCAL_HEADS, 2, HEAD_DIM // 2, ROWS), own_turn[0], -own_turn[1])
        .astype(BF)
        .reshape(GROUP, Q_PART, ROWS)
    )
    moved = jnp.concatenate([query_grad, attended.reshape(GROUP, Q_PART, ROWS)], axis=1)
    moved = exchange(moved).transpose(1, 0, 2).reshape(2 * Q_PART, 1024)
    query_grad, group_attended = moved[:Q_PART], moved[Q_PART:]
    back_terms = scatter_terms(span_mine, span_theirs, "c", "x", index)
    back_terms[1] = tie(back_terms[1], moved)
    back = total_of(back_terms)
    back = (
        back[0]
        + push(back[1].astype(BF), "y", -1).astype(F32)
        + push(back[2].astype(BF), "y", -2).astype(F32)
    )
    grad_k = rotate(back[: 2 * PART].reshape(2, PART, 1024), group_turn[0], -group_turn[1])
    grad_v = back[2 * PART :].reshape(2, PART, 1024)
    pair_grad = jnp.concatenate([grad_k, grad_v]).astype(BF).reshape(KV_PART, 1024)

    sent = jnp.concatenate([query_grad, pair_grad])
    feed_grad = tie(feed_grad, sent)
    group_resid = lax.all_gather(tie(resid_low, feed_grad), ("x", "c"), axis=0)
    feed_grad = pair_total(feed_grad, 0, b, "b").astype(BF)
    side = jax.ShapeDtypeStruct((4, ROWS, D), BF)
    side_block = pl.BlockSpec((1, ROWS, D), lambda k: (k, 0, 0))
    norma_mine, norma_theirs, gain_a = pl.pallas_call(
        project_back,
        grid=(4,),
        out_shape=(side, side, jax.ShapeDtypeStruct((8, D), F32)),
        in_specs=[
            SMEM,
            pl.BlockSpec((Q_PART + KV_PART, 2 * ROWS), lambda k: (0, k)),
            small_block,
            token_block,
        ],
        out_specs=(side_block, side_block, gains_block),
        scratch_shapes=[pltpu.VMEM((2, ROWS, D), BF)],
        cost_estimate=SMALL,
        compiler_params=params(32),
    )(index, sent, w_small, group_tokens)
    rate_a = rms_rate(inflow)
    norma_terms = scatter_terms(norma_mine, norma_theirs, "c", "x", index)
    extra = jnp.concatenate([gain_a[:1], 0.5 * gain_b[None], jnp.zeros((6, D), F32)])
    small_parts = grad_by_chunk(normed_a, sent, extra, index, (norma_terms[0],))
    small_grad = row_scatter(small_parts, b)
    norma_terms[1:] = [tie(term, small_grad, feed_grad) for term in norma_terms[1:]]
    late = jnp.concatenate([feed_grad, small_grad], axis=1)
    late = exchange(late.reshape(GROUP, OWNED, 3 * F_PAD + 256))
    feed_grad, small_grad = late, late[:, :, 3 * F_PAD :]
    norma_low = low_bits(total_of(norma_terms))
    output_parts = grad_by_chunk(
        group_resid, group_attended, jnp.zeros((8, D), F32), index, (norma_low,)
    )
    out_low = lax.psum_scatter(
        tie(feed_part, norma_low, output_parts[0]), ("x", "c"), scatter_dimension=0
    )
    other_out = swap(out_low, "t")
    out_tokens = (residual + (out_low.astype(F32) + other_out.astype(F32))).astype(BF)
    grad_norma = tensor_sum(norma_low)
    scaled = grad_norma * gains[0]
    input_grad = (
        grad_resid
        + rate_a * scaled
        - inflow * rate_a**3 * jnp.mean(scaled * inflow, axis=-1, keepdims=True)
    )

    output_grad = exchange(row_scatter(output_parts, b).reshape(GROUP, OWNED, 256))

    def update(grads, weight, moment, second, part, start, rate, pair=False):
        return pl.pallas_call(
            adam_columns(part, start, rate, pair),
            out_shape=(jax.ShapeDtypeStruct(weight.shape, F32),) * 3,
            in_specs=[VMEM] * (3 + len(grads)),
            out_specs=(VMEM,) * 3,
            cost_estimate=SMALL,
            compiler_params=params(32),
        )(*grads, weight, moment, second)

    other_grad = swap(small_grad, "t")
    query_new = update([small_grad], query_weight, query_moment, query_second, Q_PART, 0, wide_rate)
    pair_new = update(
        [small_grad, other_grad],
        keyvalue_weight,
        keyvalue_moment,
        keyvalue_second,
        KV_PART,
        Q_PART,
        wide_rate,
        True,
    )
    output_new = update(
        [output_grad], output_weight, output_moment, output_second, Q_PART, 0, output_rate
    )
    matrix = pl.BlockSpec((1, OWNED, 8 * F_PART), lambda k: (k, 0, 0))
    feed_new = pl.pallas_call(
        adam_columns(F_PART, 0, wide_rate),
        grid=(3,),
        out_shape=(jax.ShapeDtypeStruct(feedforward_weight.shape, F32),) * 3,
        in_specs=[pl.BlockSpec((GROUP, OWNED, F_PAD), lambda k: (0, 0, k))] + [matrix] * 3,
        out_specs=(matrix,) * 3,
        cost_estimate=SMALL,
        compiler_params=params(32),
    )(feed_grad, feedforward_weight, feedforward_moment, feedforward_second)
    gain_grad = small_grad.astype(F32) + other_grad.astype(F32)
    gain_grad = jnp.sum(gain_grad[:, :, Q_PART + KV_PART : Q_PART + KV_PART + 2], axis=0).T
    gains_new = adam(norm_gains, gain_grad, gains_moment, gains_second, 0.3, 0.0)
    return (
        out_tokens,
        input_grad,
        *query_new,
        *pair_new,
        *output_new,
        *feed_new,
        *gains_new,
    )


def solution(mesh):
    grid = Mesh(mesh.devices.reshape(2, 4, 4, 2, 2), ("b", "y", "x", "c", "t"))
    rows = ("b", "y", "x", "c")
    token = P(rows, None)
    split = P(rows, "t")
    whole = P(rows, None)
    feed = P(None, rows, "t")
    gain = P(None, rows)
    weights = (split,) * 3 + (whole,) * 3 + (split,) * 3 + (feed,) * 3 + (gain,) * 3
    return jax.shard_map(
        local,
        mesh=grid,
        in_specs=(token, token) + weights,
        out_specs=(token, token) + weights,
        check_vma=False,
    )
```

time: 714 us -> 589 us (0.82)
  waiting for transfers between devices: 284 us -> 225 us
  starting transfers between devices: 144 us -> 102 us
  blocking collectives: 30.7 us -> 13.6 us
  matrix products: 61.4 us -> 52.3 us
  Pallas kernels: 48.7 us -> 57.6 us
  other arithmetic: 52.1 us -> 44.5 us
    reduce_scatter x4 -> x3, waiting for transfers between devices: 63.4 us -> 22.1 us  [the longest x1 11.3 us: local(): lax.psum_scatter(normb_part.reshape(GROUP, ROWS, D), ('x', 'c'), scatter_...]
    all_gather x2 -> x4, waiting for transfers between devices: 0.01 us -> 27.9 us  [the longest x1 27.8 us: local(): group_b = lax.all_gather(normed_b, ('x', 'c'), axis=0).reshape(1024, D)]
    ppermute x54 -> x34, waiting for transfers between devices: 132 us -> 107 us  [shift(): return lax.ppermute(value, axis, [(i, (i + step) % 4) for i in range(4)])]
    pallas_call x5 -> x41, Pallas kernels: 8.08 us -> 31.5 us  [the longest x2 6.09 us: grad_by_chunk(): pl.pallas_call(chunk_grad(part), grid=(4,), out_shape=(jax.ShapeDtypeStru...]
    ppermute x54 -> x34, starting transfers between devices: 77.4 us -> 55.5 us  [shift(): return lax.ppermute(value, axis, [(i, (i + step) % 4) for i in range(4)])]
    all_to_all x7 -> x3, starting transfers between devices: 29.7 us -> 11.9 us  [exchange(): lax.all_to_all(value, ('x', 'c'), split_axis=0, concat_axis=0, tiled=True)]
    all_to_all x2 -> x1, blocking collectives: 30.7 us -> 13.6 us  [exchange(): lax.all_to_all(value, ('x', 'c'), split_axis=0, concat_axis=0, tiled=True)]
    pallas_call x9 -> x2, Pallas kernels: 22.7 us -> 5.76 us  [place(): pl.pallas_call(body, out_shape=jax.ShapeDtypeStruct(shape, pieces[0].dtyp...]
  transfers between devices with their start and end apart: 117 -> 76, of which waited for: 38 -> 41; matrix products, arithmetic and copies ran while one was open for 19% -> 15% of each run, Pallas kernels for 6% -> 9%
where the time goes in v2:
time: 589 us; the launch traced here: 578 us
  waiting for transfers between devices  225 us (38%)
  starting transfers between devices  102 us (17%)
  local copies, waits for them, and re-layouts  67.3 us (11%)
  Pallas kernels  57.6 us (10%)
  matrix products  52.3 us (9%)
  other arithmetic  44.5 us (8%)
  between operations  16.1 us (3%)
  blocking collectives  13.6 us (2%)
    ppermute x34, waiting for transfers between devices, shift(): return lax.ppermute(value, axis, [(i, (i + step) % 4) for i in range(4)])  107 us
    ppermute x34, starting transfers between devices, shift(): return lax.ppermute(value, axis, [(i, (i + step) % 4) for i in range(4)])  55.5 us
    unnamed x244, local copies, waits for them, and re-layouts  54.2 us
    dot_general x8, matrix products, dot(): lax.dot_general(left, right, (((left_dim,), (right_dim,)), ((), ())), pre...  52.3 us
    ppermute x28, waiting for transfers between devices, swap(): return lax.ppermute(value, axis, [(0, 1), (1, 0)])  45.9 us
    all_gather x1, waiting for transfers between devices, local(): group_b = lax.all_gather(normed_b, ('x', 'c'), axis=0).reshape(1024, D)  27.8 us
    ppermute x28, starting transfers between devices, swap(): return lax.ppermute(value, axis, [(0, 1), (1, 0)])  23.9 us
    all_to_all x3, waiting for transfers between devices, exchange(): lax.all_to_all(value, ('x', 'c'), split_axis=0, concat_axis=0, tiled=True)  15 us
  transfers between devices with their start and end apart: 76, of which 41 were waited for; matrix products, arithmetic and copies ran while one was open for 15% of the time, Pallas kernels for 9%

profile of v2, /device:TPU:0, one launch (start us, length us, event | category | flops | bytes accessed | tf_op | source)
XLA Modules:
  0.0 577.7 jit_solution(1928331817797970361)
XLA Ops:
  25.3 3.3 collective-permute-done.4.after_ref
  37.0 2.6 collective-permute-done.5.refs_1_
  39.6 4.0 collective-permute-done.6.refs_2_
  50.5 3.1 collective-permute-done.9
  59.0 2.6 collective-permute-done.10.refs_1_
  73.0 3.6 collective-permute-done.13.refs_1_
  87.4 4.1 shard_map.306
  97.2 5.1 collective-permute-start.19
  110.1 2.9 collective-permute-start.18
  114.2 13.6 %all_to_all.20.refs_1_ = bf16[8,160,128]{2,1,0:T(8,128)(2,1)} all-to-all(bf16[8,160,128]{2,1,0:T(8,128)(2,1)S(1)} %bitcast_bitcast_fusion), channel_id=1, replica_groups=mesh['b'=2,'y'=4,'x'=4,'c'=2,'t'=2] {'x','c'}, dimensions={0} | all-to-all | bytes 655360 | tf_op jit(solution)/shard_map/all_to_all | solution.py:271
  135.9 2.7 collective-permute-start.22
  140.5 3.2 collective-permute-done.20.refs_1_
  143.8 7.8 %collective-permute-done.21.refs_2_ = bf16[3,64,1024]{2,1,0:T(8,128)(2,1)S(1)} collective-permute-done((bf16[3,64,1024]{2,1,0:T(8,128)(2,1)S(1)}, bf16[3,64,1024]{2,1,0:T(8,128)(2,1)S(1)}, u32[]{:S(2)}, u32[]{:S(2)}) %collective-permute-start.21) | collective-permute-done | bytes 393248 | tf_op jit(solution)/shard_map/ppermute | solution.py:45
  151.6 9.4 %collective-permute-done.22.refs_3_ = bf16[3,64,1024]{2,1,0:T(8,128)(2,1)} collective-permute-done((bf16[3,64,1024]{2,1,0:T(8,128)(2,1)S(1)}, bf16[3,64,1024]{2,1,0:T(8,128)(2,1)}, u32[]{:S(2)}, u32[]{:S(2)}) %collective-permute-start.22) | collective-permute-done | bytes 393248 | tf_op jit(solution)/shard_map/ppermute | solution.py:45
  173.3 5.9 %shard_map.309 = (f32[17,128,640]{2,1,0:T(8,128)S(1)}, bf16[5,256,128]{2,1,0:T(8,128)(2,1)S(1)}) custom-call(s32[2]{0:T(128)S(1)} %pad_add_fusion.base_ref, s32[12]{0:T(128)S(1)} %stack.140.index_ref, bf16[5,256,128]{2,1,0:T(8,128)(2,1)S(1)} %bitcast.163, bf16[3,64,1024]{2,1,0:T(8,128)(2,1)S(1)} %pad_maximum_fusion.9.refs_0_, ...), custom_call_target="tpu_custom_call" | custom-call | flops 1 | bytes 1 | tf_op jit(solution)/shard_map/pallas_call | solution.py:659
  179.3 3.2 collective-permute-start.36
  182.6 2.7 shard_map.313
  188.1 3.6 collective-permute-start.34
  193.3 18.0 %collective-permute-done.35.refs_0_ = bf16[128,2560]{1,0:T(8,128)(2,1)S(1)} collective-permute-done((bf16[128,2560]{1,0:T(8,128)(2,1)S(1)}, bf16[128,2560]{1,0:T(8,128)(2,1)S(1)}, u32[]{:S(2)}, u32[]{:S(2)}) %collective-permute-start.35) | collective-permute-done | bytes 655392 | tf_op jit(solution)/shard_map/ppermute | solution.py:45
  222.3 3.0 shard_map.321
  227.6 27.8 %all-gather.12.cloned.1.call-done.refs_0_ = bf16[1024,2560]{1,0:T(8,128)(2,1)} async-done(((bf16[128,2560]{1,0:T(8,128)(2,1)}), bf16[1024,2560]{1,0:T(8,128)(2,1)}) %all-gather.12.cloned.1.call-update) | async-done | bytes 5242896 | tf_op jit(solution)/shard_map/all_gather | solution.py:679
  255.4 9.3 %fusion.1 = f32[1024,1024]{0,1:T(8,128)S(1)} fusion(bf16[1024,2560]{1,0:T(8,128)(2,1)} %all-gather.12.cloned.1.call-done.refs_0_, bf16[2560,1536]{1,0:T(8,128)(2,1)} %bitcast.183), kind=kOutput, calls=%fused_computation.5 | convolution fusion | flops 5368709120 | bytes 14680064 | tf_op jit(solution)/shard_map/dot_general | solution.py:39
  264.8 7.2 %fusion.12 = (bf16[1024,512]{0,1:T(8,128)(2,1)S(1)}, bf16[1024,512]{0,1:T(8,128)(2,1)S(1)}, bf16[1024,512]{0,1:T(8,128)(2,1)}) fusion(f32[1024,1024]{0,1:T(8,128)S(1)} %fusion.1, bf16[1024,2560]{1,0:T(8,128)(2,1)S(1)} %bitcast.159, bf16[2560,1536]{1,0:T(8,128)(2,1)} %bitcast.184), kind=kOutput, calls=%fused_computation.25 | convolution fusion | flops 2697461760 | bytes 15204352 | tf_op jit(solution)/shard_map/dot_general | solution.py:39
  272.0 7.5 %convolution_convert_fusion.2.refs_1_ = bf16[1024,2560]{1,0:T(8,128)(2,1)} fusion(bf16[2560,1536]{1,0:T(8,128)(2,1)S(1)} %bitcast.188, bf16[1024,512]{0,1:T(8,128)(2,1)S(1)} %get-tuple-element.136, bf16[1024,512]{0,1:T(8,128)(2,1)S(1)} %get-tuple-element.135), kind=kOutput, calls=%fused_computation.3 | convolution fusion | flops 5375524864 | bytes 12582912 | tf_op jit(solution)/shard_map/dot_general | solution.py:39
  279.8 5.9 %convolution_convert_fusion.3.refs_1_ = bf16[2560,512]{1,0:T(8,128)(2,1)S(1)} fusion(bf16[1024,2560]{1,0:T(8,128)(2,1)} %shard_map.322, bf16[1024,512]{0,1:T(8,128)(2,1)} %get-tuple-element.137), kind=kOutput, calls=%fused_computation.7 | convolution fusion | flops 2685665280 | bytes 8912896 | tf_op jit(solution)/shard_map/dot_general | solution.py:39
  285.7 8.4 %convolution_convert_fusion.1.refs_2_ = bf16[2560,1024]{1,0:T(8,128)(2,1)} fusion(bf16[1024,2560]{1,0:T(8,128)(2,1)S(1)} %copy-done.82, bf16[1024,512]{0,1:T(8,128)(2,1)S(1)} %copy-done.117, bf16[1024,512]{0,1:T(8,128)(2,1)S(1)} %copy-done.115), kind=kOutput, calls=%fused_computation.2 | convolution fusion | flops 5375524864 | bytes 12582912 | tf_op jit(solution)/shard_map/dot_general | solution.py:39
  294.1 6.5 %pad_maximum_fusion = bf16[2560,1536]{1,0:T(8,128)(2,1)} fusion(bf16[2560,512]{1,0:T(8,128)(2,1)S(1)} %convolution_convert_fusion.3.refs_1_, bf16[2560,1024]{1,0:T(8,128)(2,1)} %convolution_convert_fusion.1.refs_2_), kind=kLoop, calls=%fused_computation | loop fusion | flops 15728640 | bytes 15728640 | tf_op jit(solution)/shard_map/concatenate | solution.py:703
  301.8 6.5 %convolution_convert_fusion = bf16[1024,2560]{1,0:T(8,128)(2,1)} fusion(bf16[1024,512]{0,1:T(8,128)(2,1)S(1)} %copy-done.113, bf16[2560,1536]{1,0:T(8,128)(2,1)} %bitcast.185), kind=kOutput, calls=%fused_computation.1 | convolution fusion | flops 2686976000 | bytes 8912896 | tf_op jit(solution)/shard_map/dot_general | solution.py:39
  308.4 11.3 %reduce-scatter.4.cloned.1.call-done = bf16[1,128,2560]{2,1,0:T(8,128)(2,1)} async-done(((bf16[8,128,2560]{2,1,0:T(8,128)(2,1)}), bf16[1,128,2560]{2,1,0:T(8,128)(2,1)}) %reduce-scatter.4.cloned.1.call-update) | async-done | bytes 655376 | tf_op jit(solution)/shard_map/reduce_scatter | solution.py:695
  319.7 3.4 collective-permute-start.43
  323.1 12.4 %collective-permute-done.43 = bf16[128,2560]{1,0:T(8,128)(2,1)S(1)} collective-permute-done((bf16[128,2560]{1,0:T(8,128)(2,1)}, bf16[128,2560]{1,0:T(8,128)(2,1)S(1)}, u32[]{:S(2)}, u32[]{:S(2)}) %collective-permute-start.43) | collective-permute-done | bytes 655392 | tf_op jit(solution)/shard_map/ppermute | solution.py:53
  339.4 5.2 convolution_convert_fusion.5
  344.7 10.8 %shard_map.325 = (f32[5,256,128]{2,1,0:T(8,128)S(1)}, bf16[4,3,64,1024]{3,2,1,0:T(8,128)(2,1)S(1)}, bf16[4,3,64,1024]{3,2,1,0:T(8,128)(2,1)}) custom-call(s32[2]{0:T(128)S(1)} %pad_add_fusion.base_ref, s32[12]{0:T(128)S(1)} %stack.140.index_ref, bf16[5,256,128]{2,1,0:T(8,128)(2,1)S(1)} %bitcast.164, f32[17,128,640]{2,1,0:T(8,128)} %copy-done.22, ...), custom_call_target="tpu_custom_call" | custom-call | flops 1 | bytes 1 | tf_op jit(solution)/shard_map/pallas_call | solution.py:716
  356.6 4.2 all-to-all-start.1
  365.3 2.7 collective-permute-start.47
  369.7 3.3 all-to-all-done.1
  375.1 5.6 collective-permute-done.45.refs_0_
  381.5 7.9 %collective-permute-done.47 = bf16[3,64,1024]{2,1,0:T(8,128)(2,1)S(1)} collective-permute-done((bf16[3,64,1024]{2,1,0:T(8,128)(2,1)}, bf16[3,64,1024]{2,1,0:T(8,128)(2,1)S(1)}, u32[]{:S(2)}, u32[]{:S(2)}) %collective-permute-start.47) | collective-permute-done | bytes 393248 | tf_op jit(solution)/shard_map/ppermute | solution.py:45
  395.1 4.3 collective-permute-done.49
  404.6 4.9 shard_map.328
  411.2 5.1 collective-permute-done.50.received_ref
  420.3 3.1 copy-done.24
  423.4 3.2 shard_map.330
  426.6 4.4 collective-permute-start.54
  431.0 3.0 collective-permute-start.53
  436.6 2.9 collective-permute-done.54
  439.5 6.8 %collective-permute-done.53 = bf16[2,320,256]{2,1,0:T(8,128)(2,1)S(1)} collective-permute-done((bf16[2,320,256]{2,1,0:T(8,128)(2,1)S(1)}, bf16[2,320,256]{2,1,0:T(8,128)(2,1)S(1)}, u32[]{:S(2)}, u32[]{:S(2)}) %collective-permute-start.53) | collective-permute-done | bytes 327712 | tf_op jit(solution)/shard_map/ppermute | solution.py:45
  454.4 7.4 %collective-permute-done.55 = bf16[320,256]{1,0:T(8,128)(2,1)S(1)} collective-permute-done((bf16[320,256]{1,0:T(8,128)(2,1)}, bf16[320,256]{1,0:T(8,128)(2,1)S(1)}, u32[]{:S(2)}, u32[]{:S(2)}) %collective-permute-start.55) | collective-permute-done | bytes 163872 | tf_op jit(solution)/shard_map/ppermute | solution.py:53
  463.5 2.7 fusion.13.refs_2_
  466.2 3.3 collective-permute-done.58.refs_0_
  469.4 12.3 %collective-permute-done.57.refs_0_ = bf16[128,2560]{1,0:T(8,128)(2,1)} collective-permute-done((bf16[128,2560]{1,0:T(8,128)(2,1)S(1)}, bf16[128,2560]{1,0:T(8,128)(2,1)}, u32[]{:S(2)}, u32[]{:S(2)}) %collective-permute-start.57) | collective-permute-done | bytes 655392 | tf_op jit(solution)/shard_map/ppermute | solution.py:45
  483.6 2.7 copy-done.25
  486.2 2.9 shard_map.336
  491.7 2.9 collective-permute-start.60
  495.6 4.3 all-to-all-start.2
  499.9 9.9 %collective-permute-done.60 = bf16[128,2560]{1,0:T(8,128)(2,1)} collective-permute-done((bf16[128,2560]{1,0:T(8,128)(2,1)S(1)}, bf16[128,2560]{1,0:T(8,128)(2,1)}, u32[]{:S(2)}, u32[]{:S(2)}) %collective-permute-start.60) | collective-permute-done | bytes 655392 | tf_op jit(solution)/shard_map/ppermute | solution.py:53
  511.7 3.6 collective-permute-start.64
  517.3 5.9 %all-to-all-done.2.refs_0_ = bf16[8,40,1792]{2,1,0:T(8,128)(2,1)S(1)} async-done(((bf16[8,40,1792]{2,1,0:T(8,128)(2,1)}), bf16[8,40,1792]{2,1,0:T(8,128)(2,1)S(1)}, u32[]{:S(2)}, u32[]{:S(2)}) %all-to-all-start.2) | async-done | bytes 1146912 | tf_op jit(solution)/shard_map/all_to_all | solution.py:271
  524.3 5.5 collective-permute-done.63
  533.1 10.8 %reduce-scatter.8.cloned.1.call-done = bf16[1,128,2560]{2,1,0:T(8,128)(2,1)} async-done(((bf16[8,128,2560]{2,1,0:T(8,128)(2,1)}), bf16[1,128,2560]{2,1,0:T(8,128)(2,1)}) %reduce-scatter.8.cloned.1.call-update) | async-done | bytes 655376 | tf_op jit(solution)/shard_map/reduce_scatter | solution.py:788
  545.6 3.2 fusion.16
  551.4 3.6 shard_map.341
  556.9 3.4 all-to-all-start.3
  560.9 5.8 %all-to-all-done.3.refs_0_ = bf16[8,40,256]{2,1,0:T(8,128)(2,1)S(1)} async-done(((bf16[8,40,256]{2,1,0:T(8,128)(2,1)}), bf16[8,40,256]{2,1,0:T(8,128)(2,1)S(1)}, u32[]{:S(2)}, u32[]{:S(2)}) %all-to-all-start.3) | async-done | bytes 163872 | tf_op jit(solution)/shard_map/all_to_all | solution.py:271
  (467 shorter events, 183.2 us)
Async XLA Ops:
  7.2 60.6 %all-gather.10.cloned.1.call-start = ((), (), s32[]{:S(2)}) async-start(), calls=%async_computation.11 | async-start | bytes 5898240 | tf_op jit(solution)/shard_map/all_gather | solution.py:586
  12.1 7.2 %collective-permute-start.1 = (bf16[2,40,256]{2,1,0:T(8,128)(2,1)S(1)}, bf16[2,40,256]{2,1,0:T(8,128)(2,1)S(1)}, u32[]{:S(2)}, u32[]{:S(2)}) collective-permute-start(bf16[2,40,256]{2,1,0:T(8,128)(2,1)S(1)} %get-tuple-element.158), channel_id=1, source_target_pairs={{0,4},{4,8},{8,12},{12,0},{1,5},{5,9},{9,13},{13,1},{2,6},{6,10},{... | collective-permute-start | bytes 122888 | tf_op jit(solution)/shard_map/ppermute | solution.py:45
  13.7 5.5 collective-permute-start.2
  22.5 194.6 %all-gather.8.cloned.1.call-start = ((), (), s32[]{:S(2)}) async-start(), calls=%async_computation.7 | async-start | bytes 9830400 | tf_op jit(solution)/shard_map/all_gather | solution.py:651
  28.7 10.9 %collective-permute-start.5 = (bf16[2,320,256]{2,1,0:T(8,128)(2,1)S(1)}, bf16[2,320,256]{2,1,0:T(8,128)(2,1)S(1)}, u32[]{:S(2)}, u32[]{:S(2)}) collective-permute-start(bf16[2,320,256]{2,1,0:T(8,128)(2,1)S(1)} %pad_maximum_fusion.10.refs_0_), channel_id=1, source_target_pairs={{0,16},{16,32},{32,48},{48,0},{1,17},{17,33},{33,49},{49,1},{2,18}... | collective-permute-start | bytes 983048 | tf_op jit(solution)/shard_map/ppermute | solution.py:45
  30.4 13.2 %collective-permute-start.6 = (bf16[2,320,256]{2,1,0:T(8,128)(2,1)S(1)}, bf16[2,320,256]{2,1,0:T(8,128)(2,1)S(1)}, u32[]{:S(2)}, u32[]{:S(2)}) collective-permute-start(bf16[2,320,256]{2,1,0:T(8,128)(2,1)S(1)} %pad_maximum_fusion.10.refs_0_), channel_id=1, source_target_pairs={{0,48},{16,0},{32,16},{48,32},{1,49},{17,1},{33,17},{49,33},{2,50}... | collective-permute-start | bytes 983048 | tf_op jit(solution)/shard_map/ppermute | solution.py:45
  32.0 13.4 %collective-permute-start.7 = (bf16[2,320,256]{2,1,0:T(8,128)(2,1)S(1)}, bf16[2,320,256]{2,1,0:T(8,128)(2,1)S(1)}, u32[]{:S(2)}, u32[]{:S(2)}) collective-permute-start(bf16[2,320,256]{2,1,0:T(8,128)(2,1)S(1)} %pad_maximum_fusion.10.refs_0_), channel_id=1, source_target_pairs={{0,32},{16,48},{32,0},{48,16},{1,33},{17,49},{33,1},{49,17},{2,34}... | collective-permute-start | bytes 983048 | tf_op jit(solution)/shard_map/ppermute | solution.py:45
  36.3 21.7 %collective-permute-start.8 = (bf16[4,40,1536]{2,1,0:T(8,128)(2,1)}, bf16[4,40,1536]{2,1,0:T(8,128)(2,1)S(1)}, u32[]{:S(2)}, u32[]{:S(2)}) collective-permute-start(bf16[4,40,1536]{2,1,0:T(8,128)(2,1)} %get-tuple-element.63), channel_id=1, source_target_pairs={{0,2},{2,0},{1,3},{3,1},{4,6},{6,4},{5,7},{7,5},{8,10},{10,8},{9,1... | collective-permute-start | bytes 1474568 | tf_op jit(solution)/shard_map/ppermute | solution.py:53
  54.6 7.0 %collective-permute-start.10 = (bf16[2,40,1280]{2,1,0:T(8,128)(2,1)S(1)}, bf16[2,40,1280]{2,1,0:T(8,128)(2,1)S(1)}, u32[]{:S(2)}, u32[]{:S(2)}) collective-permute-start(bf16[2,40,1280]{2,1,0:T(8,128)(2,1)S(1)} %pad_maximum_fusion.13.refs_0_), channel_id=1, source_target_pairs={{0,16},{16,32},{32,48},{48,0},{1,17},{17,33},{33,49},{49,1},{2,18}... | collective-permute-start | bytes 614408 | tf_op jit(solution)/shard_map/ppermute | solution.py:45
  55.8 7.6 %collective-permute-start.11 = (bf16[2,40,1280]{2,1,0:T(8,128)(2,1)S(1)}, bf16[2,40,1280]{2,1,0:T(8,128)(2,1)S(1)}, u32[]{:S(2)}, u32[]{:S(2)}) collective-permute-start(bf16[2,40,1280]{2,1,0:T(8,128)(2,1)S(1)} %pad_maximum_fusion.13.refs_0_), channel_id=1, source_target_pairs={{0,48},{16,0},{32,16},{48,32},{1,49},{17,1},{33,17},{49,33},{2,50}... | collective-permute-start | bytes 614408 | tf_op jit(solution)/shard_map/ppermute | solution.py:45
  57.9 7.3 %collective-permute-start.12 = (bf16[2,40,1280]{2,1,0:T(8,128)(2,1)S(1)}, bf16[2,40,1280]{2,1,0:T(8,128)(2,1)S(1)}, u32[]{:S(2)}, u32[]{:S(2)}) collective-permute-start(bf16[2,40,1280]{2,1,0:T(8,128)(2,1)S(1)} %pad_maximum_fusion.13.refs_0_), channel_id=1, source_target_pairs={{0,32},{16,48},{32,0},{48,16},{1,33},{17,49},{33,1},{49,17},{2,34}... | collective-permute-start | bytes 614408 | tf_op jit(solution)/shard_map/ppermute | solution.py:45
  69.1 7.5 %collective-permute-start.13 = (bf16[2,40,1536]{2,1,0:T(8,128)(2,1)S(1)}, bf16[2,40,1536]{2,1,0:T(8,128)(2,1)S(1)}, u32[]{:S(2)}, u32[]{:S(2)}) collective-permute-start(bf16[2,40,1536]{2,1,0:T(8,128)(2,1)S(1)} %get-tuple-element.144), channel_id=1, source_target_pairs={{0,4},{4,8},{8,12},{12,0},{1,5},{5,9},{9,13},{13,1},{2,6},{6,10},{... | collective-permute-start | bytes 737288 | tf_op jit(solution)/shard_map/ppermute | solution.py:45
  69.9 8.9 %collective-permute-start.14 = (bf16[2,40,1536]{2,1,0:T(8,128)(2,1)S(1)}, bf16[2,40,1536]{2,1,0:T(8,128)(2,1)S(1)}, u32[]{:S(2)}, u32[]{:S(2)}) collective-permute-start(bf16[2,40,1536]{2,1,0:T(8,128)(2,1)S(1)} %get-tuple-element.143), channel_id=1, source_target_pairs={{0,12},{4,0},{8,4},{12,8},{1,13},{5,1},{9,5},{13,9},{2,14},{6,2},{... | collective-permute-start | bytes 737288 | tf_op jit(solution)/shard_map/ppermute | solution.py:45
  72.4 7.7 %collective-permute-start.15 = (bf16[2,40,1536]{2,1,0:T(8,128)(2,1)S(1)}, bf16[2,40,1536]{2,1,0:T(8,128)(2,1)S(1)}, u32[]{:S(2)}, u32[]{:S(2)}) collective-permute-start(bf16[2,40,1536]{2,1,0:T(8,128)(2,1)S(1)} %get-tuple-element.142), channel_id=1, source_target_pairs={{0,8},{4,12},{8,0},{12,4},{1,9},{5,13},{9,1},{13,5},{2,10},{6,14},... | collective-permute-start | bytes 737288 | tf_op jit(solution)/shard_map/ppermute | solution.py:45
  81.7 23.1 %collective-permute-start.38 = (bf16[320,1536]{1,0:T(8,128)(2,1)}, bf16[320,1536]{1,0:T(8,128)(2,1)S(1)}, u32[]{:S(2)}, u32[]{:S(2)}) collective-permute-start(bf16[320,1536]{1,0:T(8,128)(2,1)} %bitcast.35.refs_1_), channel_id=1, source_target_pairs={{0,64},{64,0},{1,65},{65,1},{2,66},{66,2},{3,67},{67,3},{4,68},{68... | collective-permute-start | bytes 2949128 | tf_op jit(solution)/shard_map/ppermute | solution.py:53
  95.1 7.2 %collective-permute-start.16 = (bf16[64,1024]{1,0:T(8,128)(2,1)S(1)}, bf16[64,1024]{1,0:T(8,128)(2,1)S(1)}, u32[]{:S(2)}, u32[]{:S(2)}) collective-permute-start(bf16[64,1024]{1,0:T(8,128)(2,1)S(1)} %bitcast.198), channel_id=1, source_target_pairs={{0,16},{16,32},{32,48},{1,17},{17,33},{33,49},{2,18},{18,34},{34,5... | collective-permute-start | bytes 393224 | tf_op jit(solution)/shard_map/ppermute | solution.py:49
  97.2 7.6 %collective-permute-start.19 = (bf16[64,1024]{1,0:T(8,128)(2,1)S(1)}, bf16[64,1024]{1,0:T(8,128)(2,1)S(1)}, u32[]{:S(2)}, u32[]{:S(2)}) collective-permute-start(bf16[64,1024]{1,0:T(8,128)(2,1)S(1)} %bitcast.199), channel_id=1, source_target_pairs={{0,32},{16,48},{1,33},{17,49},{2,34},{18,50},{3,35},{19,51},{4,36}... | collective-permute-start | bytes 393224 | tf_op jit(solution)/shard_map/ppermute | solution.py:49
  109.6 145.8 %all-gather.12.cloned.1.call-start = ((), (), s32[]{:S(2)}) async-start(), calls=%async_computation.12 | async-start | bytes 5898240 | tf_op jit(solution)/shard_map/all_gather | solution.py:679
  109.7 18.0 %collective-permute-start.17 = (bf16[8,40,1280]{2,1,0:T(8,128)(2,1)}, bf16[8,40,1280]{2,1,0:T(8,128)(2,1)S(1)}, u32[]{:S(2)}, u32[]{:S(2)}) collective-permute-start(bf16[8,40,1280]{2,1,0:T(8,128)(2,1)} %shard_map.307.refs_0_), channel_id=1, source_target_pairs={{0,4},{4,8},{8,12},{12,0},{1,5},{5,9},{9,13},{13,1},{2,6},{6,10},{... | collective-permute-start | bytes 2457608 | tf_op jit(solution)/shard_map/ppermute | solution.py:45
  110.1 17.7 %collective-permute-start.18 = (bf16[8,40,1280]{2,1,0:T(8,128)(2,1)}, bf16[8,40,1280]{2,1,0:T(8,128)(2,1)S(1)}, u32[]{:S(2)}, u32[]{:S(2)}) collective-permute-start(bf16[8,40,1280]{2,1,0:T(8,128)(2,1)} %shard_map.307.refs_0_), channel_id=1, source_target_pairs={{0,12},{4,0},{8,4},{12,8},{1,13},{5,1},{9,5},{13,9},{2,14},{6,2},{... | collective-permute-start | bytes 2457608 | tf_op jit(solution)/shard_map/ppermute | solution.py:45
  130.5 13.3 %collective-permute-start.20 = (bf16[3,64,1024]{2,1,0:T(8,128)(2,1)S(1)}, bf16[3,64,1024]{2,1,0:T(8,128)(2,1)S(1)}, u32[]{:S(2)}, u32[]{:S(2)}) collective-permute-start(bf16[3,64,1024]{2,1,0:T(8,128)(2,1)S(1)} %pad_maximum_fusion.9.refs_0_), channel_id=1, source_target_pairs={{0,4},{4,8},{8,12},{12,0},{1,5},{5,9},{9,13},{13,1},{2,6},{6,10},{... | collective-permute-start | bytes 1179656 | tf_op jit(solution)/shard_map/ppermute | solution.py:45
  132.0 19.6 %collective-permute-start.21 = (bf16[3,64,1024]{2,1,0:T(8,128)(2,1)S(1)}, bf16[3,64,1024]{2,1,0:T(8,128)(2,1)S(1)}, u32[]{:S(2)}, u32[]{:S(2)}) collective-permute-start(bf16[3,64,1024]{2,1,0:T(8,128)(2,1)S(1)} %pad_maximum_fusion.9.refs_0_), channel_id=1, source_target_pairs={{0,12},{4,0},{8,4},{12,8},{1,13},{5,1},{9,5},{13,9},{2,14},{6,2},{... | collective-permute-start | bytes 1179656 | tf_op jit(solution)/shard_map/ppermute | solution.py:45
  135.7 25.3 %collective-permute-start.27 = (bf16[4,40,1280]{2,1,0:T(8,128)(2,1)}, bf16[4,40,1280]{2,1,0:T(8,128)(2,1)}, u32[]{:S(2)}, u32[]{:S(2)}) collective-permute-start(bf16[4,40,1280]{2,1,0:T(8,128)(2,1)} %slice.178), channel_id=1, source_target_pairs={{0,4},{4,8},{8,12},{12,0},{1,5},{5,9},{9,13},{13,1},{2,6},{6,10},{... | collective-permute-start | bytes 1228808 | tf_op jit(solution)/shard_map/ppermute | solution.py:45
  135.9 25.1 %collective-permute-start.22 = (bf16[3,64,1024]{2,1,0:T(8,128)(2,1)S(1)}, bf16[3,64,1024]{2,1,0:T(8,128)(2,1)}, u32[]{:S(2)}, u32[]{:S(2)}) collective-permute-start(bf16[3,64,1024]{2,1,0:T(8,128)(2,1)S(1)} %pad_maximum_fusion.9.refs_0_), channel_id=1, source_target_pairs={{0,8},{4,12},{8,0},{12,4},{1,9},{5,13},{9,1},{13,5},{2,10},{6,14},... | collective-permute-start | bytes 1179656 | tf_op jit(solution)/shard_map/ppermute | solution.py:45
  139.6 21.9 %collective-permute-start.28 = (bf16[4,40,1280]{2,1,0:T(8,128)(2,1)S(1)}, bf16[4,40,1280]{2,1,0:T(8,128)(2,1)S(1)}, u32[]{:S(2)}, u32[]{:S(2)}) collective-permute-start(bf16[4,40,1280]{2,1,0:T(8,128)(2,1)S(1)} %slice.179), channel_id=1, source_target_pairs={{0,12},{4,0},{8,4},{12,8},{1,13},{5,1},{9,5},{13,9},{2,14},{6,2},{... | collective-permute-start | bytes 1228808 | tf_op jit(solution)/shard_map/ppermute | solution.py:45
  143.8 17.9 %collective-permute-start.24 = (bf16[3,64,1024]{2,1,0:T(8,128)(2,1)S(1)}, bf16[3,64,1024]{2,1,0:T(8,128)(2,1)S(1)}, u32[]{:S(2)}, u32[]{:S(2)}) collective-permute-start(bf16[3,64,1024]{2,1,0:T(8,128)(2,1)S(1)} %collective-permute-done.20.refs_1_), channel_id=1, source_target_pairs={{0,2},{2,0},{1,3},{3,1},{4,6},{6,4},{5,7},{7,5},{8,10},{10,8},{9,1... | collective-permute-start | bytes 1179656 | tf_op jit(solution)/shard_map/ppermute | solution.py:53
  151.6 10.6 %collective-permute-start.25 = (bf16[3,64,1024]{2,1,0:T(8,128)(2,1)S(1)}, bf16[3,64,1024]{2,1,0:T(8,128)(2,1)S(1)}, u32[]{:S(2)}, u32[]{:S(2)}) collective-permute-start(bf16[3,64,1024]{2,1,0:T(8,128)(2,1)S(1)} %collective-permute-done.21.refs_2_), channel_id=1, source_target_pairs={{0,2},{2,0},{1,3},{3,1},{4,6},{6,4},{5,7},{7,5},{8,10},{10,8},{9,1... | collective-permute-start | bytes 1179656 | tf_op jit(solution)/shard_map/ppermute | solution.py:53
  161.5 17.7 %collective-permute-start.29 = (bf16[8,40,1280]{2,1,0:T(8,128)(2,1)S(1)}, bf16[8,40,1280]{2,1,0:T(8,128)(2,1)}, u32[]{:S(2)}, u32[]{:S(2)}) collective-permute-start(bf16[8,40,1280]{2,1,0:T(8,128)(2,1)S(1)} %copy-done.11), channel_id=1, source_target_pairs={{0,2},{2,0},{1,3},{3,1},{4,6},{6,4},{5,7},{7,5},{8,10},{10,8},{9,1... | collective-permute-start | bytes 2457608 | tf_op jit(solution)/shard_map/ppermute | solution.py:53
  161.6 17.7 %collective-permute-start.30 = (bf16[8,40,1280]{2,1,0:T(8,128)(2,1)S(1)}, bf16[8,40,1280]{2,1,0:T(8,128)(2,1)}, u32[]{:S(2)}, u32[]{:S(2)}) collective-permute-start(bf16[8,40,1280]{2,1,0:T(8,128)(2,1)S(1)} %copy-done.15), channel_id=1, source_target_pairs={{0,2},{2,0},{1,3},{3,1},{4,6},{6,4},{5,7},{7,5},{8,10},{10,8},{9,1... | collective-permute-start | bytes 2457608 | tf_op jit(solution)/shard_map/ppermute | solution.py:53
  163.2 19.3 %collective-permute-start.31 = (bf16[8,40,1280]{2,1,0:T(8,128)(2,1)}, bf16[8,40,1280]{2,1,0:T(8,128)(2,1)}, u32[]{:S(2)}, u32[]{:S(2)}) collective-permute-start(bf16[8,40,1280]{2,1,0:T(8,128)(2,1)} %shard_map.311.refs_2_), channel_id=1, source_target_pairs={{0,2},{2,0},{1,3},{3,1},{4,6},{6,4},{5,7},{7,5},{8,10},{10,8},{9,1... | collective-permute-start | bytes 2457608 | tf_op jit(solution)/shard_map/ppermute | solution.py:53
  164.6 17.9 %collective-permute-start.33 = (bf16[4,40,1280]{2,1,0:T(8,128)(2,1)}, bf16[4,40,1280]{2,1,0:T(8,128)(2,1)}, u32[]{:S(2)}, u32[]{:S(2)}) collective-permute-start(bf16[4,40,1280]{2,1,0:T(8,128)(2,1)} %copy-done.55), channel_id=1, source_target_pairs={{0,2},{2,0},{1,3},{3,1},{4,6},{6,4},{5,7},{7,5},{8,10},{10,8},{9,1... | collective-permute-start | bytes 1228808 | tf_op jit(solution)/shard_map/ppermute | solution.py:53
  164.7 17.9 %collective-permute-start.32 = (bf16[4,40,1280]{2,1,0:T(8,128)(2,1)}, bf16[4,40,1280]{2,1,0:T(8,128)(2,1)}, u32[]{:S(2)}, u32[]{:S(2)}) collective-permute-start(bf16[4,40,1280]{2,1,0:T(8,128)(2,1)} %shard_map.312.refs_3_), channel_id=1, source_target_pairs={{0,2},{2,0},{1,3},{3,1},{4,6},{6,4},{5,7},{7,5},{8,10},{10,8},{9,1... | collective-permute-start | bytes 1228808 | tf_op jit(solution)/shard_map/ppermute | solution.py:53
  179.3 32.1 %collective-permute-start.35 = (bf16[128,2560]{1,0:T(8,128)(2,1)S(1)}, bf16[128,2560]{1,0:T(8,128)(2,1)S(1)}, u32[]{:S(2)}, u32[]{:S(2)}) collective-permute-start(bf16[128,2560]{1,0:T(8,128)(2,1)S(1)} %copy-done.19), channel_id=1, source_target_pairs={{0,4},{4,8},{8,12},{12,0},{1,5},{5,9},{9,13},{13,1},{2,6},{6,10},{... | collective-permute-start | bytes 1966088 | tf_op jit(solution)/shard_map/ppermute | solution.py:45
  179.3 32.8 %collective-permute-start.36 = (bf16[128,2560]{1,0:T(8,128)(2,1)S(1)}, bf16[128,2560]{1,0:T(8,128)(2,1)}, u32[]{:S(2)}, u32[]{:S(2)}) collective-permute-start(bf16[128,2560]{1,0:T(8,128)(2,1)S(1)} %copy-done.19), channel_id=1, source_target_pairs={{0,12},{4,0},{8,4},{12,8},{1,13},{5,1},{9,5},{13,9},{2,14},{6,2},{... | collective-permute-start | bytes 1966088 | tf_op jit(solution)/shard_map/ppermute | solution.py:45
  182.6 29.6 %collective-permute-start.37 = (bf16[128,2560]{1,0:T(8,128)(2,1)S(1)}, bf16[128,2560]{1,0:T(8,128)(2,1)}, u32[]{:S(2)}, u32[]{:S(2)}) collective-permute-start(bf16[128,2560]{1,0:T(8,128)(2,1)S(1)} %copy-done.19), channel_id=1, source_target_pairs={{0,8},{4,12},{8,0},{12,4},{1,9},{5,13},{9,1},{13,5},{2,10},{6,14},... | collective-permute-start | bytes 1966088 | tf_op jit(solution)/shard_map/ppermute | solution.py:45
  188.1 24.1 %collective-permute-start.34 = (bf16[128,2560]{1,0:T(8,128)(2,1)S(1)}, bf16[128,2560]{1,0:T(8,128)(2,1)}, u32[]{:S(2)}, u32[]{:S(2)}) collective-permute-start(bf16[128,2560]{1,0:T(8,128)(2,1)S(1)} %convolution_convert_fusion.4.refs_1_), channel_id=1, source_target_pairs={{0,1},{1,0},{2,3},{3,2},{4,5},{5,4},{6,7},{7,6},{8,9},{9,8},{10,11... | collective-permute-start | bytes 1966088 | tf_op jit(solution)/shard_map/ppermute | solution.py:53
  217.1 102.6 %reduce-scatter.4.cloned.1.call-start = ((), (), s32[]{:S(2)}) async-start(), calls=%async_computation.8 | async-start | bytes 5898240 | tf_op jit(solution)/shard_map/reduce_scatter | solution.py:695
  279.6 121.1 %reduce-scatter.6.cloned.1.call-start = ((), (), s32[]{:S(2)}) async-start(), calls=%async_computation.9 | async-start | bytes 9830400 | tf_op jit(solution)/shard_map/reduce_scatter | solution.py:704
  319.7 15.9 %collective-permute-start.43 = (bf16[128,2560]{1,0:T(8,128)(2,1)}, bf16[128,2560]{1,0:T(8,128)(2,1)S(1)}, u32[]{:S(2)}, u32[]{:S(2)}) collective-permute-start(bf16[128,2560]{1,0:T(8,128)(2,1)} %shard_map.324), channel_id=1, source_target_pairs={{0,1},{1,0},{2,3},{3,2},{4,5},{5,4},{6,7},{7,6},{8,9},{9,8},{10,11... | collective-permute-start | bytes 1966088 | tf_op jit(solution)/shard_map/ppermute | solution.py:53
  356.6 16.5 %all-to-all-start.1 = ((bf16[8,320,128]{2,1,0:T(8,128)(2,1)}), bf16[8,320,128]{2,1,0:T(8,128)(2,1)}, u32[]{:S(2)}, u32[]{:S(2)}) async-start(bf16[8,320,128]{2,1,0:T(8,128)(2,1)} %pad_maximum_fusion.7), calls=%async_computation.2 | async-start | bytes 1310720 | tf_op jit(solution)/shard_map/all_to_all | solution.py:271
  360.8 122.8 %all-gather.14.cloned.1.call-start = ((), (), s32[]{:S(2)}) async-start(), calls=%async_computation.13 | async-start | bytes 5898240 | tf_op jit(solution)/shard_map/all_gather | solution.py:756
  363.5 17.2 %collective-permute-start.45 = (bf16[3,64,1024]{2,1,0:T(8,128)(2,1)}, bf16[3,64,1024]{2,1,0:T(8,128)(2,1)S(1)}, u32[]{:S(2)}, u32[]{:S(2)}) collective-permute-start(bf16[3,64,1024]{2,1,0:T(8,128)(2,1)} %get-tuple-element.72), channel_id=1, source_target_pairs={{0,4},{4,8},{8,12},{12,0},{1,5},{5,9},{9,13},{13,1},{2,6},{6,10},{... | collective-permute-start | bytes 1179656 | tf_op jit(solution)/shard_map/ppermute | solution.py:45
  365.3 24.0 %collective-permute-start.47 = (bf16[3,64,1024]{2,1,0:T(8,128)(2,1)}, bf16[3,64,1024]{2,1,0:T(8,128)(2,1)S(1)}, u32[]{:S(2)}, u32[]{:S(2)}) collective-permute-start(bf16[3,64,1024]{2,1,0:T(8,128)(2,1)} %get-tuple-element.74), channel_id=1, source_target_pairs={{0,8},{4,12},{8,0},{12,4},{1,9},{5,13},{9,1},{13,5},{2,10},{6,14},... | collective-permute-start | bytes 1179656 | tf_op jit(solution)/shard_map/ppermute | solution.py:45
  368.0 21.3 %collective-permute-start.46 = (bf16[3,64,1024]{2,1,0:T(8,128)(2,1)}, bf16[3,64,1024]{2,1,0:T(8,128)(2,1)S(1)}, u32[]{:S(2)}, u32[]{:S(2)}) collective-permute-start(bf16[3,64,1024]{2,1,0:T(8,128)(2,1)} %get-tuple-element.73), channel_id=1, source_target_pairs={{0,12},{4,0},{8,4},{12,8},{1,13},{5,1},{9,5},{13,9},{2,14},{6,2},{... | collective-permute-start | bytes 1179656 | tf_op jit(solution)/shard_map/ppermute | solution.py:45
  390.6 8.8 %collective-permute-start.49 = (bf16[64,1024]{1,0:T(8,128)(2,1)S(1)}, bf16[64,1024]{1,0:T(8,128)(2,1)S(1)}, u32[]{:S(2)}, u32[]{:S(2)}) collective-permute-start(bf16[64,1024]{1,0:T(8,128)(2,1)S(1)} %get-tuple-element.153), channel_id=1, source_target_pairs={{32,0},{48,16},{33,1},{49,17},{34,2},{50,18},{35,3},{51,19},{36,4}... | collective-permute-start | bytes 393224 | tf_op jit(solution)/shard_map/ppermute | solution.py:49
  391.9 7.6 %collective-permute-start.48 = (bf16[64,1024]{1,0:T(8,128)(2,1)S(1)}, bf16[64,1024]{1,0:T(8,128)(2,1)S(1)}, u32[]{:S(2)}, u32[]{:S(2)}) collective-permute-start(bf16[64,1024]{1,0:T(8,128)(2,1)S(1)} %get-tuple-element.152), channel_id=1, source_target_pairs={{16,0},{32,16},{48,32},{17,1},{33,17},{49,33},{18,2},{34,18},{50,3... | collective-permute-start | bytes 393224 | tf_op jit(solution)/shard_map/ppermute | solution.py:49
  400.7 143.2 %reduce-scatter.8.cloned.1.call-start = ((), (), s32[]{:S(2)}) async-start(), calls=%async_computation.10 | async-start | bytes 5898240 | tf_op jit(solution)/shard_map/reduce_scatter | solution.py:788
  426.6 12.9 %collective-permute-start.54 = (bf16[2,320,256]{2,1,0:T(8,128)(2,1)S(1)}, bf16[2,320,256]{2,1,0:T(8,128)(2,1)S(1)}, u32[]{:S(2)}, u32[]{:S(2)}) collective-permute-start(bf16[2,320,256]{2,1,0:T(8,128)(2,1)S(1)} %get-tuple-element.84), channel_id=1, source_target_pairs={{0,32},{16,48},{32,0},{48,16},{1,33},{17,49},{33,1},{49,17},{2,34}... | collective-permute-start | bytes 983048 | tf_op jit(solution)/shard_map/ppermute | solution.py:45
  431.0 15.3 %collective-permute-start.53 = (bf16[2,320,256]{2,1,0:T(8,128)(2,1)S(1)}, bf16[2,320,256]{2,1,0:T(8,128)(2,1)S(1)}, u32[]{:S(2)}, u32[]{:S(2)}) collective-permute-start(bf16[2,320,256]{2,1,0:T(8,128)(2,1)S(1)} %get-tuple-element.83), channel_id=1, source_target_pairs={{0,48},{16,0},{32,16},{48,32},{1,49},{17,1},{33,17},{49,33},{2,50}... | collective-permute-start | bytes 983048 | tf_op jit(solution)/shard_map/ppermute | solution.py:45
  434.0 12.2 %collective-permute-start.52 = (bf16[2,320,256]{2,1,0:T(8,128)(2,1)S(1)}, bf16[2,320,256]{2,1,0:T(8,128)(2,1)S(1)}, u32[]{:S(2)}, u32[]{:S(2)}) collective-permute-start(bf16[2,320,256]{2,1,0:T(8,128)(2,1)S(1)} %get-tuple-element.82), channel_id=1, source_target_pairs={{0,16},{16,32},{32,48},{48,0},{1,17},{17,33},{33,49},{49,1},{2,18}... | collective-permute-start | bytes 983048 | tf_op jit(solution)/shard_map/ppermute | solution.py:45
  435.1 28.4 %collective-permute-start.56 = (bf16[320,1536]{1,0:T(8,128)(2,1)}, bf16[320,1536]{1,0:T(8,128)(2,1)}, u32[]{:S(2)}, u32[]{:S(2)}) collective-permute-start(bf16[320,1536]{1,0:T(8,128)(2,1)} %dynamic-slice_bitcast_fusion), channel_id=1, source_target_pairs={{0,64},{64,0},{1,65},{65,1},{2,66},{66,2},{3,67},{67,3},{4,68},{68... | collective-permute-start | bytes 2949128 | tf_op jit(solution)/shard_map/ppermute | solution.py:53
  447.2 14.7 %collective-permute-start.55 = (bf16[320,256]{1,0:T(8,128)(2,1)}, bf16[320,256]{1,0:T(8,128)(2,1)S(1)}, u32[]{:S(2)}, u32[]{:S(2)}) collective-permute-start(bf16[320,256]{1,0:T(8,128)(2,1)} %dynamic-slice_bitcast_fusion.2), channel_id=1, source_target_pairs={{0,64},{64,0},{1,65},{65,1},{2,66},{66,2},{3,67},{67,3},{4,68},{68... | collective-permute-start | bytes 491528 | tf_op jit(solution)/shard_map/ppermute | solution.py:53
  449.8 19.6 %collective-permute-start.58 = (bf16[128,2560]{1,0:T(8,128)(2,1)}, bf16[128,2560]{1,0:T(8,128)(2,1)}, u32[]{:S(2)}, u32[]{:S(2)}) collective-permute-start(bf16[128,2560]{1,0:T(8,128)(2,1)} %copy-done.69), channel_id=1, source_target_pairs={{0,8},{4,12},{8,0},{12,4},{1,9},{5,13},{9,1},{13,5},{2,10},{6,14},... | collective-permute-start | bytes 1966088 | tf_op jit(solution)/shard_map/ppermute | solution.py:45
  452.4 29.3 %collective-permute-start.57 = (bf16[128,2560]{1,0:T(8,128)(2,1)S(1)}, bf16[128,2560]{1,0:T(8,128)(2,1)}, u32[]{:S(2)}, u32[]{:S(2)}) collective-permute-start(bf16[128,2560]{1,0:T(8,128)(2,1)S(1)} %copy-done.68), channel_id=1, source_target_pairs={{0,12},{4,0},{8,4},{12,8},{1,13},{5,1},{9,5},{13,9},{2,14},{6,2},{... | collective-permute-start | bytes 1966088 | tf_op jit(solution)/shard_map/ppermute | solution.py:45
  453.9 27.8 %collective-permute-start.51 = (bf16[128,2560]{1,0:T(8,128)(2,1)S(1)}, bf16[128,2560]{1,0:T(8,128)(2,1)}, u32[]{:S(2)}, u32[]{:S(2)}) collective-permute-start(bf16[128,2560]{1,0:T(8,128)(2,1)S(1)} %get-tuple-element.78), channel_id=1, source_target_pairs={{0,4},{4,8},{8,12},{12,0},{1,5},{5,9},{9,13},{13,1},{2,6},{6,10},{... | collective-permute-start | bytes 1966088 | tf_op jit(solution)/shard_map/ppermute | solution.py:45
  491.7 18.2 %collective-permute-start.60 = (bf16[128,2560]{1,0:T(8,128)(2,1)S(1)}, bf16[128,2560]{1,0:T(8,128)(2,1)}, u32[]{:S(2)}, u32[]{:S(2)}) collective-permute-start(bf16[128,2560]{1,0:T(8,128)(2,1)S(1)} %copy-done.9), channel_id=1, source_target_pairs={{0,1},{1,0},{2,3},{3,2},{4,5},{5,4},{6,7},{7,6},{8,9},{9,8},{10,11... | collective-permute-start | bytes 1966088 | tf_op jit(solution)/shard_map/ppermute | solution.py:53
  495.6 27.6 %all-to-all-start.2 = ((bf16[8,40,1792]{2,1,0:T(8,128)(2,1)}), bf16[8,40,1792]{2,1,0:T(8,128)(2,1)S(1)}, u32[]{:S(2)}, u32[]{:S(2)}) async-start(bf16[8,40,1792]{2,1,0:T(8,128)(2,1)} %bitcast.190), calls=%async_computation.5 | async-start | bytes 2293760 | tf_op jit(solution)/shard_map/all_to_all | solution.py:271
  511.7 12.6 %collective-permute-start.64 = (bf16[2,320,256]{2,1,0:T(8,128)(2,1)}, bf16[2,320,256]{2,1,0:T(8,128)(2,1)}, u32[]{:S(2)}, u32[]{:S(2)}) collective-permute-start(bf16[2,320,256]{2,1,0:T(8,128)(2,1)} %copy-done.70), channel_id=1, source_target_pairs={{0,32},{16,48},{32,0},{48,16},{1,33},{17,49},{33,1},{49,17},{2,34}... | collective-permute-start | bytes 983048 | tf_op jit(solution)/shard_map/ppermute | solution.py:45
  515.3 14.5 %collective-permute-start.63 = (bf16[2,320,256]{2,1,0:T(8,128)(2,1)S(1)}, bf16[2,320,256]{2,1,0:T(8,128)(2,1)}, u32[]{:S(2)}, u32[]{:S(2)}) collective-permute-start(bf16[2,320,256]{2,1,0:T(8,128)(2,1)S(1)} %get-tuple-element.95), channel_id=1, source_target_pairs={{0,48},{16,0},{32,16},{48,32},{1,49},{17,1},{33,17},{49,33},{2,50}... | collective-permute-start | bytes 983048 | tf_op jit(solution)/shard_map/ppermute | solution.py:45
  515.9 14.0 %collective-permute-start.62 = (bf16[2,320,256]{2,1,0:T(8,128)(2,1)S(1)}, bf16[2,320,256]{2,1,0:T(8,128)(2,1)}, u32[]{:S(2)}, u32[]{:S(2)}) collective-permute-start(bf16[2,320,256]{2,1,0:T(8,128)(2,1)S(1)} %get-tuple-element.94), channel_id=1, source_target_pairs={{0,16},{16,32},{32,48},{48,0},{1,17},{17,33},{33,49},{49,1},{2,18}... | collective-permute-start | bytes 983048 | tf_op jit(solution)/shard_map/ppermute | solution.py:45
  523.3 31.8 %collective-permute-start.61 = (bf16[8,40,256]{2,1,0:T(8,128)(2,1)S(1)}, bf16[8,40,256]{2,1,0:T(8,128)(2,1)S(1)}, u32[]{:S(2)}, u32[]{:S(2)}) collective-permute-start(bf16[8,40,256]{2,1,0:T(8,128)(2,1)S(1)} %slice.194.refs_0_), channel_id=1, source_target_pairs={{0,1},{1,0},{2,3},{3,2},{4,5},{5,4},{6,7},{7,6},{8,9},{9,8},{10,11... | collective-permute-start | bytes 491528 | tf_op jit(solution)/shard_map/ppermute | solution.py:53
  532.7 23.5 %collective-permute-start.65 = (bf16[320,256]{1,0:T(8,128)(2,1)}, bf16[320,256]{1,0:T(8,128)(2,1)S(1)}, u32[]{:S(2)}, u32[]{:S(2)}) collective-permute-start(bf16[320,256]{1,0:T(8,128)(2,1)} %dynamic-slice_bitcast_fusion.1), channel_id=1, source_target_pairs={{0,64},{64,0},{1,65},{65,1},{2,66},{66,2},{3,67},{67,3},{4,68},{68... | collective-permute-start | bytes 491528 | tf_op jit(solution)/shard_map/ppermute | solution.py:53
  544.0 23.8 %collective-permute-start.59 = (bf16[128,2560]{1,0:T(8,128)(2,1)}, bf16[128,2560]{1,0:T(8,128)(2,1)}, u32[]{:S(2)}, u32[]{:S(2)}) collective-permute-start(bf16[128,2560]{1,0:T(8,128)(2,1)} %bitcast.195), channel_id=1, source_target_pairs={{0,1},{1,0},{2,3},{3,2},{4,5},{5,4},{6,7},{7,6},{8,9},{9,8},{10,11... | collective-permute-start | bytes 1966088 | tf_op jit(solution)/shard_map/ppermute | solution.py:53
  556.9 9.8 %all-to-all-start.3 = ((bf16[8,40,256]{2,1,0:T(8,128)(2,1)}), bf16[8,40,256]{2,1,0:T(8,128)(2,1)S(1)}, u32[]{:S(2)}, u32[]{:S(2)}) async-start(bf16[8,40,256]{2,1,0:T(8,128)(2,1)} %bitcast.78), calls=%async_computation.6 | async-start | bytes 327680 | tf_op jit(solution)/shard_map/all_to_all | solution.py:271
  (132 other events, 923.8 us)
Sparse Core Ops, SparseCore 0:
  22.6 37.7 all-gather.9
  109.7 80.7 all-gather.7
  217.2 38.2 all-gather.11
  279.7 39.9 reduce-scatter.3
  321.9 76.3 reduce-scatter.5
  400.9 38.7 all-gather.13
  490.7 53.1 reduce-scatter.7

commit v3 on v2

--- a/solution.py
+++ b/solution.py
@@ -479,51 +479,64 @@
     theirs_ref[0] = held[index_ref[C_AT + 1]]
 
 
-def chunk_grad(part):
-    def body(index_ref, rows_ref, cols_ref, extra_ref, *refs):
-        *out_refs, total, held = refs[-6:]
-        step = pl.program_id(0)
-
-        @pl.when(step == 0)
-        def _():
-            total[...] = jnp.zeros(total.shape, F32)
-            total[part : part + 8] = extra_ref[...]
-
+def chunk_grads(index_ref, rows_ref, cols_ref, extra_ref, rows2_ref, cols2_ref, after_ref, *refs):
+    del after_ref
+    *out_refs, total, held = refs
+    step, part, part2 = pl.program_id(0), cols_ref.shape[0], cols2_ref.shape[0]
+
+    @pl.when(step == 0)
+    def _():
+        total[...] = jnp.zeros(total.shape, F32)
+        total[part : part + 8] = extra_ref[...]
+
+    @pl.when(step < 4)
+    def _():
         total[:part] += dot(cols_ref[...], rows_ref[...].reshape(2 * ROWS, D), 1, 0)
 
-        @pl.when(step == 3)
-        def _():
-            block, whole = GROUP * OWNED, total[...].T
-            for k in range(8):
-                held[k % 4, k // 4] = whole[k * block : (k + 1) * block].astype(BF)
-            for k, out in enumerate(out_refs):
-                out[...] = held[index_ref[Y_AT + (0, 2, 1, 3)[k]]]
-
-    return body
-
-
-def grad_by_chunk(rows, cols, extra, index, after=()):
-    part = cols.shape[0]
-    shape = (2, GROUP * OWNED, 256)
+    @pl.when(step >= 4)
+    def _():
+        rows = rows2_ref[...].reshape(2 * ROWS, D)
+        total[256 : 256 + part2] += dot(cols2_ref[...], rows, 1, 0)
+
+    @pl.when(step == 7)
+    def _():
+        block, whole = GROUP * OWNED, total[...].T
+        for k in range(8):
+            held[k % 4, k // 4] = whole[k * block : (k + 1) * block].astype(BF)
+        for k, out in enumerate(out_refs):
+            out[...] = held[index_ref[Y_AT + (0, 2, 1, 3)[k]]]
+
+
+def grads_by_chunk(rows, cols, extra, rows2, cols2, index, after):
+    shape = (2, GROUP * OWNED, 512)
+
+    def first(k):
+        return jnp.minimum(k, 3)
+
+    def second(k):
+        return jnp.maximum(k - 4, 0)
+
     return pl.pallas_call(
-        chunk_grad(part),
-        grid=(4,),
+        chunk_grads,
+        grid=(8,),
         out_shape=(jax.ShapeDtypeStruct(shape, BF),) * 4,
         in_specs=[
             SMEM,
-            pl.BlockSpec((2, ROWS, D), lambda k: (k, 0, 0)),
-            pl.BlockSpec((part, 2 * ROWS), lambda k: (0, k)),
+            pl.BlockSpec((2, ROWS, D), lambda k: (first(k), 0, 0)),
+            pl.BlockSpec((cols.shape[0], 2 * ROWS), lambda k: (0, first(k))),
             pl.BlockSpec((8, D), lambda k: (0, 0)),
-        ]
-        + [ANY] * len(after),
+            pl.BlockSpec((2, ROWS, D), lambda k: (second(k), 0, 0)),
+            pl.BlockSpec((cols2.shape[0], 2 * ROWS), lambda k: (0, second(k))),
+            ANY,
+        ],
         out_specs=(pl.BlockSpec(shape, lambda k: (0, 0, 0)),) * 4,
         scratch_shapes=[
-            pltpu.VMEM((256, D), F32),
-            pltpu.VMEM((4, 2, GROUP * OWNED, 256), BF),
+            pltpu.VMEM((512, D), F32),
+            pltpu.VMEM((4, 2, GROUP * OWNED, 512), BF),
         ],
         cost_estimate=SMALL,
-        compiler_params=params(32),
-    )(index, rows, cols, extra, *after)
+        compiler_params=params(40),
+    )(index, rows, cols, extra, rows2, cols2, after)
 
 
 def row_scatter(parts, b):
@@ -637,16 +650,16 @@
     keys = rotate(raw[Q_PART : Q_PART + 2 * PART].reshape(2, PART, 1024), *group_turn)
     values = raw[Q_PART + 2 * PART : Q_PART + KV_PART].reshape(2, PART, 1024)
     pair = jnp.concatenate([keys, values]).astype(BF).reshape(KV_PART, 1024)
+    pair = tie(pair, rows_left, rows_right)
+    rows_top, rows_bottom = shift(rows_left[:4], "x", 1), shift(rows_right[4:], "x", 3)
     pair_back = [push(pair, "y", 1), push(pair, "y", 2)]
     q_raw = raw[:Q_PART].astype(BF).reshape(Q_PART, GROUP, ROWS).transpose(1, 0, 2)
     q_raw = exchange(q_raw)
     feed_partner = tie(feed_partner, *pair_back)
-    pair_back[0] = tie(pair_back[0], q_raw, rows_left, rows_right)
-    rows_left, rows_right = tie(rows_left, q_raw), tie(rows_right, q_raw)
-    rows_top, rows_bottom = shift(rows_left[:4], "x", 1), shift(rows_right[4:], "x", 3)
     q_raw = q_raw.astype(F32).reshape(LOCAL_HEADS, 2, HEAD_DIM // 2, ROWS)
     queries = rotate(q_raw, *own_turn).astype(BF).reshape(LOCAL_HEADS, HEAD_DIM, ROWS)
     spans = direct(jnp.stack([pair] + pair_back), "x")
+    spans[1:] = [tie(span, q_raw, rows_top, rows_bottom) for span in spans[1:]]
     feed_pair = both_in_order(feed, feed_partner, b)
     w_feed = lax.all_gather(feed_pair, "y", axis=1, tiled=True).reshape(D, 3 * F_PAD)
     back_pieces = direct(tie(cotangent, *spans[1:]), "x")
@@ -678,7 +691,7 @@
     normed_b = tie((residual * rate_b * gains[1]).astype(BF), w_feed)
     group_b = lax.all_gather(normed_b, ("x", "c"), axis=0).reshape(1024, D)
     group_back = group_place(back_pieces, index).reshape(1024, D)
-    d_hidden = dot(group_back, w_feed[:, 2 * F_PAD :], 1, 0)
+    d_hidden = tie(dot(group_back, w_feed[:, 2 * F_PAD :], 1, 0), normed_b)
     gate_up = dot(group_b, w_feed[:, : 2 * F_PAD], 1, 0)
     gate, up = gate_up[:, :F_PAD], gate_up[:, F_PAD:]
     root = math.sqrt(2.0 / math.pi)
@@ -737,9 +750,9 @@
         .reshape(GROUP, Q_PART, ROWS)
     )
     moved = jnp.concatenate([query_grad, attended.reshape(GROUP, Q_PART, ROWS)], axis=1)
-    moved = exchange(moved).transpose(1, 0, 2).reshape(2 * Q_PART, 1024)
+    back_terms = scatter_terms(span_mine, span_theirs, "c", "x", index)
+    moved = exchange(tie(moved, back_terms[0])).transpose(1, 0, 2).reshape(2 * Q_PART, 1024)
     query_grad, group_attended = moved[:Q_PART], moved[Q_PART:]
-    back_terms = scatter_terms(span_mine, span_theirs, "c", "x", index)
     back_terms[1] = tie(back_terms[1], moved)
     back = total_of(back_terms)
     back = (
@@ -775,19 +788,15 @@
     rate_a = rms_rate(inflow)
     norma_terms = scatter_terms(norma_mine, norma_theirs, "c", "x", index)
     extra = jnp.concatenate([gain_a[:1], 0.5 * gain_b[None], jnp.zeros((6, D), F32)])
-    small_parts = grad_by_chunk(normed_a, sent, extra, index, (norma_terms[0],))
-    small_grad = row_scatter(small_parts, b)
-    norma_terms[1:] = [tie(term, small_grad, feed_grad) for term in norma_terms[1:]]
-    late = jnp.concatenate([feed_grad, small_grad], axis=1)
-    late = exchange(late.reshape(GROUP, OWNED, 3 * F_PAD + 256))
-    feed_grad, small_grad = late, late[:, :, 3 * F_PAD :]
+    parts = grads_by_chunk(
+        normed_a, sent, extra, group_resid, group_attended, index, norma_terms[0]
+    )
+    norma_terms[1:] = [tie(term, parts[0]) for term in norma_terms[1:]]
     norma_low = low_bits(total_of(norma_terms))
-    output_parts = grad_by_chunk(
-        group_resid, group_attended, jnp.zeros((8, D), F32), index, (norma_low,)
-    )
-    out_low = lax.psum_scatter(
-        tie(feed_part, norma_low, output_parts[0]), ("x", "c"), scatter_dimension=0
-    )
+    out_low = lax.psum_scatter(tie(feed_part, parts[0]), ("x", "c"), scatter_dimension=0)
+    late = jnp.concatenate([feed_grad, row_scatter(parts, b)], axis=1)
+    late = exchange(late.reshape(GROUP, OWNED, 3 * F_PAD + 512))
+    small_grad = late[:, :, 3 * F_PAD : 3 * F_PAD + 256]
     other_out = swap(out_low, "t")
     out_tokens = (residual + (out_low.astype(F32) + other_out.astype(F32))).astype(BF)
     grad_norma = tensor_sum(norma_low)
@@ -798,7 +807,6 @@
         - inflow * rate_a**3 * jnp.mean(scaled * inflow, axis=-1, keepdims=True)
     )
 
-    output_grad = exchange(row_scatter(output_parts, b).reshape(GROUP, OWNED, 256))
 
     def update(grads, weight, moment, second, part, start, rate, pair=False):
         return pl.pallas_call(
@@ -810,8 +818,10 @@
             compiler_params=params(32),
         )(*grads, weight, moment, second)
 
-    other_grad = swap(small_grad, "t")
-    query_new = update([small_grad], query_weight, query_moment, query_second, Q_PART, 0, wide_rate)
+    other_grad = swap(tie(small_grad, other_out), "t")
+    query_new = update(
+        [late], query_weight, query_moment, query_second, Q_PART, 3 * F_PAD, wide_rate
+    )
     pair_new = update(
         [small_grad, other_grad],
         keyvalue_weight,
@@ -823,7 +833,7 @@
         True,
     )
     output_new = update(
-        [output_grad], output_weight, output_moment, output_second, Q_PART, 0, output_rate
+        [late], output_weight, output_moment, output_second, Q_PART, 3 * F_PAD + 256, output_rate
     )
     matrix = pl.BlockSpec((1, OWNED, 8 * F_PART), lambda k: (k, 0, 0))
     feed_new = pl.pallas_call(
@@ -834,7 +844,7 @@
         out_specs=(matrix,) * 3,
         cost_estimate=SMALL,
         compiler_params=params(32),
-    )(feed_grad, feedforward_weight, feedforward_moment, feedforward_second)
+    )(late, feedforward_weight, feedforward_moment, feedforward_second)
     gain_grad = small_grad.astype(F32) + other_grad.astype(F32)
     gain_grad = jnp.sum(gain_grad[:, :, Q_PART + KV_PART : Q_PART + KV_PART + 2], axis=0).T
     gains_new = adam(norm_gains, gain_grad, gains_moment, gains_second, 0.3, 0.0)

time: 589 us -> 568 us (0.964)
  blocking collectives: 13.6 us -> 0 us
  local copies, waits for them, and re-layouts: 67.3 us -> 59.2 us
  waiting for transfers between devices: 225 us -> 219 us
    all_gather x1, waiting for transfers between devices: 0.02 us -> 20.7 us  [local(): group_resid = lax.all_gather(tie(resid_low, feed_grad), ('x', 'c'), axis=0)]
    all_to_all x1 -> x0, blocking collectives: 13.6 us -> none  [exchange(): lax.all_to_all(value, ('x', 'c'), split_axis=0, concat_axis=0, tiled=True)]
    reduce_scatter x1, waiting for transfers between devices: 10.8 us -> 0.02 us  [local(): lax.psum_scatter(tie(feed_part, parts[0]), ('x', 'c'), scatter_dimension=0)]
    ppermute x34 -> x31, waiting for transfers between devices: 107 us -> 96.7 us  [shift(): return lax.ppermute(value, axis, [(i, (i + step) % 4) for i in range(4)])]
    all_to_all x3, waiting for transfers between devices: 15 us -> 24.4 us  [exchange(): lax.all_to_all(value, ('x', 'c'), split_axis=0, concat_axis=0, tiled=True)]
    ppermute x28 -> x27, waiting for transfers between devices: 45.9 us -> 38.9 us  [swap(): return lax.ppermute(value, axis, [(0, 1), (1, 0)])]
    all_gather x1, waiting for transfers between devices: 27.8 us -> 20.9 us  [local(): group_b = lax.all_gather(normed_b, ('x', 'c'), axis=0).reshape(1024, D)]
    unnamed x244 -> x195, local copies, waits for them, and re-layouts: 54.2 us -> 49.1 us
  transfers between devices with their start and end apart: 76 -> 72, of which waited for: 41 -> 38; matrix products, arithmetic and copies ran while one was open for 15% -> 17% of each run, Pallas kernels for 9% -> 8%
where the time goes in v3:
time: 568 us; the launch traced here: 557 us
  waiting for transfers between devices  219 us (39%)
  starting transfers between devices  102 us (18%)
  local copies, waits for them, and re-layouts  59.2 us (10%)
  Pallas kernels  57.6 us (10%)
  matrix products  55.3 us (10%)
  other arithmetic  48.3 us (9%)
  between operations  15.8 us (3%)
    ppermute x31, waiting for transfers between devices, shift(): return lax.ppermute(value, axis, [(i, (i + step) % 4) for i in range(4)])  96.7 us
    dot_general x8, matrix products, dot(): lax.dot_general(left, right, (((left_dim,), (right_dim,)), ((), ())), pre...  55.3 us
    ppermute x31, starting transfers between devices, shift(): return lax.ppermute(value, axis, [(i, (i + step) % 4) for i in range(4)])  51.1 us
    unnamed x195, local copies, waits for them, and re-layouts  49.1 us
    ppermute x27, waiting for transfers between devices, swap(): return lax.ppermute(value, axis, [(0, 1), (1, 0)])  38.9 us
    ppermute x27, starting transfers between devices, swap(): return lax.ppermute(value, axis, [(0, 1), (1, 0)])  28.9 us
    all_to_all x3, waiting for transfers between devices, exchange(): lax.all_to_all(value, ('x', 'c'), split_axis=0, concat_axis=0, tiled=True)  24.4 us
    all_gather x1, waiting for transfers between devices, local(): group_b = lax.all_gather(normed_b, ('x', 'c'), axis=0).reshape(1024, D)  20.9 us
  transfers between devices with their start and end apart: 72, of which 38 were waited for; matrix products, arithmetic and copies ran while one was open for 17% of the time, Pallas kernels for 8%

profile of v3, /device:TPU:0, one launch (start us, length us, event | category | flops | bytes accessed | tf_op | source)
XLA Modules:
  0.0 557.5 jit_solution(13221146225797307304)
XLA Ops:
  25.3 3.3 collective-permute-done.4.after_ref
  36.0 3.6 collective-permute-done.5.refs_1_
  39.6 4.0 collective-permute-done.6.refs_2_
  50.5 3.1 collective-permute-done.9
  69.9 2.5 collective-permute-start.14
  73.0 3.6 collective-permute-done.13.refs_1_
  81.8 3.1 collective-permute-start.38
  84.8 3.2 collective-permute-start.17
  88.2 2.5 copy-done
  92.0 4.3 shard_map.306
  102.3 4.5 collective-permute-start.18
  106.8 2.8 collective-permute-done.18.refs_1_
  115.4 2.8 collective-permute-start.22
  120.1 3.2 collective-permute-start.23
  124.1 4.1 all-to-all-start
  128.2 3.6 collective-permute-start.24
  131.8 5.1 all-to-all-done
  141.7 3.1 collective-permute-done.24.refs_0_
  155.2 6.2 %shard_map.312 = (f32[17,128,640]{2,1,0:T(8,128)S(1)}, bf16[5,256,128]{2,1,0:T(8,128)(2,1)S(1)}) custom-call(s32[2]{0:T(128)S(1)} %pad_add_fusion.base_ref, s32[12]{0:T(128)S(1)} %stack.145.index_ref, bf16[5,256,128]{2,1,0:T(8,128)(2,1)S(1)} %bitcast.156, bf16[3,64,1024]{2,1,0:T(8,128)(2,1)} %pad_maximum_fusion.9.refs_0_, ...), custom_call_target="tpu_custom_call" | custom-call | flops 1 | bytes 1 | tf_op jit(solution)/shard_map/pallas_call | solution.py:672
  162.2 2.6 collective-permute-start.36
  164.8 2.6 shard_map.314
  167.5 3.1 convolution_convert_fusion.4.refs_1_
  170.6 4.0 collective-permute-start.34
  176.2 18.0 %collective-permute-done.35.refs_0_ = bf16[128,2560]{1,0:T(8,128)(2,1)} collective-permute-done((bf16[128,2560]{1,0:T(8,128)(2,1)}, bf16[128,2560]{1,0:T(8,128)(2,1)}, u32[]{:S(2)}, u32[]{:S(2)}) %collective-permute-start.35) | collective-permute-done | bytes 655392 | tf_op jit(solution)/shard_map/ppermute | solution.py:45
  204.3 3.4 shard_map.322
  210.0 6.1 %fusion.3.refs_0_ = f32[1024,512]{1,0:T(8,128)} fusion(bf16[1024,2560]{1,0:T(8,128)(2,1)S(1)} %bitcast.152, bf16[2560,1536]{1,0:T(8,128)(2,1)} %bitcast.175), kind=kOutput, calls=%fused_computation.12 | convolution fusion | flops 2684354560 | bytes 9961472 | tf_op jit(solution)/shard_map/dot_general | solution.py:39
  216.2 20.9 %all-gather.12.cloned.1.call-done.refs_0_ = bf16[1024,2560]{1,0:T(8,128)(2,1)} async-done(((bf16[128,2560]{1,0:T(8,128)(2,1)}), bf16[1024,2560]{1,0:T(8,128)(2,1)}) %all-gather.12.cloned.1.call-update) | async-done | bytes 5242896 | tf_op jit(solution)/shard_map/all_gather | solution.py:692
  237.1 9.2 %fusion.1 = f32[1024,1024]{1,0:T(8,128)S(1)} fusion(bf16[1024,2560]{1,0:T(8,128)(2,1)} %all-gather.12.cloned.1.call-done.refs_0_, bf16[2560,1536]{1,0:T(8,128)(2,1)} %bitcast.176), kind=kOutput, calls=%fused_computation.5 | convolution fusion | flops 5368709120 | bytes 14680064 | tf_op jit(solution)/shard_map/dot_general | solution.py:39
  248.1 10.5 %convolution_convert_fusion.2.refs_1_ = bf16[1024,2560]{1,0:T(8,128)(2,1)} fusion(bf16[2560,1536]{1,0:T(8,128)(2,1)} %bitcast.177, bf16[1024,512]{1,0:T(8,128)(2,1)S(1)} %get-tuple-element.128, bf16[1024,512]{1,0:T(8,128)(2,1)S(1)} %get-tuple-element.127), kind=kOutput, calls=%fused_computation.3 | convolution fusion | flops 5375524864 | bytes 12582912 | tf_op jit(solution)/shard_map/dot_general | solution.py:39
  258.9 7.0 %convolution_convert_fusion.3.refs_1_ = bf16[2560,512]{1,0:T(8,128)(2,1)} fusion(bf16[1024,2560]{1,0:T(8,128)(2,1)} %shard_map.324, bf16[1024,512]{1,0:T(8,128)(2,1)S(1)} %get-tuple-element.129), kind=kOutput, calls=%fused_computation.7 | convolution fusion | flops 2685665280 | bytes 8912896 | tf_op jit(solution)/shard_map/dot_general | solution.py:39
  265.9 7.8 %convolution_convert_fusion.1.refs_2_ = bf16[2560,1024]{1,0:T(8,128)(2,1)} fusion(bf16[1024,2560]{1,0:T(8,128)(2,1)S(1)} %copy-done.72, bf16[1024,512]{1,0:T(8,128)(2,1)S(1)} %copy-done.82, bf16[1024,512]{1,0:T(8,128)(2,1)S(1)} %copy-done.80), kind=kOutput, calls=%fused_computation.2 | convolution fusion | flops 5375524864 | bytes 12582912 | tf_op jit(solution)/shard_map/dot_general | solution.py:39
  273.7 7.3 %pad_maximum_fusion = bf16[2560,1536]{1,0:T(8,128)(2,1)} fusion(bf16[2560,512]{1,0:T(8,128)(2,1)} %convolution_convert_fusion.3.refs_1_, bf16[2560,1024]{1,0:T(8,128)(2,1)} %convolution_convert_fusion.1.refs_2_), kind=kLoop, calls=%fused_computation | loop fusion | flops 15728640 | bytes 15728640 | tf_op jit(solution)/shard_map/concatenate | solution.py:716
  281.0 6.4 %convolution_convert_fusion = bf16[1024,2560]{1,0:T(8,128)(2,1)} fusion(bf16[1024,512]{1,0:T(8,128)(2,1)S(1)} %get-tuple-element.129, bf16[2560,1536]{1,0:T(8,128)(2,1)} %bitcast.178), kind=kOutput, calls=%fused_computation.1 | convolution fusion | flops 2686976000 | bytes 8912896 | tf_op jit(solution)/shard_map/dot_general | solution.py:39
  287.4 11.3 %reduce-scatter.4.cloned.1.call-done = bf16[1,128,2560]{2,1,0:T(8,128)(2,1)} async-done(((bf16[8,128,2560]{2,1,0:T(8,128)(2,1)}), bf16[1,128,2560]{2,1,0:T(8,128)(2,1)}) %reduce-scatter.4.cloned.1.call-update) | async-done | bytes 655376 | tf_op jit(solution)/shard_map/reduce_scatter | solution.py:708
  298.7 3.3 collective-permute-start.43
  302.1 12.4 %collective-permute-done.43 = bf16[128,2560]{1,0:T(8,128)(2,1)S(1)} collective-permute-done((bf16[128,2560]{1,0:T(8,128)(2,1)}, bf16[128,2560]{1,0:T(8,128)(2,1)S(1)}, u32[]{:S(2)}, u32[]{:S(2)}) %collective-permute-start.43) | collective-permute-done | bytes 655392 | tf_op jit(solution)/shard_map/ppermute | solution.py:53
  314.5 2.6 multiply_reduce_fusion
  318.8 5.1 convolution_convert_fusion.5
  324.0 9.9 %shard_map.327 = (f32[5,256,128]{2,1,0:T(8,128)S(1)}, bf16[4,3,64,1024]{3,2,1,0:T(8,128)(2,1)S(1)}, bf16[4,3,64,1024]{3,2,1,0:T(8,128)(2,1)S(1)}) custom-call(s32[2]{0:T(128)S(1)} %pad_add_fusion.base_ref, s32[12]{0:T(128)S(1)} %stack.145.index_ref, bf16[5,256,128]{2,1,0:T(8,128)(2,1)S(1)} %bitcast.157, f32[17,128,640]{2,1,0:T(8,128)} %copy-done.23, ...), custom_call_target="tpu_custom_call" | custom-call | flops 1 | bytes 1 | tf_op jit(solution)/shard_map/pallas_call | solution.py:729
  339.9 4.3 all-to-all-start.1
  346.2 2.7 collective-permute-start.47
  350.3 6.2 %all-to-all-done.1 = bf16[8,320,128]{2,1,0:T(8,128)(2,1)} async-done(((bf16[8,320,128]{2,1,0:T(8,128)(2,1)}), bf16[8,320,128]{2,1,0:T(8,128)(2,1)}, u32[]{:S(2)}, u32[]{:S(2)}) %all-to-all-start.1) | async-done | bytes 655392 | tf_op jit(solution)/shard_map/all_to_all | solution.py:271
  358.6 5.8 %collective-permute-done.45.refs_0_ = bf16[3,64,1024]{2,1,0:T(8,128)(2,1)} collective-permute-done((bf16[3,64,1024]{2,1,0:T(8,128)(2,1)}, bf16[3,64,1024]{2,1,0:T(8,128)(2,1)}, u32[]{:S(2)}, u32[]{:S(2)}) %collective-permute-start.45) | collective-permute-done | bytes 393248 | tf_op jit(solution)/shard_map/ppermute | solution.py:45
  364.3 8.6 %collective-permute-done.47 = bf16[3,64,1024]{2,1,0:T(8,128)(2,1)} collective-permute-done((bf16[3,64,1024]{2,1,0:T(8,128)(2,1)S(1)}, bf16[3,64,1024]{2,1,0:T(8,128)(2,1)}, u32[]{:S(2)}, u32[]{:S(2)}) %collective-permute-start.47) | collective-permute-done | bytes 393248 | tf_op jit(solution)/shard_map/ppermute | solution.py:45
  379.3 3.7 collective-permute-done.49
  385.5 2.5 copy-done.1
  389.0 4.2 shard_map.331
  393.6 4.6 collective-permute-done.50.received_ref
  401.2 20.7 %all-gather.14.cloned.1.call-done = bf16[1024,2560]{1,0:T(8,128)(2,1)} async-done(((bf16[128,2560]{1,0:T(8,128)(2,1)}), bf16[1024,2560]{1,0:T(8,128)(2,1)}) %all-gather.14.cloned.1.call-update) | async-done | bytes 5242896 | tf_op jit(solution)/shard_map/all_gather | solution.py:769
  421.9 2.5 copy-done.25
  425.7 9.3 %shard_map.335 = (bf16[2,320,512]{2,1,0:T(8,128)(2,1)S(1)}, bf16[2,320,512]{2,1,0:T(8,128)(2,1)S(1)}, bf16[2,320,512]{2,1,0:T(8,128)(2,1)}, bf16[2,320,512]{2,1,0:T(8,128)(2,1)}) custom-call(s32[12]{0:T(128)S(1)} %stack.145.index_ref, bf16[8,128,2560]{2,1,0:T(8,128)(2,1)S(1)} %copy-done.25, bf16[224,1024]{1,0:T(8,128)(2,1)S(1)} %copy-done.15, ...), custom_call_target="tpu_custom_call" | custom-call | flops 1 | bytes 1 | tf_op jit(solution)/shard_map/pallas_call | solution.py:519
  444.3 3.0 collective-permute-start.59
  447.4 12.0 %collective-permute-done.54.refs_0_ = bf16[128,2560]{1,0:T(8,128)(2,1)S(1)} collective-permute-done((bf16[128,2560]{1,0:T(8,128)(2,1)S(1)}, bf16[128,2560]{1,0:T(8,128)(2,1)S(1)}, u32[]{:S(2)}, u32[]{:S(2)}) %collective-permute-start.54) | collective-permute-done | bytes 655392 | tf_op jit(solution)/shard_map/ppermute | solution.py:45
  459.4 2.7 collective-permute-start.58
  462.1 15.6 %collective-permute-done.53.refs_0_ = bf16[128,2560]{1,0:T(8,128)(2,1)} collective-permute-done((bf16[128,2560]{1,0:T(8,128)(2,1)}, bf16[128,2560]{1,0:T(8,128)(2,1)}, u32[]{:S(2)}, u32[]{:S(2)}) %collective-permute-start.53) | collective-permute-done | bytes 655392 | tf_op jit(solution)/shard_map/ppermute | solution.py:45
  481.1 3.2 collective-permute-start.55
  484.3 10.3 %collective-permute-done.57 = bf16[2,320,512]{2,1,0:T(8,128)(2,1)} collective-permute-done((bf16[2,320,512]{2,1,0:T(8,128)(2,1)}, bf16[2,320,512]{2,1,0:T(8,128)(2,1)}, u32[]{:S(2)}, u32[]{:S(2)}) %collective-permute-start.57) | collective-permute-done | bytes 655392 | tf_op jit(solution)/shard_map/ppermute | solution.py:45
  500.5 4.6 collective-permute-done.60
  506.4 4.3 all-to-all-start.2
  513.0 3.5 fusion.16
  516.5 13.1 %all-to-all-done.2.refs_0_ = bf16[8,40,2048]{2,1,0:T(8,128)(2,1)S(1)} async-done(((bf16[8,40,2048]{2,1,0:T(8,128)(2,1)}), bf16[8,40,2048]{2,1,0:T(8,128)(2,1)S(1)}, u32[]{:S(2)}, u32[]{:S(2)}) %all-to-all-start.2) | async-done | bytes 1310752 | tf_op jit(solution)/shard_map/all_to_all | solution.py:271
  536.5 3.6 shard_map.344
  543.0 2.7 add_convert_fusion.2
  545.7 2.7 collective-permute-done.61.refs_1_
  (409 shorter events, 163.0 us)
Async XLA Ops:
  7.2 60.6 %all-gather.10.cloned.1.call-start = ((), (), s32[]{:S(2)}) async-start(), calls=%async_computation.10 | async-start | bytes 5898240 | tf_op jit(solution)/shard_map/all_gather | solution.py:599
  12.1 7.2 %collective-permute-start.1 = (bf16[2,40,256]{2,1,0:T(8,128)(2,1)S(1)}, bf16[2,40,256]{2,1,0:T(8,128)(2,1)S(1)}, u32[]{:S(2)}, u32[]{:S(2)}) collective-permute-start(bf16[2,40,256]{2,1,0:T(8,128)(2,1)S(1)} %get-tuple-element.150), channel_id=1, source_target_pairs={{0,4},{4,8},{8,12},{12,0},{1,5},{5,9},{9,13},{13,1},{2,6},{6,10},{... | collective-permute-start | bytes 122888 | tf_op jit(solution)/shard_map/ppermute | solution.py:45
  13.7 5.5 collective-permute-start.2
  15.4 5.5 collective-permute-start.3
  22.5 176.6 %all-gather.8.cloned.1.call-start = ((), (), s32[]{:S(2)}) async-start(), calls=%async_computation.6 | async-start | bytes 9830400 | tf_op jit(solution)/shard_map/all_gather | solution.py:664
  23.3 5.3 collective-permute-start.4
  28.7 10.9 %collective-permute-start.5 = (bf16[2,320,256]{2,1,0:T(8,128)(2,1)S(1)}, bf16[2,320,256]{2,1,0:T(8,128)(2,1)S(1)}, u32[]{:S(2)}, u32[]{:S(2)}) collective-permute-start(bf16[2,320,256]{2,1,0:T(8,128)(2,1)S(1)} %pad_maximum_fusion.10.refs_0_), channel_id=1, source_target_pairs={{0,16},{16,32},{32,48},{48,0},{1,17},{17,33},{33,49},{49,1},{2,18}... | collective-permute-start | bytes 983048 | tf_op jit(solution)/shard_map/ppermute | solution.py:45
  30.4 13.2 %collective-permute-start.6 = (bf16[2,320,256]{2,1,0:T(8,128)(2,1)S(1)}, bf16[2,320,256]{2,1,0:T(8,128)(2,1)S(1)}, u32[]{:S(2)}, u32[]{:S(2)}) collective-permute-start(bf16[2,320,256]{2,1,0:T(8,128)(2,1)S(1)} %pad_maximum_fusion.10.refs_0_), channel_id=1, source_target_pairs={{0,48},{16,0},{32,16},{48,32},{1,49},{17,1},{33,17},{49,33},{2,50}... | collective-permute-start | bytes 983048 | tf_op jit(solution)/shard_map/ppermute | solution.py:45
  32.0 13.4 %collective-permute-start.7 = (bf16[2,320,256]{2,1,0:T(8,128)(2,1)S(1)}, bf16[2,320,256]{2,1,0:T(8,128)(2,1)S(1)}, u32[]{:S(2)}, u32[]{:S(2)}) collective-permute-start(bf16[2,320,256]{2,1,0:T(8,128)(2,1)S(1)} %pad_maximum_fusion.10.refs_0_), channel_id=1, source_target_pairs={{0,32},{16,48},{32,0},{48,16},{1,33},{17,49},{33,1},{49,17},{2,34}... | collective-permute-start | bytes 983048 | tf_op jit(solution)/shard_map/ppermute | solution.py:45
  35.2 22.7 %collective-permute-start.8 = (bf16[4,40,1536]{2,1,0:T(8,128)(2,1)S(1)}, bf16[4,40,1536]{2,1,0:T(8,128)(2,1)}, u32[]{:S(2)}, u32[]{:S(2)}) collective-permute-start(bf16[4,40,1536]{2,1,0:T(8,128)(2,1)S(1)} %get-tuple-element.59), channel_id=1, source_target_pairs={{0,2},{2,0},{1,3},{3,1},{4,6},{6,4},{5,7},{7,5},{8,10},{10,8},{9,1... | collective-permute-start | bytes 1474568 | tf_op jit(solution)/shard_map/ppermute | solution.py:53
  48.8 4.9 collective-permute-start.9
  54.6 7.0 %collective-permute-start.10 = (bf16[2,40,1280]{2,1,0:T(8,128)(2,1)S(1)}, bf16[2,40,1280]{2,1,0:T(8,128)(2,1)S(1)}, u32[]{:S(2)}, u32[]{:S(2)}) collective-permute-start(bf16[2,40,1280]{2,1,0:T(8,128)(2,1)S(1)} %pad_maximum_fusion.13.refs_0_), channel_id=1, source_target_pairs={{0,16},{16,32},{32,48},{48,0},{1,17},{17,33},{33,49},{49,1},{2,18}... | collective-permute-start | bytes 614408 | tf_op jit(solution)/shard_map/ppermute | solution.py:45
  55.8 7.6 %collective-permute-start.11 = (bf16[2,40,1280]{2,1,0:T(8,128)(2,1)S(1)}, bf16[2,40,1280]{2,1,0:T(8,128)(2,1)S(1)}, u32[]{:S(2)}, u32[]{:S(2)}) collective-permute-start(bf16[2,40,1280]{2,1,0:T(8,128)(2,1)S(1)} %pad_maximum_fusion.13.refs_0_), channel_id=1, source_target_pairs={{0,48},{16,0},{32,16},{48,32},{1,49},{17,1},{33,17},{49,33},{2,50}... | collective-permute-start | bytes 614408 | tf_op jit(solution)/shard_map/ppermute | solution.py:45
  57.9 7.3 %collective-permute-start.12 = (bf16[2,40,1280]{2,1,0:T(8,128)(2,1)S(1)}, bf16[2,40,1280]{2,1,0:T(8,128)(2,1)S(1)}, u32[]{:S(2)}, u32[]{:S(2)}) collective-permute-start(bf16[2,40,1280]{2,1,0:T(8,128)(2,1)S(1)} %pad_maximum_fusion.13.refs_0_), channel_id=1, source_target_pairs={{0,32},{16,48},{32,0},{48,16},{1,33},{17,49},{33,1},{49,17},{2,34}... | collective-permute-start | bytes 614408 | tf_op jit(solution)/shard_map/ppermute | solution.py:45
  69.1 7.5 %collective-permute-start.13 = (bf16[2,40,1536]{2,1,0:T(8,128)(2,1)S(1)}, bf16[2,40,1536]{2,1,0:T(8,128)(2,1)S(1)}, u32[]{:S(2)}, u32[]{:S(2)}) collective-permute-start(bf16[2,40,1536]{2,1,0:T(8,128)(2,1)S(1)} %get-tuple-element.136), channel_id=1, source_target_pairs={{0,4},{4,8},{8,12},{12,0},{1,5},{5,9},{9,13},{13,1},{2,6},{6,10},{... | collective-permute-start | bytes 737288 | tf_op jit(solution)/shard_map/ppermute | solution.py:45
  69.9 9.0 %collective-permute-start.14 = (bf16[2,40,1536]{2,1,0:T(8,128)(2,1)S(1)}, bf16[2,40,1536]{2,1,0:T(8,128)(2,1)S(1)}, u32[]{:S(2)}, u32[]{:S(2)}) collective-permute-start(bf16[2,40,1536]{2,1,0:T(8,128)(2,1)S(1)} %get-tuple-element.135), channel_id=1, source_target_pairs={{0,12},{4,0},{8,4},{12,8},{1,13},{5,1},{9,5},{13,9},{2,14},{6,2},{... | collective-permute-start | bytes 737288 | tf_op jit(solution)/shard_map/ppermute | solution.py:45
  72.4 7.8 %collective-permute-start.15 = (bf16[2,40,1536]{2,1,0:T(8,128)(2,1)S(1)}, bf16[2,40,1536]{2,1,0:T(8,128)(2,1)S(1)}, u32[]{:S(2)}, u32[]{:S(2)}) collective-permute-start(bf16[2,40,1536]{2,1,0:T(8,128)(2,1)S(1)} %get-tuple-element.134), channel_id=1, source_target_pairs={{0,8},{4,12},{8,0},{12,4},{1,9},{5,13},{9,1},{13,5},{2,10},{6,14},... | collective-permute-start | bytes 737288 | tf_op jit(solution)/shard_map/ppermute | solution.py:45
  81.8 27.8 %collective-permute-start.38 = (bf16[320,1536]{1,0:T(8,128)(2,1)}, bf16[320,1536]{1,0:T(8,128)(2,1)}, u32[]{:S(2)}, u32[]{:S(2)}) collective-permute-start(bf16[320,1536]{1,0:T(8,128)(2,1)} %bitcast.35.refs_1_), channel_id=1, source_target_pairs={{0,64},{64,0},{1,65},{65,1},{2,66},{66,2},{3,67},{67,3},{4,68},{68... | collective-permute-start | bytes 2949128 | tf_op jit(solution)/shard_map/ppermute | solution.py:53
  84.8 14.8 %collective-permute-start.16 = (bf16[8,40,1280]{2,1,0:T(8,128)(2,1)}, bf16[8,40,1280]{2,1,0:T(8,128)(2,1)S(1)}, u32[]{:S(2)}, u32[]{:S(2)}) collective-permute-start(bf16[8,40,1280]{2,1,0:T(8,128)(2,1)} %shard_map.307.refs_0_), channel_id=1, source_target_pairs={{0,4},{4,8},{8,12},{12,0},{1,5},{5,9},{9,13},{13,1},{2,6},{6,10},{... | collective-permute-start | bytes 2457608 | tf_op jit(solution)/shard_map/ppermute | solution.py:45
  84.8 14.8 %collective-permute-start.17 = (bf16[8,40,1280]{2,1,0:T(8,128)(2,1)}, bf16[8,40,1280]{2,1,0:T(8,128)(2,1)S(1)}, u32[]{:S(2)}, u32[]{:S(2)}) collective-permute-start(bf16[8,40,1280]{2,1,0:T(8,128)(2,1)} %shard_map.307.refs_0_), channel_id=1, source_target_pairs={{0,12},{4,0},{8,4},{12,8},{1,13},{5,1},{9,5},{13,9},{2,14},{6,2},{... | collective-permute-start | bytes 2457608 | tf_op jit(solution)/shard_map/ppermute | solution.py:45
  100.9 5.9 %collective-permute-start.19 = (bf16[64,1024]{1,0:T(8,128)(2,1)}, bf16[64,1024]{1,0:T(8,128)(2,1)S(1)}, u32[]{:S(2)}, u32[]{:S(2)}) collective-permute-start(bf16[64,1024]{1,0:T(8,128)(2,1)} %shard_map.308), channel_id=1, source_target_pairs={{0,32},{16,48},{1,33},{17,49},{2,34},{18,50},{3,35},{19,51},{4,36}... | collective-permute-start | bytes 393224 | tf_op jit(solution)/shard_map/ppermute | solution.py:49
  102.3 7.3 %collective-permute-start.18 = (bf16[64,1024]{1,0:T(8,128)(2,1)}, bf16[64,1024]{1,0:T(8,128)(2,1)S(1)}, u32[]{:S(2)}, u32[]{:S(2)}) collective-permute-start(bf16[64,1024]{1,0:T(8,128)(2,1)} %shard_map.308), channel_id=1, source_target_pairs={{0,16},{16,32},{32,48},{1,17},{17,33},{33,49},{2,18},{18,34},{34,5... | collective-permute-start | bytes 393224 | tf_op jit(solution)/shard_map/ppermute | solution.py:49
  114.2 24.5 %collective-permute-start.21 = (bf16[4,40,1280]{2,1,0:T(8,128)(2,1)}, bf16[4,40,1280]{2,1,0:T(8,128)(2,1)S(1)}, u32[]{:S(2)}, u32[]{:S(2)}) collective-permute-start(bf16[4,40,1280]{2,1,0:T(8,128)(2,1)} %slice.180), channel_id=1, source_target_pairs={{0,4},{4,8},{8,12},{12,0},{1,5},{5,9},{9,13},{13,1},{2,6},{6,10},{... | collective-permute-start | bytes 1228808 | tf_op jit(solution)/shard_map/ppermute | solution.py:45
  115.4 23.3 %collective-permute-start.22 = (bf16[4,40,1280]{2,1,0:T(8,128)(2,1)}, bf16[4,40,1280]{2,1,0:T(8,128)(2,1)S(1)}, u32[]{:S(2)}, u32[]{:S(2)}) collective-permute-start(bf16[4,40,1280]{2,1,0:T(8,128)(2,1)} %slice.181), channel_id=1, source_target_pairs={{0,12},{4,0},{8,4},{12,8},{1,13},{5,1},{9,5},{13,9},{2,14},{6,2},{... | collective-permute-start | bytes 1228808 | tf_op jit(solution)/shard_map/ppermute | solution.py:45
  120.1 18.7 %collective-permute-start.20 = (bf16[3,64,1024]{2,1,0:T(8,128)(2,1)}, bf16[3,64,1024]{2,1,0:T(8,128)(2,1)S(1)}, u32[]{:S(2)}, u32[]{:S(2)}) collective-permute-start(bf16[3,64,1024]{2,1,0:T(8,128)(2,1)} %pad_maximum_fusion.9.refs_0_), channel_id=1, source_target_pairs={{0,4},{4,8},{8,12},{12,0},{1,5},{5,9},{9,13},{13,1},{2,6},{6,10},{... | collective-permute-start | bytes 1179656 | tf_op jit(solution)/shard_map/ppermute | solution.py:45
  120.1 20.4 %collective-permute-start.23 = (bf16[3,64,1024]{2,1,0:T(8,128)(2,1)}, bf16[3,64,1024]{2,1,0:T(8,128)(2,1)S(1)}, u32[]{:S(2)}, u32[]{:S(2)}) collective-permute-start(bf16[3,64,1024]{2,1,0:T(8,128)(2,1)} %pad_maximum_fusion.9.refs_0_), channel_id=1, source_target_pairs={{0,12},{4,0},{8,4},{12,8},{1,13},{5,1},{9,5},{13,9},{2,14},{6,2},{... | collective-permute-start | bytes 1179656 | tf_op jit(solution)/shard_map/ppermute | solution.py:45
  124.1 12.8 %all-to-all-start = ((bf16[8,160,128]{2,1,0:T(8,128)(2,1)}), bf16[8,160,128]{2,1,0:T(8,128)(2,1)}, u32[]{:S(2)}, u32[]{:S(2)}) async-start(bf16[8,160,128]{2,1,0:T(8,128)(2,1)} %bitcast_bitcast_fusion), calls=%async_computation | async-start | bytes 655360 | tf_op jit(solution)/shard_map/all_to_all | solution.py:271
  128.2 108.9 %all-gather.12.cloned.1.call-start = ((), (), s32[]{:S(2)}) async-start(), calls=%async_computation.11 | async-start | bytes 5898240 | tf_op jit(solution)/shard_map/all_gather | solution.py:692
  128.2 16.6 %collective-permute-start.24 = (bf16[3,64,1024]{2,1,0:T(8,128)(2,1)}, bf16[3,64,1024]{2,1,0:T(8,128)(2,1)}, u32[]{:S(2)}, u32[]{:S(2)}) collective-permute-start(bf16[3,64,1024]{2,1,0:T(8,128)(2,1)} %pad_maximum_fusion.9.refs_0_), channel_id=1, source_target_pairs={{0,8},{4,12},{8,0},{12,4},{1,9},{5,13},{9,1},{13,5},{2,10},{6,14},... | collective-permute-start | bytes 1179656 | tf_op jit(solution)/shard_map/ppermute | solution.py:45
  140.4 4.9 collective-permute-start.26
  141.2 4.7 collective-permute-start.27
  145.3 16.1 %collective-permute-start.29 = (bf16[8,40,1280]{2,1,0:T(8,128)(2,1)S(1)}, bf16[8,40,1280]{2,1,0:T(8,128)(2,1)}, u32[]{:S(2)}, u32[]{:S(2)}) collective-permute-start(bf16[8,40,1280]{2,1,0:T(8,128)(2,1)S(1)} %copy-done.10), channel_id=1, source_target_pairs={{0,2},{2,0},{1,3},{3,1},{4,6},{6,4},{5,7},{7,5},{8,10},{10,8},{9,1... | collective-permute-start | bytes 2457608 | tf_op jit(solution)/shard_map/ppermute | solution.py:53
  145.4 16.8 %collective-permute-start.30 = (bf16[8,40,1280]{2,1,0:T(8,128)(2,1)}, bf16[8,40,1280]{2,1,0:T(8,128)(2,1)}, u32[]{:S(2)}, u32[]{:S(2)}) collective-permute-start(bf16[8,40,1280]{2,1,0:T(8,128)(2,1)} %copy-done.29), channel_id=1, source_target_pairs={{0,2},{2,0},{1,3},{3,1},{4,6},{6,4},{5,7},{7,5},{8,10},{10,8},{9,1... | collective-permute-start | bytes 2457608 | tf_op jit(solution)/shard_map/ppermute | solution.py:53
  145.9 18.9 %collective-permute-start.31 = (bf16[8,40,1280]{2,1,0:T(8,128)(2,1)}, bf16[8,40,1280]{2,1,0:T(8,128)(2,1)}, u32[]{:S(2)}, u32[]{:S(2)}) collective-permute-start(bf16[8,40,1280]{2,1,0:T(8,128)(2,1)} %copy-done.32), channel_id=1, source_target_pairs={{0,2},{2,0},{1,3},{3,1},{4,6},{6,4},{5,7},{7,5},{8,10},{10,8},{9,1... | collective-permute-start | bytes 2457608 | tf_op jit(solution)/shard_map/ppermute | solution.py:53
  146.9 17.9 %collective-permute-start.33 = (bf16[4,40,1280]{2,1,0:T(8,128)(2,1)S(1)}, bf16[4,40,1280]{2,1,0:T(8,128)(2,1)}, u32[]{:S(2)}, u32[]{:S(2)}) collective-permute-start(bf16[4,40,1280]{2,1,0:T(8,128)(2,1)S(1)} %copy-done.17), channel_id=1, source_target_pairs={{0,2},{2,0},{1,3},{3,1},{4,6},{6,4},{5,7},{7,5},{8,10},{10,8},{9,1... | collective-permute-start | bytes 1228808 | tf_op jit(solution)/shard_map/ppermute | solution.py:53
  148.0 16.8 %collective-permute-start.32 = (bf16[4,40,1280]{2,1,0:T(8,128)(2,1)}, bf16[4,40,1280]{2,1,0:T(8,128)(2,1)}, u32[]{:S(2)}, u32[]{:S(2)}) collective-permute-start(bf16[4,40,1280]{2,1,0:T(8,128)(2,1)} %shard_map.313.refs_3_), channel_id=1, source_target_pairs={{0,2},{2,0},{1,3},{3,1},{4,6},{6,4},{5,7},{7,5},{8,10},{10,8},{9,1... | collective-permute-start | bytes 1228808 | tf_op jit(solution)/shard_map/ppermute | solution.py:53
  161.5 32.7 %collective-permute-start.35 = (bf16[128,2560]{1,0:T(8,128)(2,1)}, bf16[128,2560]{1,0:T(8,128)(2,1)}, u32[]{:S(2)}, u32[]{:S(2)}) collective-permute-start(bf16[128,2560]{1,0:T(8,128)(2,1)} %shard_map.315.refs_0_), channel_id=1, source_target_pairs={{0,4},{4,8},{8,12},{12,0},{1,5},{5,9},{9,13},{13,1},{2,6},{6,10},{... | collective-permute-start | bytes 1966088 | tf_op jit(solution)/shard_map/ppermute | solution.py:45
  162.2 32.0 %collective-permute-start.36 = (bf16[128,2560]{1,0:T(8,128)(2,1)}, bf16[128,2560]{1,0:T(8,128)(2,1)}, u32[]{:S(2)}, u32[]{:S(2)}) collective-permute-start(bf16[128,2560]{1,0:T(8,128)(2,1)} %shard_map.315.refs_0_), channel_id=1, source_target_pairs={{0,12},{4,0},{8,4},{12,8},{1,13},{5,1},{9,5},{13,9},{2,14},{6,2},{... | collective-permute-start | bytes 1966088 | tf_op jit(solution)/shard_map/ppermute | solution.py:45
  164.8 29.4 %collective-permute-start.37 = (bf16[128,2560]{1,0:T(8,128)(2,1)}, bf16[128,2560]{1,0:T(8,128)(2,1)}, u32[]{:S(2)}, u32[]{:S(2)}) collective-permute-start(bf16[128,2560]{1,0:T(8,128)(2,1)} %shard_map.315.refs_0_), channel_id=1, source_target_pairs={{0,8},{4,12},{8,0},{12,4},{1,9},{5,13},{9,1},{13,5},{2,10},{6,14},... | collective-permute-start | bytes 1966088 | tf_op jit(solution)/shard_map/ppermute | solution.py:45
  170.6 23.6 %collective-permute-start.34 = (bf16[128,2560]{1,0:T(8,128)(2,1)}, bf16[128,2560]{1,0:T(8,128)(2,1)}, u32[]{:S(2)}, u32[]{:S(2)}) collective-permute-start(bf16[128,2560]{1,0:T(8,128)(2,1)} %convolution_convert_fusion.4.refs_1_), channel_id=1, source_target_pairs={{0,1},{1,0},{2,3},{3,2},{4,5},{5,4},{6,7},{7,6},{8,9},{9,8},{10,11... | collective-permute-start | bytes 1966088 | tf_op jit(solution)/shard_map/ppermute | solution.py:53
  199.1 99.7 %reduce-scatter.4.cloned.1.call-start = ((), (), s32[]{:S(2)}) async-start(), calls=%async_computation.7 | async-start | bytes 5898240 | tf_op jit(solution)/shard_map/reduce_scatter | solution.py:708
  258.6 125.5 %reduce-scatter.6.cloned.1.call-start = ((), (), s32[]{:S(2)}) async-start(), calls=%async_computation.8 | async-start | bytes 9830400 | tf_op jit(solution)/shard_map/reduce_scatter | solution.py:717
  298.7 15.8 %collective-permute-start.43 = (bf16[128,2560]{1,0:T(8,128)(2,1)}, bf16[128,2560]{1,0:T(8,128)(2,1)S(1)}, u32[]{:S(2)}, u32[]{:S(2)}) collective-permute-start(bf16[128,2560]{1,0:T(8,128)(2,1)} %shard_map.326), channel_id=1, source_target_pairs={{0,1},{1,0},{2,3},{3,2},{4,5},{5,4},{6,7},{7,6},{8,9},{9,8},{10,11... | collective-permute-start | bytes 1966088 | tf_op jit(solution)/shard_map/ppermute | solution.py:53
  339.9 16.6 %all-to-all-start.1 = ((bf16[8,320,128]{2,1,0:T(8,128)(2,1)}), bf16[8,320,128]{2,1,0:T(8,128)(2,1)}, u32[]{:S(2)}, u32[]{:S(2)}) async-start(bf16[8,320,128]{2,1,0:T(8,128)(2,1)} %shard_map.329), calls=%async_computation.2 | async-start | bytes 1310720 | tf_op jit(solution)/shard_map/all_to_all | solution.py:271
  344.3 77.6 %all-gather.14.cloned.1.call-start = ((), (), s32[]{:S(2)}) async-start(), calls=%async_computation.12 | async-start | bytes 5898240 | tf_op jit(solution)/shard_map/all_gather | solution.py:769
  344.3 20.0 %collective-permute-start.45 = (bf16[3,64,1024]{2,1,0:T(8,128)(2,1)}, bf16[3,64,1024]{2,1,0:T(8,128)(2,1)}, u32[]{:S(2)}, u32[]{:S(2)}) collective-permute-start(bf16[3,64,1024]{2,1,0:T(8,128)(2,1)} %copy-done.62), channel_id=1, source_target_pairs={{0,4},{4,8},{8,12},{12,0},{1,5},{5,9},{9,13},{13,1},{2,6},{6,10},{... | collective-permute-start | bytes 1179656 | tf_op jit(solution)/shard_map/ppermute | solution.py:45
  346.2 26.7 %collective-permute-start.47 = (bf16[3,64,1024]{2,1,0:T(8,128)(2,1)S(1)}, bf16[3,64,1024]{2,1,0:T(8,128)(2,1)}, u32[]{:S(2)}, u32[]{:S(2)}) collective-permute-start(bf16[3,64,1024]{2,1,0:T(8,128)(2,1)S(1)} %get-tuple-element.71), channel_id=1, source_target_pairs={{0,8},{4,12},{8,0},{12,4},{1,9},{5,13},{9,1},{13,5},{2,10},{6,14},... | collective-permute-start | bytes 1179656 | tf_op jit(solution)/shard_map/ppermute | solution.py:45
  348.9 24.0 %collective-permute-start.46 = (bf16[3,64,1024]{2,1,0:T(8,128)(2,1)S(1)}, bf16[3,64,1024]{2,1,0:T(8,128)(2,1)}, u32[]{:S(2)}, u32[]{:S(2)}) collective-permute-start(bf16[3,64,1024]{2,1,0:T(8,128)(2,1)S(1)} %get-tuple-element.70), channel_id=1, source_target_pairs={{0,12},{4,0},{8,4},{12,8},{1,13},{5,1},{9,5},{13,9},{2,14},{6,2},{... | collective-permute-start | bytes 1179656 | tf_op jit(solution)/shard_map/ppermute | solution.py:45
  374.5 8.4 %collective-permute-start.49 = (bf16[64,1024]{1,0:T(8,128)(2,1)S(1)}, bf16[64,1024]{1,0:T(8,128)(2,1)S(1)}, u32[]{:S(2)}, u32[]{:S(2)}) collective-permute-start(bf16[64,1024]{1,0:T(8,128)(2,1)S(1)} %get-tuple-element.145), channel_id=1, source_target_pairs={{32,0},{48,16},{33,1},{49,17},{34,2},{50,18},{35,3},{51,19},{36,4}... | collective-permute-start | bytes 393224 | tf_op jit(solution)/shard_map/ppermute | solution.py:49
  375.8 7.1 %collective-permute-start.48 = (bf16[64,1024]{1,0:T(8,128)(2,1)S(1)}, bf16[64,1024]{1,0:T(8,128)(2,1)S(1)}, u32[]{:S(2)}, u32[]{:S(2)}) collective-permute-start(bf16[64,1024]{1,0:T(8,128)(2,1)S(1)} %get-tuple-element.144), channel_id=1, source_target_pairs={{16,0},{32,16},{48,32},{17,1},{33,17},{49,33},{18,2},{34,18},{50,3... | collective-permute-start | bytes 393224 | tf_op jit(solution)/shard_map/ppermute | solution.py:49
  384.2 126.6 %reduce-scatter.8.cloned.1.call-start = ((), (), s32[]{:S(2)}) async-start(), calls=%async_computation.9 | async-start | bytes 5898240 | tf_op jit(solution)/shard_map/reduce_scatter | solution.py:796
  393.2 5.0 collective-permute-start.50
  436.7 22.6 %collective-permute-start.54 = (bf16[128,2560]{1,0:T(8,128)(2,1)S(1)}, bf16[128,2560]{1,0:T(8,128)(2,1)S(1)}, u32[]{:S(2)}, u32[]{:S(2)}) collective-permute-start(bf16[128,2560]{1,0:T(8,128)(2,1)S(1)} %get-tuple-element.79), channel_id=1, source_target_pairs={{0,8},{4,12},{8,0},{12,4},{1,9},{5,13},{9,1},{13,5},{2,10},{6,14},... | collective-permute-start | bytes 1966088 | tf_op jit(solution)/shard_map/ppermute | solution.py:45
  438.6 39.1 %collective-permute-start.53 = (bf16[128,2560]{1,0:T(8,128)(2,1)}, bf16[128,2560]{1,0:T(8,128)(2,1)}, u32[]{:S(2)}, u32[]{:S(2)}) collective-permute-start(bf16[128,2560]{1,0:T(8,128)(2,1)} %get-tuple-element.78), channel_id=1, source_target_pairs={{0,12},{4,0},{8,4},{12,8},{1,13},{5,1},{9,5},{13,9},{2,14},{6,2},{... | collective-permute-start | bytes 1966088 | tf_op jit(solution)/shard_map/ppermute | solution.py:45
  440.0 39.2 %collective-permute-start.52 = (bf16[128,2560]{1,0:T(8,128)(2,1)}, bf16[128,2560]{1,0:T(8,128)(2,1)}, u32[]{:S(2)}, u32[]{:S(2)}) collective-permute-start(bf16[128,2560]{1,0:T(8,128)(2,1)} %get-tuple-element.77), channel_id=1, source_target_pairs={{0,4},{4,8},{8,12},{12,0},{1,5},{5,9},{9,13},{13,1},{2,6},{6,10},{... | collective-permute-start | bytes 1966088 | tf_op jit(solution)/shard_map/ppermute | solution.py:45
  442.8 55.4 %collective-permute-start.56 = (bf16[320,1536]{1,0:T(8,128)(2,1)}, bf16[320,1536]{1,0:T(8,128)(2,1)}, u32[]{:S(2)}, u32[]{:S(2)}) collective-permute-start(bf16[320,1536]{1,0:T(8,128)(2,1)} %dynamic-slice_bitcast_fusion), channel_id=1, source_target_pairs={{0,64},{64,0},{1,65},{65,1},{2,66},{66,2},{3,67},{67,3},{4,68},{68... | collective-permute-start | bytes 2949128 | tf_op jit(solution)/shard_map/ppermute | solution.py:53
  444.3 40.0 %collective-permute-start.59 = (bf16[2,320,512]{2,1,0:T(8,128)(2,1)}, bf16[2,320,512]{2,1,0:T(8,128)(2,1)}, u32[]{:S(2)}, u32[]{:S(2)}) collective-permute-start(bf16[2,320,512]{2,1,0:T(8,128)(2,1)} %get-tuple-element.82), channel_id=1, source_target_pairs={{0,32},{16,48},{32,0},{48,16},{1,33},{17,49},{33,1},{49,17},{2,34}... | collective-permute-start | bytes 1966088 | tf_op jit(solution)/shard_map/ppermute | solution.py:45
  459.4 25.0 %collective-permute-start.58 = (bf16[2,320,512]{2,1,0:T(8,128)(2,1)}, bf16[2,320,512]{2,1,0:T(8,128)(2,1)}, u32[]{:S(2)}, u32[]{:S(2)}) collective-permute-start(bf16[2,320,512]{2,1,0:T(8,128)(2,1)} %get-tuple-element.81), channel_id=1, source_target_pairs={{0,48},{16,0},{32,16},{48,32},{1,49},{17,1},{33,17},{49,33},{2,50}... | collective-permute-start | bytes 1966088 | tf_op jit(solution)/shard_map/ppermute | solution.py:45
  477.7 16.9 %collective-permute-start.57 = (bf16[2,320,512]{2,1,0:T(8,128)(2,1)}, bf16[2,320,512]{2,1,0:T(8,128)(2,1)}, u32[]{:S(2)}, u32[]{:S(2)}) collective-permute-start(bf16[2,320,512]{2,1,0:T(8,128)(2,1)} %copy-done.61), channel_id=1, source_target_pairs={{0,16},{16,32},{32,48},{48,0},{1,17},{17,33},{33,49},{49,1},{2,18}... | collective-permute-start | bytes 1966088 | tf_op jit(solution)/shard_map/ppermute | solution.py:45
  481.1 18.5 %collective-permute-start.55 = (bf16[128,2560]{1,0:T(8,128)(2,1)S(1)}, bf16[128,2560]{1,0:T(8,128)(2,1)S(1)}, u32[]{:S(2)}, u32[]{:S(2)}) collective-permute-start(bf16[128,2560]{1,0:T(8,128)(2,1)S(1)} %add_convert_fusion.1), channel_id=1, source_target_pairs={{0,1},{1,0},{2,3},{3,2},{4,5},{5,4},{6,7},{7,6},{8,9},{9,8},{10,11... | collective-permute-start | bytes 1966088 | tf_op jit(solution)/shard_map/ppermute | solution.py:53
  496.6 8.5 %collective-permute-start.60 = (bf16[320,512]{1,0:T(8,128)(2,1)S(1)}, bf16[320,512]{1,0:T(8,128)(2,1)S(1)}, u32[]{:S(2)}, u32[]{:S(2)}) collective-permute-start(bf16[320,512]{1,0:T(8,128)(2,1)S(1)} %dynamic-slice_bitcast_fusion.1), channel_id=1, source_target_pairs={{0,64},{64,0},{1,65},{65,1},{2,66},{66,2},{3,67},{67,3},{4,68},{68... | collective-permute-start | bytes 983048 | tf_op jit(solution)/shard_map/ppermute | solution.py:53
  506.4 23.1 %all-to-all-start.2 = ((bf16[8,40,2048]{2,1,0:T(8,128)(2,1)}), bf16[8,40,2048]{2,1,0:T(8,128)(2,1)S(1)}, u32[]{:S(2)}, u32[]{:S(2)}) async-start(bf16[8,40,2048]{2,1,0:T(8,128)(2,1)} %bitcast.181), calls=%async_computation.5 | async-start | bytes 2621440 | tf_op jit(solution)/shard_map/all_to_all | solution.py:271
  510.8 30.0 %collective-permute-start.51 = (bf16[128,2560]{1,0:T(8,128)(2,1)}, bf16[128,2560]{1,0:T(8,128)(2,1)}, u32[]{:S(2)}, u32[]{:S(2)}) collective-permute-start(bf16[128,2560]{1,0:T(8,128)(2,1)} %bitcast.187), channel_id=1, source_target_pairs={{0,1},{1,0},{2,3},{3,2},{4,5},{5,4},{6,7},{7,6},{8,9},{9,8},{10,11... | collective-permute-start | bytes 1966088 | tf_op jit(solution)/shard_map/ppermute | solution.py:53
  540.8 7.6 %collective-permute-start.61 = (bf16[8,40,256]{2,1,0:T(8,128)(2,1)}, bf16[8,40,256]{2,1,0:T(8,128)(2,1)S(1)}, u32[]{:S(2)}, u32[]{:S(2)}) collective-permute-start(bf16[8,40,256]{2,1,0:T(8,128)(2,1)} %shard_map.341), channel_id=1, source_target_pairs={{0,1},{1,0},{2,3},{3,2},{4,5},{5,4},{6,7},{7,6},{8,9},{9,8},{10,11... | collective-permute-start | bytes 491528 | tf_op jit(solution)/shard_map/ppermute | solution.py:53
  (103 other events, 574.0 us)
Sparse Core Ops, SparseCore 0:
  22.6 37.7 all-gather.9
  113.5 79.0 all-gather.7
  199.2 37.8 all-gather.11
  258.8 39.9 reduce-scatter.3
  301.0 76.3 reduce-scatter.5
  384.3 37.5 all-gather.13
  436.8 60.3 reduce-scatter.7

commit v4 on v3

--- a/solution.py
+++ b/solution.py
@@ -539,11 +539,8 @@
     )(index, rows, cols, extra, rows2, cols2, after)
 
 
-def row_scatter(parts, b):
-    total = parts[0].astype(F32)
-    for step, part in zip(STEPS[1:], parts[1:]):
-        total = total + shift(part, "y", step).astype(F32)
-    return pair_total(low_bits(total), 0, b, "b").astype(BF)
+def along_y(parts):
+    return [parts[0]] + [shift(part, "y", step) for step, part in zip(STEPS[1:], parts[1:])]
 
 
 def rms_rate(values):
@@ -786,15 +783,17 @@
         compiler_params=params(32),
     )(index, sent, w_small, group_tokens)
     rate_a = rms_rate(inflow)
-    norma_terms = scatter_terms(norma_mine, norma_theirs, "c", "x", index)
+    norma_terms = scatter_terms(norma_mine, norma_theirs, "c", "x", index, after=(feed_grad,))
     extra = jnp.concatenate([gain_a[:1], 0.5 * gain_b[None], jnp.zeros((6, D), F32)])
     parts = grads_by_chunk(
         normed_a, sent, extra, group_resid, group_attended, index, norma_terms[0]
     )
-    norma_terms[1:] = [tie(term, parts[0]) for term in norma_terms[1:]]
+    row_terms = along_y(parts)
+    norma_terms[1:] = [tie(term, *row_terms[1:]) for term in norma_terms[1:]]
     norma_low = low_bits(total_of(norma_terms))
     out_low = lax.psum_scatter(tie(feed_part, parts[0]), ("x", "c"), scatter_dimension=0)
-    late = jnp.concatenate([feed_grad, row_scatter(parts, b)], axis=1)
+    row_grad = pair_total(low_bits(total_of(row_terms)), 0, b, "b").astype(BF)
+    late = jnp.concatenate([feed_grad, row_grad], axis=1)
     late = exchange(late.reshape(GROUP, OWNED, 3 * F_PAD + 512))
     small_grad = late[:, :, 3 * F_PAD : 3 * F_PAD + 256]
     other_out = swap(out_low, "t")

time: 568 us -> 566 us (level)
  the two profiles are of different devices: /device:TPU:0 before, /device:TPU:7 now
where the time goes in v4:
time: 566 us; the launch traced here: 555 us
  waiting for transfers between devices  188 us (33%)
  starting transfers between devices  131 us (23%)
  local copies, waits for them, and re-layouts  66.2 us (12%)
  Pallas kernels  56.7 us (10%)
  matrix products  55.3 us (10%)
  other arithmetic  42.4 us (7%)
  between operations  15.8 us (3%)
    ppermute x31, waiting for transfers between devices, shift(): return lax.ppermute(value, axis, [(i, (i + step) % 4) for i in range(4)])  85.3 us
    unnamed x215, local copies, waits for them, and re-layouts  56.1 us
    dot_general x8, matrix products, dot(): lax.dot_general(left, right, (((left_dim,), (right_dim,)), ((), ())), pre...  55.3 us
    ppermute x27, starting transfers between devices, swap(): return lax.ppermute(value, axis, [(0, 1), (1, 0)])  52.9 us
    ppermute x27, waiting for transfers between devices, swap(): return lax.ppermute(value, axis, [(0, 1), (1, 0)])  51.4 us
    ppermute x31, starting transfers between devices, shift(): return lax.ppermute(value, axis, [(i, (i + step) % 4) for i in range(4)])  37 us
    all_to_all x3, starting transfers between devices, exchange(): lax.all_to_all(value, ('x', 'c'), split_axis=0, concat_axis=0, tiled=True)  31.2 us
    all_gather x1, waiting for transfers between devices, local(): group_b = lax.all_gather(normed_b, ('x', 'c'), axis=0).reshape(1024, D)  19.1 us
  transfers between devices with their start and end apart: 72, of which 35 were waited for; matrix products, arithmetic and copies ran while one was open for 15% of the time, Pallas kernels for 8%

profile of v4, /device:TPU:7, one launch (start us, length us, event | category | flops | bytes accessed | tf_op | source)
XLA Modules:
  0.0 555.5 jit_solution(6957306048163854652)
XLA Ops:
  22.4 2.7 collective-permute-done.4.after_ref
  30.8 4.0 collective-permute-start.8
  35.4 5.2 collective-permute-done.7.refs_3_
  40.6 2.3 shard_map.299
  45.3 2.8 collective-permute-done.9
  52.9 2.4 collective-permute-done.10.refs_1_
  63.4 2.4 collective-permute-start.15
  67.0 5.3 collective-permute-done.14.refs_2_
  76.7 2.5 copy-done
  80.5 4.1 shard_map.306
  84.6 2.3 copy-done.24
  88.5 5.3 collective-permute-start.19
  107.4 2.2 collective-permute-start.20
  110.4 17.5 %all-to-all-start = ((bf16[8,160,128]{2,1,0:T(8,128)(2,1)}), bf16[8,160,128]{2,1,0:T(8,128)(2,1)S(1)}, u32[]{:S(2)}, u32[]{:S(2)}) async-start(bf16[8,160,128]{2,1,0:T(8,128)(2,1)} %bitcast_bitcast_fusion), calls=%async_computation | async-start | bytes 655360 | tf_op jit(solution)/shard_map/all_to_all | solution.py:271
  129.3 4.2 all-to-all-done
  136.0 9.6 %collective-permute-start.26 = (bf16[3,64,1024]{2,1,0:T(8,128)(2,1)}, bf16[3,64,1024]{2,1,0:T(8,128)(2,1)S(1)}, u32[]{:S(2)}, u32[]{:S(2)}) collective-permute-start(bf16[3,64,1024]{2,1,0:T(8,128)(2,1)} %shard_map.309.refs_1_), channel_id=1, source_target_pairs={{0,2},{2,0},{1,3},{3,1},{4,6},{6,4},{5,7},{7,5},{8,10},{10,8},{9,1... | collective-permute-start | bytes 1179656 | tf_op jit(solution)/shard_map/ppermute | solution.py:53
  160.0 5.1 shard_map.312
  166.8 3.6 shard_map.314
  170.4 3.1 convolution_convert_fusion.4.refs_1_
  173.6 3.6 collective-permute-start.34
  177.8 3.7 collective-permute-done.35.refs_0_
  181.6 15.3 %collective-permute-done.36.refs_0_ = bf16[128,2560]{1,0:T(8,128)(2,1)} collective-permute-done((bf16[128,2560]{1,0:T(8,128)(2,1)S(1)}, bf16[128,2560]{1,0:T(8,128)(2,1)}, u32[]{:S(2)}, u32[]{:S(2)}) %collective-permute-start.36) | collective-permute-done | bytes 655392 | tf_op jit(solution)/shard_map/ppermute | solution.py:45
  207.6 3.2 shard_map.322
  210.9 2.3 copy-done.6
  213.1 6.1 %fusion.3.refs_0_ = f32[1024,512]{1,0:T(8,128)} fusion(bf16[1024,2560]{1,0:T(8,128)(2,1)S(1)} %bitcast.152, bf16[2560,1536]{1,0:T(8,128)(2,1)} %bitcast.175), kind=kOutput, calls=%fused_computation.12 | convolution fusion | flops 2684354560 | bytes 9961472 | tf_op jit(solution)/shard_map/dot_general | solution.py:39
  219.2 19.1 %all-gather.12.cloned.1.call-done.refs_0_ = bf16[1024,2560]{1,0:T(8,128)(2,1)} async-done(((bf16[128,2560]{1,0:T(8,128)(2,1)}), bf16[1024,2560]{1,0:T(8,128)(2,1)}) %all-gather.12.cloned.1.call-update) | async-done | bytes 5242896 | tf_op jit(solution)/shard_map/all_gather | solution.py:689
  238.4 9.2 %fusion.1 = f32[1024,1024]{1,0:T(8,128)S(1)} fusion(bf16[1024,2560]{1,0:T(8,128)(2,1)} %all-gather.12.cloned.1.call-done.refs_0_, bf16[2560,1536]{1,0:T(8,128)(2,1)} %bitcast.176), kind=kOutput, calls=%fused_computation.5 | convolution fusion | flops 5368709120 | bytes 14680064 | tf_op jit(solution)/shard_map/dot_general | solution.py:39
  249.4 10.5 %convolution_convert_fusion.2.refs_1_ = bf16[1024,2560]{1,0:T(8,128)(2,1)} fusion(bf16[2560,1536]{1,0:T(8,128)(2,1)} %bitcast.177, bf16[1024,512]{1,0:T(8,128)(2,1)S(1)} %get-tuple-element.128, bf16[1024,512]{1,0:T(8,128)(2,1)S(1)} %get-tuple-element.127), kind=kOutput, calls=%fused_computation.3 | convolution fusion | flops 5375524864 | bytes 12582912 | tf_op jit(solution)/shard_map/dot_general | solution.py:39
  260.2 7.0 %convolution_convert_fusion.3.refs_1_ = bf16[2560,512]{1,0:T(8,128)(2,1)} fusion(bf16[1024,2560]{1,0:T(8,128)(2,1)} %shard_map.324, bf16[1024,512]{1,0:T(8,128)(2,1)S(1)} %get-tuple-element.129), kind=kOutput, calls=%fused_computation.7 | convolution fusion | flops 2685665280 | bytes 8912896 | tf_op jit(solution)/shard_map/dot_general | solution.py:39
  267.2 7.8 %convolution_convert_fusion.1.refs_2_ = bf16[2560,1024]{1,0:T(8,128)(2,1)} fusion(bf16[1024,2560]{1,0:T(8,128)(2,1)S(1)} %copy-done.82, bf16[1024,512]{1,0:T(8,128)(2,1)S(1)} %copy-done.92, bf16[1024,512]{1,0:T(8,128)(2,1)S(1)} %copy-done.90), kind=kOutput, calls=%fused_computation.2 | convolution fusion | flops 5375524864 | bytes 12582912 | tf_op jit(solution)/shard_map/dot_general | solution.py:39
  274.9 7.2 %pad_maximum_fusion = bf16[2560,1536]{1,0:T(8,128)(2,1)} fusion(bf16[2560,512]{1,0:T(8,128)(2,1)} %convolution_convert_fusion.3.refs_1_, bf16[2560,1024]{1,0:T(8,128)(2,1)} %convolution_convert_fusion.1.refs_2_), kind=kLoop, calls=%fused_computation | loop fusion | flops 15728640 | bytes 15728640 | tf_op jit(solution)/shard_map/concatenate | solution.py:713
  282.2 6.4 %convolution_convert_fusion = bf16[1024,2560]{1,0:T(8,128)(2,1)} fusion(bf16[1024,512]{1,0:T(8,128)(2,1)S(1)} %get-tuple-element.129, bf16[2560,1536]{1,0:T(8,128)(2,1)} %bitcast.178), kind=kOutput, calls=%fused_computation.1 | convolution fusion | flops 2686976000 | bytes 8912896 | tf_op jit(solution)/shard_map/dot_general | solution.py:39
  288.6 11.8 %reduce-scatter.4.cloned.1.call-done = bf16[1,128,2560]{2,1,0:T(8,128)(2,1)} async-done(((bf16[8,128,2560]{2,1,0:T(8,128)(2,1)}), bf16[1,128,2560]{2,1,0:T(8,128)(2,1)}) %reduce-scatter.4.cloned.1.call-update) | async-done | bytes 655376 | tf_op jit(solution)/shard_map/reduce_scatter | solution.py:705
  300.5 3.0 collective-permute-start.43
  303.5 13.7 %collective-permute-done.43 = bf16[128,2560]{1,0:T(8,128)(2,1)S(1)} collective-permute-done((bf16[128,2560]{1,0:T(8,128)(2,1)}, bf16[128,2560]{1,0:T(8,128)(2,1)S(1)}, u32[]{:S(2)}, u32[]{:S(2)}) %collective-permute-start.43) | collective-permute-done | bytes 655392 | tf_op jit(solution)/shard_map/ppermute | solution.py:53
  320.9 5.2 convolution_convert_fusion.5
  326.2 9.5 %shard_map.327 = (f32[5,256,128]{2,1,0:T(8,128)S(1)}, bf16[4,3,64,1024]{3,2,1,0:T(8,128)(2,1)S(1)}, bf16[4,3,64,1024]{3,2,1,0:T(8,128)(2,1)S(1)}) custom-call(s32[2]{0:T(128)S(1)} %pad_add_fusion.base_ref, s32[12]{0:T(128)S(1)} %stack.145.index_ref, bf16[5,256,128]{2,1,0:T(8,128)(2,1)S(1)} %bitcast.157, f32[17,128,640]{2,1,0:T(8,128)} %copy-done.23, ...), custom_call_target="tpu_custom_call" | custom-call | flops 1 | bytes 1 | tf_op jit(solution)/shard_map/pallas_call | solution.py:726
  336.8 2.3 collective-permute-done.44.received_ref
  340.9 4.4 all-to-all-start.1
  345.5 2.3 collective-permute-start.47
  348.0 6.6 %all-to-all-done.1 = bf16[8,320,128]{2,1,0:T(8,128)(2,1)S(1)} async-done(((bf16[8,320,128]{2,1,0:T(8,128)(2,1)}), bf16[8,320,128]{2,1,0:T(8,128)(2,1)S(1)}, u32[]{:S(2)}, u32[]{:S(2)}) %all-to-all-start.1) | async-done | bytes 655392 | tf_op jit(solution)/shard_map/all_to_all | solution.py:271
  355.5 7.0 %collective-permute-done.45.refs_0_ = bf16[3,64,1024]{2,1,0:T(8,128)(2,1)S(1)} collective-permute-done((bf16[3,64,1024]{2,1,0:T(8,128)(2,1)S(1)}, bf16[3,64,1024]{2,1,0:T(8,128)(2,1)S(1)}, u32[]{:S(2)}, u32[]{:S(2)}) %collective-permute-start.45) | collective-permute-done | bytes 393248 | tf_op jit(solution)/shard_map/ppermute | solution.py:45
  364.0 6.8 %collective-permute-done.46 = bf16[3,64,1024]{2,1,0:T(8,128)(2,1)} collective-permute-done((bf16[3,64,1024]{2,1,0:T(8,128)(2,1)S(1)}, bf16[3,64,1024]{2,1,0:T(8,128)(2,1)}, u32[]{:S(2)}, u32[]{:S(2)}) %collective-permute-start.46) | collective-permute-done | bytes 393248 | tf_op jit(solution)/shard_map/ppermute | solution.py:45
  375.1 5.2 collective-permute-done.49
  382.9 2.5 copy-done.1
  385.4 4.9 shard_map.331
  397.3 22.0 %collective-permute-done.51 = bf16[320,1536]{1,0:T(8,128)(2,1)S(1)} collective-permute-done((bf16[320,1536]{1,0:T(8,128)(2,1)}, bf16[320,1536]{1,0:T(8,128)(2,1)S(1)}, u32[]{:S(2)}, u32[]{:S(2)}) %collective-permute-start.51) | collective-permute-done | bytes 983072 | tf_op jit(solution)/shard_map/ppermute | solution.py:53
  422.6 2.3 shard_map.334
  427.4 2.5 copy-done.25
  429.9 8.2 %shard_map.335 = (bf16[2,320,512]{2,1,0:T(8,128)(2,1)S(1)}, bf16[2,320,512]{2,1,0:T(8,128)(2,1)S(1)}, bf16[2,320,512]{2,1,0:T(8,128)(2,1)S(1)}, bf16[2,320,512]{2,1,0:T(8,128)(2,1)S(1)}) custom-call(s32[12]{0:T(128)S(1)} %stack.145.index_ref, bf16[8,128,2560]{2,1,0:T(8,128)(2,1)S(1)} %copy-done.25, bf16[224,1024]{1,0:T(8,128)(2,1)S(1)} %copy-done.13, ...), custom_call_target="tpu_custom_call" | custom-call | flops 1 | bytes 1 | tf_op jit(solution)/shard_map/pallas_call | solution.py:519
  441.5 3.5 collective-permute-start.54
  445.1 2.2 collective-permute-start.56
  450.8 7.9 %collective-permute-done.54.refs_1_ = bf16[2,320,512]{2,1,0:T(8,128)(2,1)S(1)} collective-permute-done((bf16[2,320,512]{2,1,0:T(8,128)(2,1)}, bf16[2,320,512]{2,1,0:T(8,128)(2,1)S(1)}, u32[]{:S(2)}, u32[]{:S(2)}) %collective-permute-start.54) | collective-permute-done | bytes 655392 | tf_op jit(solution)/shard_map/ppermute | solution.py:45
  458.7 3.1 collective-permute-start.53
  461.9 12.5 %collective-permute-done.56.refs_3_ = bf16[2,320,512]{2,1,0:T(8,128)(2,1)S(1)} collective-permute-done((bf16[2,320,512]{2,1,0:T(8,128)(2,1)}, bf16[2,320,512]{2,1,0:T(8,128)(2,1)S(1)}, u32[]{:S(2)}, u32[]{:S(2)}) %collective-permute-start.56) | collective-permute-done | bytes 655392 | tf_op jit(solution)/shard_map/ppermute | solution.py:45
  476.2 10.5 %collective-permute-done.57.refs_0_ = bf16[128,2560]{1,0:T(8,128)(2,1)} collective-permute-done((bf16[128,2560]{1,0:T(8,128)(2,1)}, bf16[128,2560]{1,0:T(8,128)(2,1)}, u32[]{:S(2)}, u32[]{:S(2)}) %collective-permute-start.57) | collective-permute-done | bytes 655392 | tf_op jit(solution)/shard_map/ppermute | solution.py:45
  486.7 3.1 collective-permute-done.53.refs_0_
  491.7 2.9 collective-permute-start.59
  497.0 9.2 %all-to-all-start.2 = ((bf16[8,40,2048]{2,1,0:T(8,128)(2,1)}), bf16[8,40,2048]{2,1,0:T(8,128)(2,1)S(1)}, u32[]{:S(2)}, u32[]{:S(2)}) async-start(bf16[8,40,2048]{2,1,0:T(8,128)(2,1)} %bitcast.182), calls=%async_computation.5 | async-start | bytes 2621440 | tf_op jit(solution)/shard_map/all_to_all | solution.py:271
  508.9 15.9 %collective-permute-start.52 = (bf16[128,2560]{1,0:T(8,128)(2,1)}, bf16[128,2560]{1,0:T(8,128)(2,1)}, u32[]{:S(2)}, u32[]{:S(2)}) collective-permute-start(bf16[128,2560]{1,0:T(8,128)(2,1)} %bitcast.189), channel_id=1, source_target_pairs={{0,1},{1,0},{2,3},{3,2},{4,5},{5,4},{6,7},{7,6},{8,9},{9,8},{10,11... | collective-permute-start | bytes 1966088 | tf_op jit(solution)/shard_map/ppermute | solution.py:53
  524.7 3.1 fusion.16
  536.2 3.5 shard_map.344
  541.1 2.3 add_convert_fusion.2
  543.4 3.0 collective-permute-done.61.refs_1_
  (429 shorter events, 148.2 us)
Async XLA Ops:
  7.2 53.3 %all-gather.10.cloned.1.call-start = ((), (), s32[]{:S(2)}) async-start(), calls=%async_computation.10 | async-start | bytes 5898240 | tf_op jit(solution)/shard_map/all_gather | solution.py:596
  12.4 4.6 collective-permute-start.1
  12.6 4.5 collective-permute-start.2
  13.9 4.4 collective-permute-start.3
  19.9 181.9 %all-gather.8.cloned.1.call-start = ((), (), s32[]{:S(2)}) async-start(), calls=%async_computation.6 | async-start | bytes 9830400 | tf_op jit(solution)/shard_map/all_gather | solution.py:661
  20.7 4.3 collective-permute-start.4
  25.1 10.2 %collective-permute-start.5 = (bf16[2,320,256]{2,1,0:T(8,128)(2,1)S(1)}, bf16[2,320,256]{2,1,0:T(8,128)(2,1)S(1)}, u32[]{:S(2)}, u32[]{:S(2)}) collective-permute-start(bf16[2,320,256]{2,1,0:T(8,128)(2,1)S(1)} %pad_maximum_fusion.10.refs_0_), channel_id=1, source_target_pairs={{0,16},{16,32},{32,48},{48,0},{1,17},{17,33},{33,49},{49,1},{2,18}... | collective-permute-start | bytes 983048 | tf_op jit(solution)/shard_map/ppermute | solution.py:45
  26.5 8.9 %collective-permute-start.6 = (bf16[2,320,256]{2,1,0:T(8,128)(2,1)S(1)}, bf16[2,320,256]{2,1,0:T(8,128)(2,1)S(1)}, u32[]{:S(2)}, u32[]{:S(2)}) collective-permute-start(bf16[2,320,256]{2,1,0:T(8,128)(2,1)S(1)} %pad_maximum_fusion.10.refs_0_), channel_id=1, source_target_pairs={{0,48},{16,0},{32,16},{48,32},{1,49},{17,1},{33,17},{49,33},{2,50}... | collective-permute-start | bytes 983048 | tf_op jit(solution)/shard_map/ppermute | solution.py:45
  28.0 12.6 %collective-permute-start.7 = (bf16[2,320,256]{2,1,0:T(8,128)(2,1)S(1)}, bf16[2,320,256]{2,1,0:T(8,128)(2,1)S(1)}, u32[]{:S(2)}, u32[]{:S(2)}) collective-permute-start(bf16[2,320,256]{2,1,0:T(8,128)(2,1)S(1)} %pad_maximum_fusion.10.refs_0_), channel_id=1, source_target_pairs={{0,32},{16,48},{32,0},{48,16},{1,33},{17,49},{33,1},{49,17},{2,34}... | collective-permute-start | bytes 983048 | tf_op jit(solution)/shard_map/ppermute | solution.py:45
  30.8 21.1 %collective-permute-start.8 = (bf16[4,40,1536]{2,1,0:T(8,128)(2,1)S(1)}, bf16[4,40,1536]{2,1,0:T(8,128)(2,1)S(1)}, u32[]{:S(2)}, u32[]{:S(2)}) collective-permute-start(bf16[4,40,1536]{2,1,0:T(8,128)(2,1)S(1)} %get-tuple-element.59), channel_id=1, source_target_pairs={{0,2},{2,0},{1,3},{3,1},{4,6},{6,4},{5,7},{7,5},{8,10},{10,8},{9,1... | collective-permute-start | bytes 1474568 | tf_op jit(solution)/shard_map/ppermute | solution.py:53
  44.0 4.1 collective-permute-start.9
  49.0 6.3 %collective-permute-start.10 = (bf16[2,40,1280]{2,1,0:T(8,128)(2,1)S(1)}, bf16[2,40,1280]{2,1,0:T(8,128)(2,1)S(1)}, u32[]{:S(2)}, u32[]{:S(2)}) collective-permute-start(bf16[2,40,1280]{2,1,0:T(8,128)(2,1)S(1)} %pad_maximum_fusion.13.refs_0_), channel_id=1, source_target_pairs={{0,16},{16,32},{32,48},{48,0},{1,17},{17,33},{33,49},{49,1},{2,18}... | collective-permute-start | bytes 614408 | tf_op jit(solution)/shard_map/ppermute | solution.py:45
  50.0 6.6 %collective-permute-start.11 = (bf16[2,40,1280]{2,1,0:T(8,128)(2,1)S(1)}, bf16[2,40,1280]{2,1,0:T(8,128)(2,1)S(1)}, u32[]{:S(2)}, u32[]{:S(2)}) collective-permute-start(bf16[2,40,1280]{2,1,0:T(8,128)(2,1)S(1)} %pad_maximum_fusion.13.refs_0_), channel_id=1, source_target_pairs={{0,48},{16,0},{32,16},{48,32},{1,49},{17,1},{33,17},{49,33},{2,50}... | collective-permute-start | bytes 614408 | tf_op jit(solution)/shard_map/ppermute | solution.py:45
  51.8 6.1 %collective-permute-start.12 = (bf16[2,40,1280]{2,1,0:T(8,128)(2,1)S(1)}, bf16[2,40,1280]{2,1,0:T(8,128)(2,1)S(1)}, u32[]{:S(2)}, u32[]{:S(2)}) collective-permute-start(bf16[2,40,1280]{2,1,0:T(8,128)(2,1)S(1)} %pad_maximum_fusion.13.refs_0_), channel_id=1, source_target_pairs={{0,32},{16,48},{32,0},{48,16},{1,33},{17,49},{33,1},{49,17},{2,34}... | collective-permute-start | bytes 614408 | tf_op jit(solution)/shard_map/ppermute | solution.py:45
  61.8 5.1 collective-permute-start.13
  63.3 8.9 %collective-permute-start.14 = (bf16[2,40,1536]{2,1,0:T(8,128)(2,1)S(1)}, bf16[2,40,1536]{2,1,0:T(8,128)(2,1)S(1)}, u32[]{:S(2)}, u32[]{:S(2)}) collective-permute-start(bf16[2,40,1536]{2,1,0:T(8,128)(2,1)S(1)} %get-tuple-element.135), channel_id=1, source_target_pairs={{0,12},{4,0},{8,4},{12,8},{1,13},{5,1},{9,5},{13,9},{2,14},{6,2},{... | collective-permute-start | bytes 737288 | tf_op jit(solution)/shard_map/ppermute | solution.py:45
  63.4 8.8 %collective-permute-start.15 = (bf16[2,40,1536]{2,1,0:T(8,128)(2,1)S(1)}, bf16[2,40,1536]{2,1,0:T(8,128)(2,1)S(1)}, u32[]{:S(2)}, u32[]{:S(2)}) collective-permute-start(bf16[2,40,1536]{2,1,0:T(8,128)(2,1)S(1)} %get-tuple-element.134), channel_id=1, source_target_pairs={{0,8},{4,12},{8,0},{12,4},{1,9},{5,13},{9,1},{13,5},{2,10},{6,14},... | collective-permute-start | bytes 737288 | tf_op jit(solution)/shard_map/ppermute | solution.py:45
  73.8 23.7 %collective-permute-start.38 = (bf16[320,1536]{1,0:T(8,128)(2,1)}, bf16[320,1536]{1,0:T(8,128)(2,1)S(1)}, u32[]{:S(2)}, u32[]{:S(2)}) collective-permute-start(bf16[320,1536]{1,0:T(8,128)(2,1)} %bitcast.35.refs_1_), channel_id=1, source_target_pairs={{0,64},{64,0},{1,65},{65,1},{2,66},{66,2},{3,67},{67,3},{4,68},{68... | collective-permute-start | bytes 2949128 | tf_op jit(solution)/shard_map/ppermute | solution.py:53
  75.1 12.8 %collective-permute-start.16 = (bf16[8,40,1280]{2,1,0:T(8,128)(2,1)}, bf16[8,40,1280]{2,1,0:T(8,128)(2,1)}, u32[]{:S(2)}, u32[]{:S(2)}) collective-permute-start(bf16[8,40,1280]{2,1,0:T(8,128)(2,1)} %shard_map.307.refs_0_), channel_id=1, source_target_pairs={{0,4},{4,8},{8,12},{12,0},{1,5},{5,9},{9,13},{13,1},{2,6},{6,10},{... | collective-permute-start | bytes 2457608 | tf_op jit(solution)/shard_map/ppermute | solution.py:45
  75.5 13.0 %collective-permute-start.17 = (bf16[8,40,1280]{2,1,0:T(8,128)(2,1)}, bf16[8,40,1280]{2,1,0:T(8,128)(2,1)}, u32[]{:S(2)}, u32[]{:S(2)}) collective-permute-start(bf16[8,40,1280]{2,1,0:T(8,128)(2,1)} %shard_map.307.refs_0_), channel_id=1, source_target_pairs={{0,12},{4,0},{8,4},{12,8},{1,13},{5,1},{9,5},{13,9},{2,14},{6,2},{... | collective-permute-start | bytes 2457608 | tf_op jit(solution)/shard_map/ppermute | solution.py:45
  88.5 7.6 %collective-permute-start.19 = (bf16[64,1024]{1,0:T(8,128)(2,1)}, bf16[64,1024]{1,0:T(8,128)(2,1)S(1)}, u32[]{:S(2)}, u32[]{:S(2)}) collective-permute-start(bf16[64,1024]{1,0:T(8,128)(2,1)} %shard_map.308), channel_id=1, source_target_pairs={{0,32},{16,48},{1,33},{17,49},{2,34},{18,50},{3,35},{19,51},{4,36}... | collective-permute-start | bytes 393224 | tf_op jit(solution)/shard_map/ppermute | solution.py:49
  104.1 30.3 %collective-permute-start.21 = (bf16[4,40,1280]{2,1,0:T(8,128)(2,1)}, bf16[4,40,1280]{2,1,0:T(8,128)(2,1)S(1)}, u32[]{:S(2)}, u32[]{:S(2)}) collective-permute-start(bf16[4,40,1280]{2,1,0:T(8,128)(2,1)} %slice.180), channel_id=1, source_target_pairs={{0,4},{4,8},{8,12},{12,0},{1,5},{5,9},{9,13},{13,1},{2,6},{6,10},{... | collective-permute-start | bytes 1228808 | tf_op jit(solution)/shard_map/ppermute | solution.py:45
  106.8 27.5 %collective-permute-start.22 = (bf16[4,40,1280]{2,1,0:T(8,128)(2,1)}, bf16[4,40,1280]{2,1,0:T(8,128)(2,1)S(1)}, u32[]{:S(2)}, u32[]{:S(2)}) collective-permute-start(bf16[4,40,1280]{2,1,0:T(8,128)(2,1)} %slice.181), channel_id=1, source_target_pairs={{0,12},{4,0},{8,4},{12,8},{1,13},{5,1},{9,5},{13,9},{2,14},{6,2},{... | collective-permute-start | bytes 1228808 | tf_op jit(solution)/shard_map/ppermute | solution.py:45
  107.4 27.0 %collective-permute-start.20 = (bf16[3,64,1024]{2,1,0:T(8,128)(2,1)S(1)}, bf16[3,64,1024]{2,1,0:T(8,128)(2,1)S(1)}, u32[]{:S(2)}, u32[]{:S(2)}) collective-permute-start(bf16[3,64,1024]{2,1,0:T(8,128)(2,1)S(1)} %pad_maximum_fusion.9.refs_0_), channel_id=1, source_target_pairs={{0,4},{4,8},{8,12},{12,0},{1,5},{5,9},{9,13},{13,1},{2,6},{6,10},{... | collective-permute-start | bytes 1179656 | tf_op jit(solution)/shard_map/ppermute | solution.py:45
  109.6 36.0 %collective-permute-start.23 = (bf16[3,64,1024]{2,1,0:T(8,128)(2,1)S(1)}, bf16[3,64,1024]{2,1,0:T(8,128)(2,1)S(1)}, u32[]{:S(2)}, u32[]{:S(2)}) collective-permute-start(bf16[3,64,1024]{2,1,0:T(8,128)(2,1)S(1)} %pad_maximum_fusion.9.refs_0_), channel_id=1, source_target_pairs={{0,12},{4,0},{8,4},{12,8},{1,13},{5,1},{9,5},{13,9},{2,14},{6,2},{... | collective-permute-start | bytes 1179656 | tf_op jit(solution)/shard_map/ppermute | solution.py:45
  110.4 23.1 %all-to-all-start = ((bf16[8,160,128]{2,1,0:T(8,128)(2,1)}), bf16[8,160,128]{2,1,0:T(8,128)(2,1)S(1)}, u32[]{:S(2)}, u32[]{:S(2)}) async-start(bf16[8,160,128]{2,1,0:T(8,128)(2,1)} %bitcast_bitcast_fusion), calls=%async_computation | async-start | bytes 655360 | tf_op jit(solution)/shard_map/all_to_all | solution.py:271
  127.9 110.4 %all-gather.12.cloned.1.call-start = ((), (), s32[]{:S(2)}) async-start(), calls=%async_computation.11 | async-start | bytes 5898240 | tf_op jit(solution)/shard_map/all_gather | solution.py:689
  127.9 18.4 %collective-permute-start.24 = (bf16[3,64,1024]{2,1,0:T(8,128)(2,1)S(1)}, bf16[3,64,1024]{2,1,0:T(8,128)(2,1)S(1)}, u32[]{:S(2)}, u32[]{:S(2)}) collective-permute-start(bf16[3,64,1024]{2,1,0:T(8,128)(2,1)S(1)} %pad_maximum_fusion.9.refs_0_), channel_id=1, source_target_pairs={{0,8},{4,12},{8,0},{12,4},{1,9},{5,13},{9,1},{13,5},{2,10},{6,14},... | collective-permute-start | bytes 1179656 | tf_op jit(solution)/shard_map/ppermute | solution.py:45
  136.0 12.2 %collective-permute-start.26 = (bf16[3,64,1024]{2,1,0:T(8,128)(2,1)}, bf16[3,64,1024]{2,1,0:T(8,128)(2,1)S(1)}, u32[]{:S(2)}, u32[]{:S(2)}) collective-permute-start(bf16[3,64,1024]{2,1,0:T(8,128)(2,1)} %shard_map.309.refs_1_), channel_id=1, source_target_pairs={{0,2},{2,0},{1,3},{3,1},{4,6},{6,4},{5,7},{7,5},{8,10},{10,8},{9,1... | collective-permute-start | bytes 1179656 | tf_op jit(solution)/shard_map/ppermute | solution.py:53
  147.7 17.5 %collective-permute-start.29 = (bf16[8,40,1280]{2,1,0:T(8,128)(2,1)S(1)}, bf16[8,40,1280]{2,1,0:T(8,128)(2,1)}, u32[]{:S(2)}, u32[]{:S(2)}) collective-permute-start(bf16[8,40,1280]{2,1,0:T(8,128)(2,1)S(1)} %copy-done.8), channel_id=1, source_target_pairs={{0,2},{2,0},{1,3},{3,1},{4,6},{6,4},{5,7},{7,5},{8,10},{10,8},{9,1... | collective-permute-start | bytes 2457608 | tf_op jit(solution)/shard_map/ppermute | solution.py:53
  148.2 17.1 %collective-permute-start.30 = (bf16[8,40,1280]{2,1,0:T(8,128)(2,1)}, bf16[8,40,1280]{2,1,0:T(8,128)(2,1)}, u32[]{:S(2)}, u32[]{:S(2)}) collective-permute-start(bf16[8,40,1280]{2,1,0:T(8,128)(2,1)} %collective-permute-done.16.refs_1_), channel_id=1, source_target_pairs={{0,2},{2,0},{1,3},{3,1},{4,6},{6,4},{5,7},{7,5},{8,10},{10,8},{9,1... | collective-permute-start | bytes 2457608 | tf_op jit(solution)/shard_map/ppermute | solution.py:53
  148.3 18.4 %collective-permute-start.31 = (bf16[8,40,1280]{2,1,0:T(8,128)(2,1)}, bf16[8,40,1280]{2,1,0:T(8,128)(2,1)}, u32[]{:S(2)}, u32[]{:S(2)}) collective-permute-start(bf16[8,40,1280]{2,1,0:T(8,128)(2,1)} %collective-permute-done.17.refs_2_), channel_id=1, source_target_pairs={{0,2},{2,0},{1,3},{3,1},{4,6},{6,4},{5,7},{7,5},{8,10},{10,8},{9,1... | collective-permute-start | bytes 2457608 | tf_op jit(solution)/shard_map/ppermute | solution.py:53
  149.7 17.1 %collective-permute-start.33 = (bf16[4,40,1280]{2,1,0:T(8,128)(2,1)S(1)}, bf16[4,40,1280]{2,1,0:T(8,128)(2,1)}, u32[]{:S(2)}, u32[]{:S(2)}) collective-permute-start(bf16[4,40,1280]{2,1,0:T(8,128)(2,1)S(1)} %copy-done.15), channel_id=1, source_target_pairs={{0,2},{2,0},{1,3},{3,1},{4,6},{6,4},{5,7},{7,5},{8,10},{10,8},{9,1... | collective-permute-start | bytes 1228808 | tf_op jit(solution)/shard_map/ppermute | solution.py:53
  150.5 16.3 %collective-permute-start.32 = (bf16[4,40,1280]{2,1,0:T(8,128)(2,1)}, bf16[4,40,1280]{2,1,0:T(8,128)(2,1)}, u32[]{:S(2)}, u32[]{:S(2)}) collective-permute-start(bf16[4,40,1280]{2,1,0:T(8,128)(2,1)} %shard_map.313.refs_3_), channel_id=1, source_target_pairs={{0,2},{2,0},{1,3},{3,1},{4,6},{6,4},{5,7},{7,5},{8,10},{10,8},{9,1... | collective-permute-start | bytes 1228808 | tf_op jit(solution)/shard_map/ppermute | solution.py:53
  165.2 16.4 %collective-permute-start.35 = (bf16[128,2560]{1,0:T(8,128)(2,1)S(1)}, bf16[128,2560]{1,0:T(8,128)(2,1)}, u32[]{:S(2)}, u32[]{:S(2)}) collective-permute-start(bf16[128,2560]{1,0:T(8,128)(2,1)S(1)} %copy-done.22), channel_id=1, source_target_pairs={{0,4},{4,8},{8,12},{12,0},{1,5},{5,9},{9,13},{13,1},{2,6},{6,10},{... | collective-permute-start | bytes 1966088 | tf_op jit(solution)/shard_map/ppermute | solution.py:45
  165.3 31.6 %collective-permute-start.36 = (bf16[128,2560]{1,0:T(8,128)(2,1)S(1)}, bf16[128,2560]{1,0:T(8,128)(2,1)}, u32[]{:S(2)}, u32[]{:S(2)}) collective-permute-start(bf16[128,2560]{1,0:T(8,128)(2,1)S(1)} %copy-done.22), channel_id=1, source_target_pairs={{0,12},{4,0},{8,4},{12,8},{1,13},{5,1},{9,5},{13,9},{2,14},{6,2},{... | collective-permute-start | bytes 1966088 | tf_op jit(solution)/shard_map/ppermute | solution.py:45
  166.7 30.2 %collective-permute-start.37 = (bf16[128,2560]{1,0:T(8,128)(2,1)S(1)}, bf16[128,2560]{1,0:T(8,128)(2,1)}, u32[]{:S(2)}, u32[]{:S(2)}) collective-permute-start(bf16[128,2560]{1,0:T(8,128)(2,1)S(1)} %copy-done.22), channel_id=1, source_target_pairs={{0,8},{4,12},{8,0},{12,4},{1,9},{5,13},{9,1},{13,5},{2,10},{6,14},... | collective-permute-start | bytes 1966088 | tf_op jit(solution)/shard_map/ppermute | solution.py:45
  173.6 23.4 %collective-permute-start.34 = (bf16[128,2560]{1,0:T(8,128)(2,1)}, bf16[128,2560]{1,0:T(8,128)(2,1)}, u32[]{:S(2)}, u32[]{:S(2)}) collective-permute-start(bf16[128,2560]{1,0:T(8,128)(2,1)} %convolution_convert_fusion.4.refs_1_), channel_id=1, source_target_pairs={{0,1},{1,0},{2,3},{3,2},{4,5},{5,4},{6,7},{7,6},{8,9},{9,8},{10,11... | collective-permute-start | bytes 1966088 | tf_op jit(solution)/shard_map/ppermute | solution.py:53
  201.8 98.7 %reduce-scatter.4.cloned.1.call-start = ((), (), s32[]{:S(2)}) async-start(), calls=%async_computation.7 | async-start | bytes 5898240 | tf_op jit(solution)/shard_map/reduce_scatter | solution.py:705
  203.0 3.7 collective-permute-start.41
  203.4 4.2 collective-permute-start.42
  259.9 121.5 %reduce-scatter.6.cloned.1.call-start = ((), (), s32[]{:S(2)}) async-start(), calls=%async_computation.8 | async-start | bytes 9830400 | tf_op jit(solution)/shard_map/reduce_scatter | solution.py:714
  300.5 16.8 %collective-permute-start.43 = (bf16[128,2560]{1,0:T(8,128)(2,1)}, bf16[128,2560]{1,0:T(8,128)(2,1)S(1)}, u32[]{:S(2)}, u32[]{:S(2)}) collective-permute-start(bf16[128,2560]{1,0:T(8,128)(2,1)} %shard_map.326), channel_id=1, source_target_pairs={{0,1},{1,0},{2,3},{3,2},{4,5},{5,4},{6,7},{7,6},{8,9},{9,8},{10,11... | collective-permute-start | bytes 1966088 | tf_op jit(solution)/shard_map/ppermute | solution.py:53
  340.9 13.7 %all-to-all-start.1 = ((bf16[8,320,128]{2,1,0:T(8,128)(2,1)}), bf16[8,320,128]{2,1,0:T(8,128)(2,1)S(1)}, u32[]{:S(2)}, u32[]{:S(2)}) async-start(bf16[8,320,128]{2,1,0:T(8,128)(2,1)} %shard_map.329), calls=%async_computation.2 | async-start | bytes 1310720 | tf_op jit(solution)/shard_map/all_to_all | solution.py:271
  345.4 82.1 %all-gather.14.cloned.1.call-start = ((), (), s32[]{:S(2)}) async-start(), calls=%async_computation.12 | async-start | bytes 5898240 | tf_op jit(solution)/shard_map/all_gather | solution.py:766
  345.4 17.1 %collective-permute-start.45 = (bf16[3,64,1024]{2,1,0:T(8,128)(2,1)S(1)}, bf16[3,64,1024]{2,1,0:T(8,128)(2,1)S(1)}, u32[]{:S(2)}, u32[]{:S(2)}) collective-permute-start(bf16[3,64,1024]{2,1,0:T(8,128)(2,1)S(1)} %get-tuple-element.69), channel_id=1, source_target_pairs={{0,4},{4,8},{8,12},{12,0},{1,5},{5,9},{9,13},{13,1},{2,6},{6,10},{... | collective-permute-start | bytes 1179656 | tf_op jit(solution)/shard_map/ppermute | solution.py:45
  345.5 17.8 %collective-permute-start.47 = (bf16[3,64,1024]{2,1,0:T(8,128)(2,1)S(1)}, bf16[3,64,1024]{2,1,0:T(8,128)(2,1)S(1)}, u32[]{:S(2)}, u32[]{:S(2)}) collective-permute-start(bf16[3,64,1024]{2,1,0:T(8,128)(2,1)S(1)} %get-tuple-element.71), channel_id=1, source_target_pairs={{0,8},{4,12},{8,0},{12,4},{1,9},{5,13},{9,1},{13,5},{2,10},{6,14},... | collective-permute-start | bytes 1179656 | tf_op jit(solution)/shard_map/ppermute | solution.py:45
  347.7 23.1 %collective-permute-start.46 = (bf16[3,64,1024]{2,1,0:T(8,128)(2,1)S(1)}, bf16[3,64,1024]{2,1,0:T(8,128)(2,1)}, u32[]{:S(2)}, u32[]{:S(2)}) collective-permute-start(bf16[3,64,1024]{2,1,0:T(8,128)(2,1)S(1)} %get-tuple-element.70), channel_id=1, source_target_pairs={{0,12},{4,0},{8,4},{12,8},{1,13},{5,1},{9,5},{13,9},{2,14},{6,2},{... | collective-permute-start | bytes 1179656 | tf_op jit(solution)/shard_map/ppermute | solution.py:45
  372.3 7.9 %collective-permute-start.49 = (bf16[64,1024]{1,0:T(8,128)(2,1)S(1)}, bf16[64,1024]{1,0:T(8,128)(2,1)S(1)}, u32[]{:S(2)}, u32[]{:S(2)}) collective-permute-start(bf16[64,1024]{1,0:T(8,128)(2,1)S(1)} %get-tuple-element.145), channel_id=1, source_target_pairs={{32,0},{48,16},{33,1},{49,17},{34,2},{50,18},{35,3},{51,19},{36,4}... | collective-permute-start | bytes 393224 | tf_op jit(solution)/shard_map/ppermute | solution.py:49
  373.6 6.6 %collective-permute-start.48 = (bf16[64,1024]{1,0:T(8,128)(2,1)S(1)}, bf16[64,1024]{1,0:T(8,128)(2,1)S(1)}, u32[]{:S(2)}, u32[]{:S(2)}) collective-permute-start(bf16[64,1024]{1,0:T(8,128)(2,1)S(1)} %get-tuple-element.144), channel_id=1, source_target_pairs={{16,0},{32,16},{48,32},{17,1},{33,17},{49,33},{18,2},{34,18},{50,3... | collective-permute-start | bytes 393224 | tf_op jit(solution)/shard_map/ppermute | solution.py:49
  381.5 127.4 %reduce-scatter.8.cloned.1.call-start = ((), (), s32[]{:S(2)}) async-start(), calls=%async_computation.9 | async-start | bytes 5898240 | tf_op jit(solution)/shard_map/reduce_scatter | solution.py:794
  391.7 29.1 %collective-permute-start.50 = (bf16[4,128,2560]{2,1,0:T(8,128)(2,1)}, bf16[4,128,2560]{2,1,0:T(8,128)(2,1)}, u32[]{:S(2)}, u32[]{:S(2)}) collective-permute-start(bf16[4,128,2560]{2,1,0:T(8,128)(2,1)} %get-tuple-element.74), channel_id=1, source_target_pairs={{0,2},{2,0},{1,3},{3,1},{4,6},{6,4},{5,7},{7,5},{8,10},{10,8},{9,1... | collective-permute-start | bytes 7864328 | tf_op jit(solution)/shard_map/ppermute | solution.py:53
  395.6 23.7 %collective-permute-start.51 = (bf16[320,1536]{1,0:T(8,128)(2,1)}, bf16[320,1536]{1,0:T(8,128)(2,1)S(1)}, u32[]{:S(2)}, u32[]{:S(2)}) collective-permute-start(bf16[320,1536]{1,0:T(8,128)(2,1)} %dynamic-slice_bitcast_fusion), channel_id=1, source_target_pairs={{0,64},{64,0},{1,65},{65,1},{2,66},{66,2},{3,67},{67,3},{4,68},{68... | collective-permute-start | bytes 2949128 | tf_op jit(solution)/shard_map/ppermute | solution.py:53
  441.5 17.2 %collective-permute-start.54 = (bf16[2,320,512]{2,1,0:T(8,128)(2,1)}, bf16[2,320,512]{2,1,0:T(8,128)(2,1)S(1)}, u32[]{:S(2)}, u32[]{:S(2)}) collective-permute-start(bf16[2,320,512]{2,1,0:T(8,128)(2,1)} %copy-done.69), channel_id=1, source_target_pairs={{0,16},{16,32},{32,48},{48,0},{1,17},{17,33},{33,49},{49,1},{2,18}... | collective-permute-start | bytes 1966088 | tf_op jit(solution)/shard_map/ppermute | solution.py:45
  445.1 16.8 %collective-permute-start.55 = (bf16[2,320,512]{2,1,0:T(8,128)(2,1)}, bf16[2,320,512]{2,1,0:T(8,128)(2,1)S(1)}, u32[]{:S(2)}, u32[]{:S(2)}) collective-permute-start(bf16[2,320,512]{2,1,0:T(8,128)(2,1)} %copy-done.68), channel_id=1, source_target_pairs={{0,48},{16,0},{32,16},{48,32},{1,49},{17,1},{33,17},{49,33},{2,50}... | collective-permute-start | bytes 1966088 | tf_op jit(solution)/shard_map/ppermute | solution.py:45
  445.1 29.3 %collective-permute-start.56 = (bf16[2,320,512]{2,1,0:T(8,128)(2,1)}, bf16[2,320,512]{2,1,0:T(8,128)(2,1)S(1)}, u32[]{:S(2)}, u32[]{:S(2)}) collective-permute-start(bf16[2,320,512]{2,1,0:T(8,128)(2,1)} %copy-done.67), channel_id=1, source_target_pairs={{0,32},{16,48},{32,0},{48,16},{1,33},{17,49},{33,1},{49,17},{2,34}... | collective-permute-start | bytes 1966088 | tf_op jit(solution)/shard_map/ppermute | solution.py:45
  447.3 28.9 %collective-permute-start.58 = (bf16[128,2560]{1,0:T(8,128)(2,1)}, bf16[128,2560]{1,0:T(8,128)(2,1)}, u32[]{:S(2)}, u32[]{:S(2)}) collective-permute-start(bf16[128,2560]{1,0:T(8,128)(2,1)} %copy-done.66), channel_id=1, source_target_pairs={{0,8},{4,12},{8,0},{12,4},{1,9},{5,13},{9,1},{13,5},{2,10},{6,14},... | collective-permute-start | bytes 1966088 | tf_op jit(solution)/shard_map/ppermute | solution.py:45
  449.1 37.7 %collective-permute-start.57 = (bf16[128,2560]{1,0:T(8,128)(2,1)}, bf16[128,2560]{1,0:T(8,128)(2,1)}, u32[]{:S(2)}, u32[]{:S(2)}) collective-permute-start(bf16[128,2560]{1,0:T(8,128)(2,1)} %copy-done.65), channel_id=1, source_target_pairs={{0,12},{4,0},{8,4},{12,8},{1,13},{5,1},{9,5},{13,9},{2,14},{6,2},{... | collective-permute-start | bytes 1966088 | tf_op jit(solution)/shard_map/ppermute | solution.py:45
  458.7 31.1 %collective-permute-start.53 = (bf16[128,2560]{1,0:T(8,128)(2,1)}, bf16[128,2560]{1,0:T(8,128)(2,1)}, u32[]{:S(2)}, u32[]{:S(2)}) collective-permute-start(bf16[128,2560]{1,0:T(8,128)(2,1)} %copy-done.64), channel_id=1, source_target_pairs={{0,4},{4,8},{8,12},{12,0},{1,5},{5,9},{9,13},{13,1},{2,6},{6,10},{... | collective-permute-start | bytes 1966088 | tf_op jit(solution)/shard_map/ppermute | solution.py:45
  474.9 19.8 %collective-permute-start.60 = (bf16[320,512]{1,0:T(8,128)(2,1)S(1)}, bf16[320,512]{1,0:T(8,128)(2,1)}, u32[]{:S(2)}, u32[]{:S(2)}) collective-permute-start(bf16[320,512]{1,0:T(8,128)(2,1)S(1)} %dynamic-slice_bitcast_fusion.1), channel_id=1, source_target_pairs={{0,64},{64,0},{1,65},{65,1},{2,66},{66,2},{3,67},{67,3},{4,68},{68... | collective-permute-start | bytes 983048 | tf_op jit(solution)/shard_map/ppermute | solution.py:53
  491.7 14.4 %collective-permute-start.59 = (bf16[128,2560]{1,0:T(8,128)(2,1)S(1)}, bf16[128,2560]{1,0:T(8,128)(2,1)S(1)}, u32[]{:S(2)}, u32[]{:S(2)}) collective-permute-start(bf16[128,2560]{1,0:T(8,128)(2,1)S(1)} %add_convert_fusion.1), channel_id=1, source_target_pairs={{0,1},{1,0},{2,3},{3,2},{4,5},{5,4},{6,7},{7,6},{8,9},{9,8},{10,11... | collective-permute-start | bytes 1966088 | tf_op jit(solution)/shard_map/ppermute | solution.py:53
  497.0 30.8 %all-to-all-start.2 = ((bf16[8,40,2048]{2,1,0:T(8,128)(2,1)}), bf16[8,40,2048]{2,1,0:T(8,128)(2,1)S(1)}, u32[]{:S(2)}, u32[]{:S(2)}) async-start(bf16[8,40,2048]{2,1,0:T(8,128)(2,1)} %bitcast.182), calls=%async_computation.5 | async-start | bytes 2621440 | tf_op jit(solution)/shard_map/all_to_all | solution.py:271
  508.9 31.6 %collective-permute-start.52 = (bf16[128,2560]{1,0:T(8,128)(2,1)}, bf16[128,2560]{1,0:T(8,128)(2,1)}, u32[]{:S(2)}, u32[]{:S(2)}) collective-permute-start(bf16[128,2560]{1,0:T(8,128)(2,1)} %bitcast.189), channel_id=1, source_target_pairs={{0,1},{1,0},{2,3},{3,2},{4,5},{5,4},{6,7},{7,6},{8,9},{9,8},{10,11... | collective-permute-start | bytes 1966088 | tf_op jit(solution)/shard_map/ppermute | solution.py:53
  540.5 6.0 %collective-permute-start.61 = (bf16[8,40,256]{2,1,0:T(8,128)(2,1)}, bf16[8,40,256]{2,1,0:T(8,128)(2,1)S(1)}, u32[]{:S(2)}, u32[]{:S(2)}) collective-permute-start(bf16[8,40,256]{2,1,0:T(8,128)(2,1)} %shard_map.341), channel_id=1, source_target_pairs={{0,1},{1,0},{2,3},{3,2},{4,5},{5,4},{6,7},{7,6},{8,9},{9,8},{10,11... | collective-permute-start | bytes 491528 | tf_op jit(solution)/shard_map/ppermute | solution.py:53
  (113 other events, 560.8 us)
Sparse Core Ops, SparseCore 0:
  20.0 38.7 all-gather.9
  102.4 90.1 all-gather.7
  201.9 36.4 all-gather.11
  260.0 40.3 reduce-scatter.3
  302.7 77.3 reduce-scatter.5
  382.2 38.7 all-gather.13
  441.7 67.1 reduce-scatter.7

commit v5 on v4

--- a/solution.py
+++ b/solution.py
@@ -783,7 +783,8 @@
         compiler_params=params(32),
     )(index, sent, w_small, group_tokens)
     rate_a = rms_rate(inflow)
-    norma_terms = scatter_terms(norma_mine, norma_theirs, "c", "x", index, after=(feed_grad,))
+    norma_terms = scatter_terms(norma_mine, norma_theirs, "c", "x", index)
+    norma_terms[0] = tie(norma_terms[0], feed_grad)
     extra = jnp.concatenate([gain_a[:1], 0.5 * gain_b[None], jnp.zeros((6, D), F32)])
     parts = grads_by_chunk(
         normed_a, sent, extra, group_resid, group_attended, index, norma_terms[0]

time: 566 us -> 559 us (0.988)
  the two profiles are of different devices: /device:TPU:7 before, /device:TPU:0 now
where the time goes in v5:
time: 559 us; the launch traced here: 549 us
  waiting for transfers between devices  205 us (37%)
  starting transfers between devices  104 us (19%)
  local copies, waits for them, and re-layouts  68.9 us (12%)
  Pallas kernels  56.4 us (10%)
  matrix products  55.5 us (10%)
  other arithmetic  43.6 us (8%)
  between operations  15.9 us (3%)
    ppermute x31, waiting for transfers between devices, shift(): return lax.ppermute(value, axis, [(i, (i + step) % 4) for i in range(4)])  98.4 us
    unnamed x233, local copies, waits for them, and re-layouts  56.3 us
    dot_general x8, matrix products, dot(): lax.dot_general(left, right, (((left_dim,), (right_dim,)), ((), ())), pre...  55.5 us
    ppermute x31, starting transfers between devices, shift(): return lax.ppermute(value, axis, [(i, (i + step) % 4) for i in range(4)])  52.9 us
    ppermute x27, waiting for transfers between devices, swap(): return lax.ppermute(value, axis, [(0, 1), (1, 0)])  52.3 us
    ppermute x27, starting transfers between devices, swap(): return lax.ppermute(value, axis, [(0, 1), (1, 0)])  30.4 us
    all_gather x1, waiting for transfers between devices, local(): group_b = lax.all_gather(normed_b, ('x', 'c'), axis=0).reshape(1024, D)  19.9 us
    all_to_all x3, waiting for transfers between devices, exchange(): lax.all_to_all(value, ('x', 'c'), split_axis=0, concat_axis=0, tiled=True)  14.7 us
  transfers between devices with their start and end apart: 72, of which 42 were waited for; matrix products, arithmetic and copies ran while one was open for 16% of the time, Pallas kernels for 8%

profile of v5, /device:TPU:0, one launch (start us, length us, event | category | flops | bytes accessed | tf_op | source)
XLA Modules:
  0.0 548.7 jit_solution(8669175051304251827)
XLA Ops:
  25.3 3.3 collective-permute-done.4.after_ref
  36.0 3.6 collective-permute-done.5.refs_1_
  39.6 4.0 collective-permute-done.6.refs_2_
  50.5 3.1 collective-permute-done.9
  59.0 2.6 collective-permute-done.10.refs_1_
  69.9 2.5 collective-permute-start.14
  73.0 3.6 collective-permute-done.13.refs_1_
  81.8 3.1 collective-permute-start.38
  84.8 3.2 collective-permute-start.17
  88.2 2.5 copy-done
  92.0 4.1 shard_map.306
  101.1 4.4 collective-permute-start.18
  105.6 2.8 collective-permute-done.18.refs_1_
  116.8 3.2 collective-permute-start.22
  120.1 3.2 collective-permute-start.23
  124.1 3.4 all-to-all-start
  127.6 3.6 collective-permute-start.24
  131.2 5.0 all-to-all-done
  140.0 4.1 collective-permute-done.24.refs_0_
  157.5 5.1 shard_map.312
  163.4 4.6 collective-permute-start.36
  169.4 3.1 shard_map.314
  172.6 3.1 convolution_convert_fusion.4.refs_1_
  175.7 3.9 collective-permute-start.34
  180.6 2.6 collective-permute-done.35.refs_0_
  183.2 13.3 %collective-permute-done.36.refs_0_ = bf16[128,2560]{1,0:T(8,128)(2,1)} collective-permute-done((bf16[128,2560]{1,0:T(8,128)(2,1)S(1)}, bf16[128,2560]{1,0:T(8,128)(2,1)}, u32[]{:S(2)}, u32[]{:S(2)}) %collective-permute-start.36) | collective-permute-done | bytes 655392 | tf_op jit(solution)/shard_map/ppermute | solution.py:45
  208.6 3.2 shard_map.322
  214.1 6.3 %fusion.3.refs_0_ = f32[1024,512]{1,0:T(8,128)} fusion(bf16[1024,2560]{1,0:T(8,128)(2,1)S(1)} %bitcast.152, bf16[2560,1536]{1,0:T(8,128)(2,1)} %bitcast.175), kind=kOutput, calls=%fused_computation.12 | convolution fusion | flops 2684354560 | bytes 9961472 | tf_op jit(solution)/shard_map/dot_general | solution.py:39
  220.4 19.9 %all-gather.12.cloned.1.call-done.refs_0_ = bf16[1024,2560]{1,0:T(8,128)(2,1)} async-done(((bf16[128,2560]{1,0:T(8,128)(2,1)}), bf16[1024,2560]{1,0:T(8,128)(2,1)}) %all-gather.12.cloned.1.call-update) | async-done | bytes 5242896 | tf_op jit(solution)/shard_map/all_gather | solution.py:689
  240.2 9.2 %fusion.1 = f32[1024,1024]{1,0:T(8,128)S(1)} fusion(bf16[1024,2560]{1,0:T(8,128)(2,1)} %all-gather.12.cloned.1.call-done.refs_0_, bf16[2560,1536]{1,0:T(8,128)(2,1)} %bitcast.176), kind=kOutput, calls=%fused_computation.5 | convolution fusion | flops 5368709120 | bytes 14680064 | tf_op jit(solution)/shard_map/dot_general | solution.py:39
  251.2 10.5 %convolution_convert_fusion.2.refs_1_ = bf16[1024,2560]{1,0:T(8,128)(2,1)} fusion(bf16[2560,1536]{1,0:T(8,128)(2,1)} %bitcast.177, bf16[1024,512]{1,0:T(8,128)(2,1)S(1)} %get-tuple-element.128, bf16[1024,512]{1,0:T(8,128)(2,1)S(1)} %get-tuple-element.127), kind=kOutput, calls=%fused_computation.3 | convolution fusion | flops 5375524864 | bytes 12582912 | tf_op jit(solution)/shard_map/dot_general | solution.py:39
  262.1 7.0 %convolution_convert_fusion.3.refs_1_ = bf16[2560,512]{1,0:T(8,128)(2,1)} fusion(bf16[1024,2560]{1,0:T(8,128)(2,1)} %shard_map.324, bf16[1024,512]{1,0:T(8,128)(2,1)S(1)} %get-tuple-element.129), kind=kOutput, calls=%fused_computation.7 | convolution fusion | flops 2685665280 | bytes 8912896 | tf_op jit(solution)/shard_map/dot_general | solution.py:39
  269.0 7.8 %convolution_convert_fusion.1.refs_2_ = bf16[2560,1024]{1,0:T(8,128)(2,1)} fusion(bf16[1024,2560]{1,0:T(8,128)(2,1)S(1)} %copy-done.91, bf16[1024,512]{1,0:T(8,128)(2,1)S(1)} %copy-done.102, bf16[1024,512]{1,0:T(8,128)(2,1)S(1)} %copy-done.100), kind=kOutput, calls=%fused_computation.2 | convolution fusion | flops 5375524864 | bytes 12582912 | tf_op jit(solution)/shard_map/dot_general | solution.py:39
  276.8 7.3 %pad_maximum_fusion = bf16[2560,1536]{1,0:T(8,128)(2,1)} fusion(bf16[2560,512]{1,0:T(8,128)(2,1)} %convolution_convert_fusion.3.refs_1_, bf16[2560,1024]{1,0:T(8,128)(2,1)} %convolution_convert_fusion.1.refs_2_), kind=kLoop, calls=%fused_computation | loop fusion | flops 15728640 | bytes 15728640 | tf_op jit(solution)/shard_map/concatenate | solution.py:713
  284.1 6.5 %convolution_convert_fusion = bf16[1024,2560]{1,0:T(8,128)(2,1)} fusion(bf16[1024,512]{1,0:T(8,128)(2,1)S(1)} %get-tuple-element.129, bf16[2560,1536]{1,0:T(8,128)(2,1)} %bitcast.178), kind=kOutput, calls=%fused_computation.1 | convolution fusion | flops 2686976000 | bytes 8912896 | tf_op jit(solution)/shard_map/dot_general | solution.py:39
  290.6 11.3 %reduce-scatter.4.cloned.1.call-done = bf16[1,128,2560]{2,1,0:T(8,128)(2,1)} async-done(((bf16[8,128,2560]{2,1,0:T(8,128)(2,1)}), bf16[1,128,2560]{2,1,0:T(8,128)(2,1)}) %reduce-scatter.4.cloned.1.call-update) | async-done | bytes 655376 | tf_op jit(solution)/shard_map/reduce_scatter | solution.py:705
  301.9 3.3 collective-permute-start.43
  305.2 12.4 %collective-permute-done.43 = bf16[128,2560]{1,0:T(8,128)(2,1)S(1)} collective-permute-done((bf16[128,2560]{1,0:T(8,128)(2,1)}, bf16[128,2560]{1,0:T(8,128)(2,1)S(1)}, u32[]{:S(2)}, u32[]{:S(2)}) %collective-permute-start.43) | collective-permute-done | bytes 655392 | tf_op jit(solution)/shard_map/ppermute | solution.py:53
  321.3 5.2 convolution_convert_fusion.5
  326.6 9.4 %shard_map.327 = (f32[5,256,128]{2,1,0:T(8,128)S(1)}, bf16[4,3,64,1024]{3,2,1,0:T(8,128)(2,1)S(1)}, bf16[4,3,64,1024]{3,2,1,0:T(8,128)(2,1)S(1)}) custom-call(s32[2]{0:T(128)S(1)} %pad_add_fusion.base_ref, s32[12]{0:T(128)S(1)} %stack.145.index_ref, bf16[5,256,128]{2,1,0:T(8,128)(2,1)S(1)} %bitcast.157, f32[17,128,640]{2,1,0:T(8,128)} %copy-done.26, ...), custom_call_target="tpu_custom_call" | custom-call | flops 1 | bytes 1 | tf_op jit(solution)/shard_map/pallas_call | solution.py:726
  341.3 3.7 all-to-all-start.1
  347.0 2.7 collective-permute-start.47
  351.4 5.9 %all-to-all-done.1 = bf16[8,320,128]{2,1,0:T(8,128)(2,1)S(1)} async-done(((bf16[8,320,128]{2,1,0:T(8,128)(2,1)}), bf16[8,320,128]{2,1,0:T(8,128)(2,1)S(1)}, u32[]{:S(2)}, u32[]{:S(2)}) %all-to-all-start.1) | async-done | bytes 655392 | tf_op jit(solution)/shard_map/all_to_all | solution.py:271
  358.2 6.8 %collective-permute-done.45.refs_0_ = bf16[3,64,1024]{2,1,0:T(8,128)(2,1)S(1)} collective-permute-done((bf16[3,64,1024]{2,1,0:T(8,128)(2,1)S(1)}, bf16[3,64,1024]{2,1,0:T(8,128)(2,1)S(1)}, u32[]{:S(2)}, u32[]{:S(2)}) %collective-permute-start.45) | collective-permute-done | bytes 393248 | tf_op jit(solution)/shard_map/ppermute | solution.py:45
  365.7 7.9 %collective-permute-done.47 = bf16[3,64,1024]{2,1,0:T(8,128)(2,1)S(1)} collective-permute-done((bf16[3,64,1024]{2,1,0:T(8,128)(2,1)S(1)}, bf16[3,64,1024]{2,1,0:T(8,128)(2,1)S(1)}, u32[]{:S(2)}, u32[]{:S(2)}) %collective-permute-start.47) | collective-permute-done | bytes 393248 | tf_op jit(solution)/shard_map/ppermute | solution.py:45
  379.4 5.0 collective-permute-done.49
  387.0 2.5 copy-done.1
  389.5 4.9 shard_map.331
  402.1 2.6 shard_map.334
  408.3 14.5 %collective-permute-done.51 = bf16[320,1536]{1,0:T(8,128)(2,1)} collective-permute-done((bf16[320,1536]{1,0:T(8,128)(2,1)}, bf16[320,1536]{1,0:T(8,128)(2,1)}, u32[]{:S(2)}, u32[]{:S(2)}) %collective-permute-start.51) | collective-permute-done | bytes 983072 | tf_op jit(solution)/shard_map/ppermute | solution.py:53
  426.5 2.5 copy-done.28
  429.0 8.2 %shard_map.336 = (bf16[2,320,512]{2,1,0:T(8,128)(2,1)S(1)}, bf16[2,320,512]{2,1,0:T(8,128)(2,1)S(1)}, bf16[2,320,512]{2,1,0:T(8,128)(2,1)S(1)}, bf16[2,320,512]{2,1,0:T(8,128)(2,1)S(1)}) custom-call(s32[12]{0:T(128)S(1)} %stack.145.index_ref, bf16[8,128,2560]{2,1,0:T(8,128)(2,1)S(1)} %copy-done.28, bf16[224,1024]{1,0:T(8,128)(2,1)S(1)} %copy-done.16, ...), custom_call_target="tpu_custom_call" | custom-call | flops 1 | bytes 1 | tf_op jit(solution)/shard_map/pallas_call | solution.py:519
  439.4 4.2 collective-permute-start.54
  448.0 11.0 %collective-permute-done.54.refs_1_ = bf16[2,320,512]{2,1,0:T(8,128)(2,1)S(1)} collective-permute-done((bf16[2,320,512]{2,1,0:T(8,128)(2,1)}, bf16[2,320,512]{2,1,0:T(8,128)(2,1)S(1)}, u32[]{:S(2)}, u32[]{:S(2)}) %collective-permute-start.54) | collective-permute-done | bytes 655392 | tf_op jit(solution)/shard_map/ppermute | solution.py:45
  461.4 11.2 %collective-permute-done.56.refs_3_ = bf16[2,320,512]{2,1,0:T(8,128)(2,1)S(1)} collective-permute-done((bf16[2,320,512]{2,1,0:T(8,128)(2,1)S(1)}, bf16[2,320,512]{2,1,0:T(8,128)(2,1)S(1)}, u32[]{:S(2)}, u32[]{:S(2)}) %collective-permute-start.56) | collective-permute-done | bytes 655392 | tf_op jit(solution)/shard_map/ppermute | solution.py:45
  475.4 11.8 %collective-permute-done.57.refs_0_ = bf16[128,2560]{1,0:T(8,128)(2,1)} collective-permute-done((bf16[128,2560]{1,0:T(8,128)(2,1)S(1)}, bf16[128,2560]{1,0:T(8,128)(2,1)}, u32[]{:S(2)}, u32[]{:S(2)}) %collective-permute-start.57) | collective-permute-done | bytes 655392 | tf_op jit(solution)/shard_map/ppermute | solution.py:45
  490.5 3.3 collective-permute-start.59
  496.1 4.6 all-to-all-start.2
  500.7 6.2 %collective-permute-done.59 = bf16[128,2560]{1,0:T(8,128)(2,1)S(1)} collective-permute-done((bf16[128,2560]{1,0:T(8,128)(2,1)S(1)}, bf16[128,2560]{1,0:T(8,128)(2,1)S(1)}, u32[]{:S(2)}, u32[]{:S(2)}) %collective-permute-start.59) | collective-permute-done | bytes 655392 | tf_op jit(solution)/shard_map/ppermute | solution.py:53
  507.5 5.1 collective-permute-start.52
  512.5 3.1 fusion.16
  515.6 3.8 all-to-all-done.2.refs_0_
  527.7 3.5 shard_map.345
  535.3 4.4 collective-permute-done.61.refs_1_
  (448 shorter events, 173.2 us)
Async XLA Ops:
  7.2 60.6 %all-gather.10.cloned.1.call-start = ((), (), s32[]{:S(2)}) async-start(), calls=%async_computation.10 | async-start | bytes 5898240 | tf_op jit(solution)/shard_map/all_gather | solution.py:596
  12.1 7.2 %collective-permute-start.1 = (bf16[2,40,256]{2,1,0:T(8,128)(2,1)S(1)}, bf16[2,40,256]{2,1,0:T(8,128)(2,1)S(1)}, u32[]{:S(2)}, u32[]{:S(2)}) collective-permute-start(bf16[2,40,256]{2,1,0:T(8,128)(2,1)S(1)} %get-tuple-element.150), channel_id=1, source_target_pairs={{0,4},{4,8},{8,12},{12,0},{1,5},{5,9},{9,13},{13,1},{2,6},{6,10},{... | collective-permute-start | bytes 122888 | tf_op jit(solution)/shard_map/ppermute | solution.py:45
  13.7 5.5 %collective-permute-start.2 = (bf16[2,40,256]{2,1,0:T(8,128)(2,1)S(1)}, bf16[2,40,256]{2,1,0:T(8,128)(2,1)S(1)}, u32[]{:S(2)}, u32[]{:S(2)}) collective-permute-start(bf16[2,40,256]{2,1,0:T(8,128)(2,1)S(1)} %get-tuple-element.151), channel_id=1, source_target_pairs={{0,12},{4,0},{8,4},{12,8},{1,13},{5,1},{9,5},{13,9},{2,14},{6,2},{... | collective-permute-start | bytes 122888 | tf_op jit(solution)/shard_map/ppermute | solution.py:45
  15.4 5.5 %collective-permute-start.3 = (bf16[2,40,256]{2,1,0:T(8,128)(2,1)S(1)}, bf16[2,40,256]{2,1,0:T(8,128)(2,1)S(1)}, u32[]{:S(2)}, u32[]{:S(2)}) collective-permute-start(bf16[2,40,256]{2,1,0:T(8,128)(2,1)S(1)} %get-tuple-element.148), channel_id=1, source_target_pairs={{0,8},{4,12},{8,0},{12,4},{1,9},{5,13},{9,1},{13,5},{2,10},{6,14},... | collective-permute-start | bytes 122888 | tf_op jit(solution)/shard_map/ppermute | solution.py:45
  22.5 180.8 %all-gather.8.cloned.1.call-start = ((), (), s32[]{:S(2)}) async-start(), calls=%async_computation.6 | async-start | bytes 9830400 | tf_op jit(solution)/shard_map/all_gather | solution.py:661
  23.3 5.3 collective-permute-start.4
  28.7 10.9 %collective-permute-start.5 = (bf16[2,320,256]{2,1,0:T(8,128)(2,1)S(1)}, bf16[2,320,256]{2,1,0:T(8,128)(2,1)S(1)}, u32[]{:S(2)}, u32[]{:S(2)}) collective-permute-start(bf16[2,320,256]{2,1,0:T(8,128)(2,1)S(1)} %pad_maximum_fusion.10.refs_0_), channel_id=1, source_target_pairs={{0,16},{16,32},{32,48},{48,0},{1,17},{17,33},{33,49},{49,1},{2,18}... | collective-permute-start | bytes 983048 | tf_op jit(solution)/shard_map/ppermute | solution.py:45
  30.4 13.2 %collective-permute-start.6 = (bf16[2,320,256]{2,1,0:T(8,128)(2,1)S(1)}, bf16[2,320,256]{2,1,0:T(8,128)(2,1)S(1)}, u32[]{:S(2)}, u32[]{:S(2)}) collective-permute-start(bf16[2,320,256]{2,1,0:T(8,128)(2,1)S(1)} %pad_maximum_fusion.10.refs_0_), channel_id=1, source_target_pairs={{0,48},{16,0},{32,16},{48,32},{1,49},{17,1},{33,17},{49,33},{2,50}... | collective-permute-start | bytes 983048 | tf_op jit(solution)/shard_map/ppermute | solution.py:45
  32.0 13.4 %collective-permute-start.7 = (bf16[2,320,256]{2,1,0:T(8,128)(2,1)S(1)}, bf16[2,320,256]{2,1,0:T(8,128)(2,1)S(1)}, u32[]{:S(2)}, u32[]{:S(2)}) collective-permute-start(bf16[2,320,256]{2,1,0:T(8,128)(2,1)S(1)} %pad_maximum_fusion.10.refs_0_), channel_id=1, source_target_pairs={{0,32},{16,48},{32,0},{48,16},{1,33},{17,49},{33,1},{49,17},{2,34}... | collective-permute-start | bytes 983048 | tf_op jit(solution)/shard_map/ppermute | solution.py:45
  35.2 22.7 %collective-permute-start.8 = (bf16[4,40,1536]{2,1,0:T(8,128)(2,1)S(1)}, bf16[4,40,1536]{2,1,0:T(8,128)(2,1)S(1)}, u32[]{:S(2)}, u32[]{:S(2)}) collective-permute-start(bf16[4,40,1536]{2,1,0:T(8,128)(2,1)S(1)} %get-tuple-element.59), channel_id=1, source_target_pairs={{0,2},{2,0},{1,3},{3,1},{4,6},{6,4},{5,7},{7,5},{8,10},{10,8},{9,1... | collective-permute-start | bytes 1474568 | tf_op jit(solution)/shard_map/ppermute | solution.py:53
  48.8 4.9 collective-permute-start.9
  54.6 7.0 %collective-permute-start.10 = (bf16[2,40,1280]{2,1,0:T(8,128)(2,1)S(1)}, bf16[2,40,1280]{2,1,0:T(8,128)(2,1)S(1)}, u32[]{:S(2)}, u32[]{:S(2)}) collective-permute-start(bf16[2,40,1280]{2,1,0:T(8,128)(2,1)S(1)} %pad_maximum_fusion.13.refs_0_), channel_id=1, source_target_pairs={{0,16},{16,32},{32,48},{48,0},{1,17},{17,33},{33,49},{49,1},{2,18}... | collective-permute-start | bytes 614408 | tf_op jit(solution)/shard_map/ppermute | solution.py:45
  55.8 7.6 %collective-permute-start.11 = (bf16[2,40,1280]{2,1,0:T(8,128)(2,1)S(1)}, bf16[2,40,1280]{2,1,0:T(8,128)(2,1)S(1)}, u32[]{:S(2)}, u32[]{:S(2)}) collective-permute-start(bf16[2,40,1280]{2,1,0:T(8,128)(2,1)S(1)} %pad_maximum_fusion.13.refs_0_), channel_id=1, source_target_pairs={{0,48},{16,0},{32,16},{48,32},{1,49},{17,1},{33,17},{49,33},{2,50}... | collective-permute-start | bytes 614408 | tf_op jit(solution)/shard_map/ppermute | solution.py:45
  57.9 7.3 %collective-permute-start.12 = (bf16[2,40,1280]{2,1,0:T(8,128)(2,1)S(1)}, bf16[2,40,1280]{2,1,0:T(8,128)(2,1)S(1)}, u32[]{:S(2)}, u32[]{:S(2)}) collective-permute-start(bf16[2,40,1280]{2,1,0:T(8,128)(2,1)S(1)} %pad_maximum_fusion.13.refs_0_), channel_id=1, source_target_pairs={{0,32},{16,48},{32,0},{48,16},{1,33},{17,49},{33,1},{49,17},{2,34}... | collective-permute-start | bytes 614408 | tf_op jit(solution)/shard_map/ppermute | solution.py:45
  69.1 7.5 %collective-permute-start.13 = (bf16[2,40,1536]{2,1,0:T(8,128)(2,1)S(1)}, bf16[2,40,1536]{2,1,0:T(8,128)(2,1)S(1)}, u32[]{:S(2)}, u32[]{:S(2)}) collective-permute-start(bf16[2,40,1536]{2,1,0:T(8,128)(2,1)S(1)} %get-tuple-element.136), channel_id=1, source_target_pairs={{0,4},{4,8},{8,12},{12,0},{1,5},{5,9},{9,13},{13,1},{2,6},{6,10},{... | collective-permute-start | bytes 737288 | tf_op jit(solution)/shard_map/ppermute | solution.py:45
  69.9 9.0 %collective-permute-start.14 = (bf16[2,40,1536]{2,1,0:T(8,128)(2,1)S(1)}, bf16[2,40,1536]{2,1,0:T(8,128)(2,1)S(1)}, u32[]{:S(2)}, u32[]{:S(2)}) collective-permute-start(bf16[2,40,1536]{2,1,0:T(8,128)(2,1)S(1)} %get-tuple-element.135), channel_id=1, source_target_pairs={{0,12},{4,0},{8,4},{12,8},{1,13},{5,1},{9,5},{13,9},{2,14},{6,2},{... | collective-permute-start | bytes 737288 | tf_op jit(solution)/shard_map/ppermute | solution.py:45
  72.4 7.8 %collective-permute-start.15 = (bf16[2,40,1536]{2,1,0:T(8,128)(2,1)S(1)}, bf16[2,40,1536]{2,1,0:T(8,128)(2,1)S(1)}, u32[]{:S(2)}, u32[]{:S(2)}) collective-permute-start(bf16[2,40,1536]{2,1,0:T(8,128)(2,1)S(1)} %get-tuple-element.134), channel_id=1, source_target_pairs={{0,8},{4,12},{8,0},{12,4},{1,9},{5,13},{9,1},{13,5},{2,10},{6,14},... | collective-permute-start | bytes 737288 | tf_op jit(solution)/shard_map/ppermute | solution.py:45
  81.8 26.6 %collective-permute-start.38 = (bf16[320,1536]{1,0:T(8,128)(2,1)}, bf16[320,1536]{1,0:T(8,128)(2,1)S(1)}, u32[]{:S(2)}, u32[]{:S(2)}) collective-permute-start(bf16[320,1536]{1,0:T(8,128)(2,1)} %bitcast.35.refs_1_), channel_id=1, source_target_pairs={{0,64},{64,0},{1,65},{65,1},{2,66},{66,2},{3,67},{67,3},{4,68},{68... | collective-permute-start | bytes 2949128 | tf_op jit(solution)/shard_map/ppermute | solution.py:53
  84.8 14.8 %collective-permute-start.16 = (bf16[8,40,1280]{2,1,0:T(8,128)(2,1)}, bf16[8,40,1280]{2,1,0:T(8,128)(2,1)}, u32[]{:S(2)}, u32[]{:S(2)}) collective-permute-start(bf16[8,40,1280]{2,1,0:T(8,128)(2,1)} %shard_map.307.refs_0_), channel_id=1, source_target_pairs={{0,4},{4,8},{8,12},{12,0},{1,5},{5,9},{9,13},{13,1},{2,6},{6,10},{... | collective-permute-start | bytes 2457608 | tf_op jit(solution)/shard_map/ppermute | solution.py:45
  84.8 14.8 %collective-permute-start.17 = (bf16[8,40,1280]{2,1,0:T(8,128)(2,1)}, bf16[8,40,1280]{2,1,0:T(8,128)(2,1)}, u32[]{:S(2)}, u32[]{:S(2)}) collective-permute-start(bf16[8,40,1280]{2,1,0:T(8,128)(2,1)} %shard_map.307.refs_0_), channel_id=1, source_target_pairs={{0,12},{4,0},{8,4},{12,8},{1,13},{5,1},{9,5},{13,9},{2,14},{6,2},{... | collective-permute-start | bytes 2457608 | tf_op jit(solution)/shard_map/ppermute | solution.py:45
  99.7 5.9 %collective-permute-start.19 = (bf16[64,1024]{1,0:T(8,128)(2,1)}, bf16[64,1024]{1,0:T(8,128)(2,1)S(1)}, u32[]{:S(2)}, u32[]{:S(2)}) collective-permute-start(bf16[64,1024]{1,0:T(8,128)(2,1)} %shard_map.308), channel_id=1, source_target_pairs={{0,32},{16,48},{1,33},{17,49},{2,34},{18,50},{3,35},{19,51},{4,36}... | collective-permute-start | bytes 393224 | tf_op jit(solution)/shard_map/ppermute | solution.py:49
  101.1 7.2 %collective-permute-start.18 = (bf16[64,1024]{1,0:T(8,128)(2,1)}, bf16[64,1024]{1,0:T(8,128)(2,1)S(1)}, u32[]{:S(2)}, u32[]{:S(2)}) collective-permute-start(bf16[64,1024]{1,0:T(8,128)(2,1)} %shard_map.308), channel_id=1, source_target_pairs={{0,16},{16,32},{32,48},{1,17},{17,33},{33,49},{2,18},{18,34},{34,5... | collective-permute-start | bytes 393224 | tf_op jit(solution)/shard_map/ppermute | solution.py:49
  115.0 22.2 %collective-permute-start.21 = (bf16[4,40,1280]{2,1,0:T(8,128)(2,1)}, bf16[4,40,1280]{2,1,0:T(8,128)(2,1)S(1)}, u32[]{:S(2)}, u32[]{:S(2)}) collective-permute-start(bf16[4,40,1280]{2,1,0:T(8,128)(2,1)} %slice.180), channel_id=1, source_target_pairs={{0,4},{4,8},{8,12},{12,0},{1,5},{5,9},{9,13},{13,1},{2,6},{6,10},{... | collective-permute-start | bytes 1228808 | tf_op jit(solution)/shard_map/ppermute | solution.py:45
  116.8 20.4 %collective-permute-start.22 = (bf16[4,40,1280]{2,1,0:T(8,128)(2,1)}, bf16[4,40,1280]{2,1,0:T(8,128)(2,1)S(1)}, u32[]{:S(2)}, u32[]{:S(2)}) collective-permute-start(bf16[4,40,1280]{2,1,0:T(8,128)(2,1)} %slice.181), channel_id=1, source_target_pairs={{0,12},{4,0},{8,4},{12,8},{1,13},{5,1},{9,5},{13,9},{2,14},{6,2},{... | collective-permute-start | bytes 1228808 | tf_op jit(solution)/shard_map/ppermute | solution.py:45
  120.1 17.1 %collective-permute-start.20 = (bf16[3,64,1024]{2,1,0:T(8,128)(2,1)S(1)}, bf16[3,64,1024]{2,1,0:T(8,128)(2,1)S(1)}, u32[]{:S(2)}, u32[]{:S(2)}) collective-permute-start(bf16[3,64,1024]{2,1,0:T(8,128)(2,1)S(1)} %pad_maximum_fusion.9.refs_0_), channel_id=1, source_target_pairs={{0,4},{4,8},{8,12},{12,0},{1,5},{5,9},{9,13},{13,1},{2,6},{6,10},{... | collective-permute-start | bytes 1179656 | tf_op jit(solution)/shard_map/ppermute | solution.py:45
  120.1 18.6 %collective-permute-start.23 = (bf16[3,64,1024]{2,1,0:T(8,128)(2,1)S(1)}, bf16[3,64,1024]{2,1,0:T(8,128)(2,1)S(1)}, u32[]{:S(2)}, u32[]{:S(2)}) collective-permute-start(bf16[3,64,1024]{2,1,0:T(8,128)(2,1)S(1)} %pad_maximum_fusion.9.refs_0_), channel_id=1, source_target_pairs={{0,12},{4,0},{8,4},{12,8},{1,13},{5,1},{9,5},{13,9},{2,14},{6,2},{... | collective-permute-start | bytes 1179656 | tf_op jit(solution)/shard_map/ppermute | solution.py:45
  124.1 12.1 %all-to-all-start = ((bf16[8,160,128]{2,1,0:T(8,128)(2,1)}), bf16[8,160,128]{2,1,0:T(8,128)(2,1)S(1)}, u32[]{:S(2)}, u32[]{:S(2)}) async-start(bf16[8,160,128]{2,1,0:T(8,128)(2,1)} %bitcast_bitcast_fusion), calls=%async_computation | async-start | bytes 655360 | tf_op jit(solution)/shard_map/all_to_all | solution.py:271
  127.6 112.6 %all-gather.12.cloned.1.call-start = ((), (), s32[]{:S(2)}) async-start(), calls=%async_computation.11 | async-start | bytes 5898240 | tf_op jit(solution)/shard_map/all_gather | solution.py:689
  127.6 16.5 %collective-permute-start.24 = (bf16[3,64,1024]{2,1,0:T(8,128)(2,1)S(1)}, bf16[3,64,1024]{2,1,0:T(8,128)(2,1)S(1)}, u32[]{:S(2)}, u32[]{:S(2)}) collective-permute-start(bf16[3,64,1024]{2,1,0:T(8,128)(2,1)S(1)} %pad_maximum_fusion.9.refs_0_), channel_id=1, source_target_pairs={{0,8},{4,12},{8,0},{12,4},{1,9},{5,13},{9,1},{13,5},{2,10},{6,14},... | collective-permute-start | bytes 1179656 | tf_op jit(solution)/shard_map/ppermute | solution.py:45
  138.8 6.7 %collective-permute-start.26 = (bf16[3,64,1024]{2,1,0:T(8,128)(2,1)}, bf16[3,64,1024]{2,1,0:T(8,128)(2,1)S(1)}, u32[]{:S(2)}, u32[]{:S(2)}) collective-permute-start(bf16[3,64,1024]{2,1,0:T(8,128)(2,1)} %shard_map.309.refs_1_), channel_id=1, source_target_pairs={{0,2},{2,0},{1,3},{3,1},{4,6},{6,4},{5,7},{7,5},{8,10},{10,8},{9,1... | collective-permute-start | bytes 1179656 | tf_op jit(solution)/shard_map/ppermute | solution.py:53
  139.5 6.4 %collective-permute-start.27 = (bf16[3,64,1024]{2,1,0:T(8,128)(2,1)}, bf16[3,64,1024]{2,1,0:T(8,128)(2,1)S(1)}, u32[]{:S(2)}, u32[]{:S(2)}) collective-permute-start(bf16[3,64,1024]{2,1,0:T(8,128)(2,1)} %shard_map.310.refs_2_), channel_id=1, source_target_pairs={{0,2},{2,0},{1,3},{3,1},{4,6},{6,4},{5,7},{7,5},{8,10},{10,8},{9,1... | collective-permute-start | bytes 1179656 | tf_op jit(solution)/shard_map/ppermute | solution.py:53
  145.4 17.2 %collective-permute-start.29 = (bf16[8,40,1280]{2,1,0:T(8,128)(2,1)S(1)}, bf16[8,40,1280]{2,1,0:T(8,128)(2,1)}, u32[]{:S(2)}, u32[]{:S(2)}) collective-permute-start(bf16[8,40,1280]{2,1,0:T(8,128)(2,1)S(1)} %copy-done.8), channel_id=1, source_target_pairs={{0,2},{2,0},{1,3},{3,1},{4,6},{6,4},{5,7},{7,5},{8,10},{10,8},{9,1... | collective-permute-start | bytes 2457608 | tf_op jit(solution)/shard_map/ppermute | solution.py:53
  145.5 17.9 %collective-permute-start.30 = (bf16[8,40,1280]{2,1,0:T(8,128)(2,1)}, bf16[8,40,1280]{2,1,0:T(8,128)(2,1)}, u32[]{:S(2)}, u32[]{:S(2)}) collective-permute-start(bf16[8,40,1280]{2,1,0:T(8,128)(2,1)} %collective-permute-done.16.refs_1_), channel_id=1, source_target_pairs={{0,2},{2,0},{1,3},{3,1},{4,6},{6,4},{5,7},{7,5},{8,10},{10,8},{9,1... | collective-permute-start | bytes 2457608 | tf_op jit(solution)/shard_map/ppermute | solution.py:53
  146.0 22.0 %collective-permute-start.31 = (bf16[8,40,1280]{2,1,0:T(8,128)(2,1)}, bf16[8,40,1280]{2,1,0:T(8,128)(2,1)}, u32[]{:S(2)}, u32[]{:S(2)}) collective-permute-start(bf16[8,40,1280]{2,1,0:T(8,128)(2,1)} %collective-permute-done.17.refs_2_), channel_id=1, source_target_pairs={{0,2},{2,0},{1,3},{3,1},{4,6},{6,4},{5,7},{7,5},{8,10},{10,8},{9,1... | collective-permute-start | bytes 2457608 | tf_op jit(solution)/shard_map/ppermute | solution.py:53
  147.4 22.0 %collective-permute-start.33 = (bf16[4,40,1280]{2,1,0:T(8,128)(2,1)S(1)}, bf16[4,40,1280]{2,1,0:T(8,128)(2,1)}, u32[]{:S(2)}, u32[]{:S(2)}) collective-permute-start(bf16[4,40,1280]{2,1,0:T(8,128)(2,1)S(1)} %copy-done.18), channel_id=1, source_target_pairs={{0,2},{2,0},{1,3},{3,1},{4,6},{6,4},{5,7},{7,5},{8,10},{10,8},{9,1... | collective-permute-start | bytes 1228808 | tf_op jit(solution)/shard_map/ppermute | solution.py:53
  148.2 21.2 %collective-permute-start.32 = (bf16[4,40,1280]{2,1,0:T(8,128)(2,1)}, bf16[4,40,1280]{2,1,0:T(8,128)(2,1)}, u32[]{:S(2)}, u32[]{:S(2)}) collective-permute-start(bf16[4,40,1280]{2,1,0:T(8,128)(2,1)} %shard_map.313.refs_3_), channel_id=1, source_target_pairs={{0,2},{2,0},{1,3},{3,1},{4,6},{6,4},{5,7},{7,5},{8,10},{10,8},{9,1... | collective-permute-start | bytes 1228808 | tf_op jit(solution)/shard_map/ppermute | solution.py:53
  162.7 20.5 %collective-permute-start.35 = (bf16[128,2560]{1,0:T(8,128)(2,1)S(1)}, bf16[128,2560]{1,0:T(8,128)(2,1)}, u32[]{:S(2)}, u32[]{:S(2)}) collective-permute-start(bf16[128,2560]{1,0:T(8,128)(2,1)S(1)} %copy-done.25), channel_id=1, source_target_pairs={{0,4},{4,8},{8,12},{12,0},{1,5},{5,9},{9,13},{13,1},{2,6},{6,10},{... | collective-permute-start | bytes 1966088 | tf_op jit(solution)/shard_map/ppermute | solution.py:45
  163.4 33.1 %collective-permute-start.36 = (bf16[128,2560]{1,0:T(8,128)(2,1)S(1)}, bf16[128,2560]{1,0:T(8,128)(2,1)}, u32[]{:S(2)}, u32[]{:S(2)}) collective-permute-start(bf16[128,2560]{1,0:T(8,128)(2,1)S(1)} %copy-done.25), channel_id=1, source_target_pairs={{0,12},{4,0},{8,4},{12,8},{1,13},{5,1},{9,5},{13,9},{2,14},{6,2},{... | collective-permute-start | bytes 1966088 | tf_op jit(solution)/shard_map/ppermute | solution.py:45
  168.0 30.5 %collective-permute-start.37 = (bf16[128,2560]{1,0:T(8,128)(2,1)S(1)}, bf16[128,2560]{1,0:T(8,128)(2,1)}, u32[]{:S(2)}, u32[]{:S(2)}) collective-permute-start(bf16[128,2560]{1,0:T(8,128)(2,1)S(1)} %copy-done.25), channel_id=1, source_target_pairs={{0,8},{4,12},{8,0},{12,4},{1,9},{5,13},{9,1},{13,5},{2,10},{6,14},... | collective-permute-start | bytes 1966088 | tf_op jit(solution)/shard_map/ppermute | solution.py:45
  175.7 22.7 %collective-permute-start.34 = (bf16[128,2560]{1,0:T(8,128)(2,1)}, bf16[128,2560]{1,0:T(8,128)(2,1)}, u32[]{:S(2)}, u32[]{:S(2)}) collective-permute-start(bf16[128,2560]{1,0:T(8,128)(2,1)} %convolution_convert_fusion.4.refs_1_), channel_id=1, source_target_pairs={{0,1},{1,0},{2,3},{3,2},{4,5},{5,4},{6,7},{7,6},{8,9},{9,8},{10,11... | collective-permute-start | bytes 1966088 | tf_op jit(solution)/shard_map/ppermute | solution.py:53
  203.3 98.5 %reduce-scatter.4.cloned.1.call-start = ((), (), s32[]{:S(2)}) async-start(), calls=%async_computation.7 | async-start | bytes 5898240 | tf_op jit(solution)/shard_map/reduce_scatter | solution.py:705
  261.8 123.8 %reduce-scatter.6.cloned.1.call-start = ((), (), s32[]{:S(2)}) async-start(), calls=%async_computation.8 | async-start | bytes 9830400 | tf_op jit(solution)/shard_map/reduce_scatter | solution.py:714
  301.9 15.7 %collective-permute-start.43 = (bf16[128,2560]{1,0:T(8,128)(2,1)}, bf16[128,2560]{1,0:T(8,128)(2,1)S(1)}, u32[]{:S(2)}, u32[]{:S(2)}) collective-permute-start(bf16[128,2560]{1,0:T(8,128)(2,1)} %shard_map.326), channel_id=1, source_target_pairs={{0,1},{1,0},{2,3},{3,2},{4,5},{5,4},{6,7},{7,6},{8,9},{9,8},{10,11... | collective-permute-start | bytes 1966088 | tf_op jit(solution)/shard_map/ppermute | solution.py:53
  341.3 15.9 %all-to-all-start.1 = ((bf16[8,320,128]{2,1,0:T(8,128)(2,1)}), bf16[8,320,128]{2,1,0:T(8,128)(2,1)S(1)}, u32[]{:S(2)}, u32[]{:S(2)}) async-start(bf16[8,320,128]{2,1,0:T(8,128)(2,1)} %shard_map.329), calls=%async_computation.2 | async-start | bytes 1310720 | tf_op jit(solution)/shard_map/all_to_all | solution.py:271
  345.0 80.2 %all-gather.14.cloned.1.call-start = ((), (), s32[]{:S(2)}) async-start(), calls=%async_computation.12 | async-start | bytes 5898240 | tf_op jit(solution)/shard_map/all_gather | solution.py:766
  345.1 19.9 %collective-permute-start.45 = (bf16[3,64,1024]{2,1,0:T(8,128)(2,1)S(1)}, bf16[3,64,1024]{2,1,0:T(8,128)(2,1)S(1)}, u32[]{:S(2)}, u32[]{:S(2)}) collective-permute-start(bf16[3,64,1024]{2,1,0:T(8,128)(2,1)S(1)} %get-tuple-element.69), channel_id=1, source_target_pairs={{0,4},{4,8},{8,12},{12,0},{1,5},{5,9},{9,13},{13,1},{2,6},{6,10},{... | collective-permute-start | bytes 1179656 | tf_op jit(solution)/shard_map/ppermute | solution.py:45
  347.0 26.6 %collective-permute-start.47 = (bf16[3,64,1024]{2,1,0:T(8,128)(2,1)S(1)}, bf16[3,64,1024]{2,1,0:T(8,128)(2,1)S(1)}, u32[]{:S(2)}, u32[]{:S(2)}) collective-permute-start(bf16[3,64,1024]{2,1,0:T(8,128)(2,1)S(1)} %get-tuple-element.71), channel_id=1, source_target_pairs={{0,8},{4,12},{8,0},{12,4},{1,9},{5,13},{9,1},{13,5},{2,10},{6,14},... | collective-permute-start | bytes 1179656 | tf_op jit(solution)/shard_map/ppermute | solution.py:45
  349.7 24.7 %collective-permute-start.46 = (bf16[3,64,1024]{2,1,0:T(8,128)(2,1)S(1)}, bf16[3,64,1024]{2,1,0:T(8,128)(2,1)}, u32[]{:S(2)}, u32[]{:S(2)}) collective-permute-start(bf16[3,64,1024]{2,1,0:T(8,128)(2,1)S(1)} %get-tuple-element.70), channel_id=1, source_target_pairs={{0,12},{4,0},{8,4},{12,8},{1,13},{5,1},{9,5},{13,9},{2,14},{6,2},{... | collective-permute-start | bytes 1179656 | tf_op jit(solution)/shard_map/ppermute | solution.py:45
  376.0 8.4 %collective-permute-start.49 = (bf16[64,1024]{1,0:T(8,128)(2,1)S(1)}, bf16[64,1024]{1,0:T(8,128)(2,1)S(1)}, u32[]{:S(2)}, u32[]{:S(2)}) collective-permute-start(bf16[64,1024]{1,0:T(8,128)(2,1)S(1)} %get-tuple-element.145), channel_id=1, source_target_pairs={{32,0},{48,16},{33,1},{49,17},{34,2},{50,18},{35,3},{51,19},{36,4}... | collective-permute-start | bytes 393224 | tf_op jit(solution)/shard_map/ppermute | solution.py:49
  377.3 7.1 %collective-permute-start.48 = (bf16[64,1024]{1,0:T(8,128)(2,1)S(1)}, bf16[64,1024]{1,0:T(8,128)(2,1)S(1)}, u32[]{:S(2)}, u32[]{:S(2)}) collective-permute-start(bf16[64,1024]{1,0:T(8,128)(2,1)S(1)} %get-tuple-element.144), channel_id=1, source_target_pairs={{16,0},{32,16},{48,32},{17,1},{33,17},{49,33},{18,2},{34,18},{50,3... | collective-permute-start | bytes 393224 | tf_op jit(solution)/shard_map/ppermute | solution.py:49
  385.6 121.8 %reduce-scatter.8.cloned.1.call-start = ((), (), s32[]{:S(2)}) async-start(), calls=%async_computation.9 | async-start | bytes 5898240 | tf_op jit(solution)/shard_map/reduce_scatter | solution.py:795
  395.9 6.2 %collective-permute-start.50 = (bf16[4,128,2560]{2,1,0:T(8,128)(2,1)}, bf16[4,128,2560]{2,1,0:T(8,128)(2,1)}, u32[]{:S(2)}, u32[]{:S(2)}) collective-permute-start(bf16[4,128,2560]{2,1,0:T(8,128)(2,1)} %get-tuple-element.74), channel_id=1, source_target_pairs={{0,2},{2,0},{1,3},{3,1},{4,6},{6,4},{5,7},{7,5},{8,10},{10,8},{9,1... | collective-permute-start | bytes 7864328 | tf_op jit(solution)/shard_map/ppermute | solution.py:53
  398.3 24.5 %collective-permute-start.51 = (bf16[320,1536]{1,0:T(8,128)(2,1)}, bf16[320,1536]{1,0:T(8,128)(2,1)}, u32[]{:S(2)}, u32[]{:S(2)}) collective-permute-start(bf16[320,1536]{1,0:T(8,128)(2,1)} %dynamic-slice_bitcast_fusion), channel_id=1, source_target_pairs={{0,64},{64,0},{1,65},{65,1},{2,66},{66,2},{3,67},{67,3},{4,68},{68... | collective-permute-start | bytes 2949128 | tf_op jit(solution)/shard_map/ppermute | solution.py:53
  439.4 19.6 %collective-permute-start.54 = (bf16[2,320,512]{2,1,0:T(8,128)(2,1)}, bf16[2,320,512]{2,1,0:T(8,128)(2,1)S(1)}, u32[]{:S(2)}, u32[]{:S(2)}) collective-permute-start(bf16[2,320,512]{2,1,0:T(8,128)(2,1)} %copy-done.77), channel_id=1, source_target_pairs={{0,16},{16,32},{32,48},{48,0},{1,17},{17,33},{33,49},{49,1},{2,18}... | collective-permute-start | bytes 1966088 | tf_op jit(solution)/shard_map/ppermute | solution.py:45
  443.6 17.9 %collective-permute-start.55 = (bf16[2,320,512]{2,1,0:T(8,128)(2,1)}, bf16[2,320,512]{2,1,0:T(8,128)(2,1)S(1)}, u32[]{:S(2)}, u32[]{:S(2)}) collective-permute-start(bf16[2,320,512]{2,1,0:T(8,128)(2,1)} %copy-done.76), channel_id=1, source_target_pairs={{0,48},{16,0},{32,16},{48,32},{1,49},{17,1},{33,17},{49,33},{2,50}... | collective-permute-start | bytes 1966088 | tf_op jit(solution)/shard_map/ppermute | solution.py:45
  443.6 29.0 %collective-permute-start.56 = (bf16[2,320,512]{2,1,0:T(8,128)(2,1)S(1)}, bf16[2,320,512]{2,1,0:T(8,128)(2,1)S(1)}, u32[]{:S(2)}, u32[]{:S(2)}) collective-permute-start(bf16[2,320,512]{2,1,0:T(8,128)(2,1)S(1)} %copy-done.75), channel_id=1, source_target_pairs={{0,32},{16,48},{32,0},{48,16},{1,33},{17,49},{33,1},{49,17},{2,34}... | collective-permute-start | bytes 1966088 | tf_op jit(solution)/shard_map/ppermute | solution.py:45
  445.9 29.5 %collective-permute-start.58 = (bf16[128,2560]{1,0:T(8,128)(2,1)S(1)}, bf16[128,2560]{1,0:T(8,128)(2,1)}, u32[]{:S(2)}, u32[]{:S(2)}) collective-permute-start(bf16[128,2560]{1,0:T(8,128)(2,1)S(1)} %copy-done.73), channel_id=1, source_target_pairs={{0,8},{4,12},{8,0},{12,4},{1,9},{5,13},{9,1},{13,5},{2,10},{6,14},... | collective-permute-start | bytes 1966088 | tf_op jit(solution)/shard_map/ppermute | solution.py:45
  446.7 40.5 %collective-permute-start.57 = (bf16[128,2560]{1,0:T(8,128)(2,1)S(1)}, bf16[128,2560]{1,0:T(8,128)(2,1)}, u32[]{:S(2)}, u32[]{:S(2)}) collective-permute-start(bf16[128,2560]{1,0:T(8,128)(2,1)S(1)} %copy-done.71), channel_id=1, source_target_pairs={{0,12},{4,0},{8,4},{12,8},{1,13},{5,1},{9,5},{13,9},{2,14},{6,2},{... | collective-permute-start | bytes 1966088 | tf_op jit(solution)/shard_map/ppermute | solution.py:45
  459.0 29.3 %collective-permute-start.53 = (bf16[128,2560]{1,0:T(8,128)(2,1)S(1)}, bf16[128,2560]{1,0:T(8,128)(2,1)}, u32[]{:S(2)}, u32[]{:S(2)}) collective-permute-start(bf16[128,2560]{1,0:T(8,128)(2,1)S(1)} %copy-done.69), channel_id=1, source_target_pairs={{0,4},{4,8},{8,12},{12,0},{1,5},{5,9},{9,13},{13,1},{2,6},{6,10},{... | collective-permute-start | bytes 1966088 | tf_op jit(solution)/shard_map/ppermute | solution.py:45
  473.8 19.9 %collective-permute-start.60 = (bf16[320,512]{1,0:T(8,128)(2,1)}, bf16[320,512]{1,0:T(8,128)(2,1)}, u32[]{:S(2)}, u32[]{:S(2)}) collective-permute-start(bf16[320,512]{1,0:T(8,128)(2,1)} %dynamic-slice_bitcast_fusion.1), channel_id=1, source_target_pairs={{0,64},{64,0},{1,65},{65,1},{2,66},{66,2},{3,67},{67,3},{4,68},{68... | collective-permute-start | bytes 983048 | tf_op jit(solution)/shard_map/ppermute | solution.py:53
  490.5 16.5 %collective-permute-start.59 = (bf16[128,2560]{1,0:T(8,128)(2,1)S(1)}, bf16[128,2560]{1,0:T(8,128)(2,1)S(1)}, u32[]{:S(2)}, u32[]{:S(2)}) collective-permute-start(bf16[128,2560]{1,0:T(8,128)(2,1)S(1)} %add_convert_fusion.1), channel_id=1, source_target_pairs={{0,1},{1,0},{2,3},{3,2},{4,5},{5,4},{6,7},{7,6},{8,9},{9,8},{10,11... | collective-permute-start | bytes 1966088 | tf_op jit(solution)/shard_map/ppermute | solution.py:53
  496.1 23.4 %all-to-all-start.2 = ((bf16[8,40,2048]{2,1,0:T(8,128)(2,1)}), bf16[8,40,2048]{2,1,0:T(8,128)(2,1)S(1)}, u32[]{:S(2)}, u32[]{:S(2)}) async-start(bf16[8,40,2048]{2,1,0:T(8,128)(2,1)} %bitcast.182), calls=%async_computation.5 | async-start | bytes 2621440 | tf_op jit(solution)/shard_map/all_to_all | solution.py:271
  507.5 24.5 %collective-permute-start.52 = (bf16[128,2560]{1,0:T(8,128)(2,1)}, bf16[128,2560]{1,0:T(8,128)(2,1)}, u32[]{:S(2)}, u32[]{:S(2)}) collective-permute-start(bf16[128,2560]{1,0:T(8,128)(2,1)} %bitcast.189), channel_id=1, source_target_pairs={{0,1},{1,0},{2,3},{3,2},{4,5},{5,4},{6,7},{7,6},{8,9},{9,8},{10,11... | collective-permute-start | bytes 1966088 | tf_op jit(solution)/shard_map/ppermute | solution.py:53
  532.0 7.6 %collective-permute-start.61 = (bf16[8,40,256]{2,1,0:T(8,128)(2,1)}, bf16[8,40,256]{2,1,0:T(8,128)(2,1)S(1)}, u32[]{:S(2)}, u32[]{:S(2)}) collective-permute-start(bf16[8,40,256]{2,1,0:T(8,128)(2,1)} %shard_map.342), channel_id=1, source_target_pairs={{0,1},{1,0},{2,3},{3,2},{4,5},{5,4},{6,7},{7,6},{8,9},{9,8},{10,11... | collective-permute-start | bytes 491528 | tf_op jit(solution)/shard_map/ppermute | solution.py:53
  (122 other events, 650.3 us)
Sparse Core Ops, SparseCore 0:
  22.6 37.7 all-gather.9
  113.2 79.4 all-gather.7
  203.4 36.7 all-gather.11
  261.9 39.9 reduce-scatter.3
  304.1 76.3 reduce-scatter.5
  385.8 37.0 all-gather.13
  439.5 65.0 reduce-scatter.7
